TPU v7x, 32 devices: a whole 2x2x4 slice. The times are simulated.
32 devices in a mesh: ctx: 8 (over y, x, core), grp: 4 (over z).
Axes of the slice: x: 2, y: 2, z: 4, core: 2. Of those that a mesh axis runs over, the one named last changes fastest.
Arguments:
- saved_input: bfloat16 [4, 2048, 1024], P('grp', None, 'ctx'), may hold values from -6 to 6
- out_grad: bfloat16 [4, 2048, 1024], P('grp', None, 'ctx'), may hold values from -0.1875 to 0.1875
- filters: float32 [4, 2048, 1024], P('grp', 'ctx'), may hold values from -6 to 6
- adapter_down: bfloat16 [16, 4, 2048], P(None, 'grp'), may hold values from -0.0625 to 0.0625
- adapter_up: bfloat16 [16, 4, 2048], P(None, 'grp'), may hold values from -0.25 to 0.25
Outputs:
- grad_input: bfloat16 [4, 2048, 1024], P('grp', None, 'ctx')
- grad_filter: float32 [4, 2048, 1024], P('grp', 'ctx')
- grad_down: float32 [16, 4, 2048], P(None, 'grp')
- grad_up: float32 [16, 4, 2048], P(None, 'grp')
All inputs are finite; a program needn't handle non-finite values.
Results may differ from a plain program's by a relative error of at most 0.0075.
Values may be sent and summed in bfloat16 or wider, within the bound.
No kernel may reach another device: no remote copies, remote signals or barrier semaphores. Data moves between devices by JAX's collectives and lax.ppermute only.
A program may use at most 64 MiB of HBM per device.

v0:
```python
import functools
import math

import jax
import jax.numpy as jnp
import ml_dtypes
import numpy as np
from jax import lax
from jax.experimental import pallas as pl
from jax.experimental.pallas import tpu as pltpu
from jax.sharding import PartitionSpec as P

HIGH = lax.Precision.HIGHEST
BF16 = jnp.bfloat16
F32 = jnp.float32
TABLE_ENTRIES = 1 << 22
HALF = 256
VMEM_BYTES = 20 * 1024 * 1024


@functools.lru_cache(maxsize=None)
def dft_table(length):
    period = 2 * length
    phase = np.outer(np.arange(length), np.arange(length)) % period * (2.0 * np.pi / period)
    cos, sin = np.cos(phase), np.sin(phase)
    sin[:, 0] = 1.0 - 2.0 * (np.arange(length) % 2)
    half = min(HALF, length)
    both = np.stack([cos.reshape(length, -1, half), sin.reshape(length, -1, half)], axis=2)
    return both.reshape(length, period).astype(ml_dtypes.bfloat16)


def dot(left, right):
    return jnp.dot(left, right, preferred_element_type=F32)


def dot_nt(left, right):
    return lax.dot_general(left, right, (((1,), (1,)), ((), ())), preferred_element_type=F32)


def dot_tn(left, right):
    return lax.dot_general(left, right, (((0,), (0,)), ((), ())), preferred_element_type=F32)


def shape(dims, kind):
    return jax.ShapeDtypeStruct(dims, kind)


def own_index(index_ref, offset):
    return jnp.bitwise_xor(index_ref[0], offset)


def part(index, size):
    return pl.ds(pl.multiple_of(index * size, size), size)


def cross_spectrum(first, left, right, half, scale):
    lc, ls, rc, rs = left[:, :half], left[:, half:], right[:, :half], right[:, half:]
    cc, ss = lc * rc, ls * rs
    real, imag = cc + ss, ls * rc - lc * rs
    if first:
        lane = lax.broadcasted_iota(jnp.int32, lc.shape, 1) == 0
        real = jnp.where(lane, 0.5 * cc, real)
        imag = jnp.where(lane, 0.5 * ss, imag)
    return jnp.concatenate([(scale * real).astype(BF16), (scale * imag).astype(BF16)], axis=1)


def blocks(table_ref):
    length, period = table_ref.shape
    width = 2 * min(HALF, length)
    return [slice(i, i + width) for i in range(0, period, width)]


def filter_spec_kernel(filt_ref, table_ref, out_ref):
    out_ref[...] = dot(filt_ref[...].astype(BF16), table_ref[...])


def input_pack_kernel(index_ref, down_ref, tok_ref, sibling_ref, acts_ref, *pack_refs):
    acts_ref[...] = dot(down_ref[...], tok_ref[...]).astype(BF16)
    chans = pack_refs[0].shape[1]
    for i, pack_ref in enumerate(pack_refs):
        rows = part(own_index(index_ref, 2 * i), chans)
        pack_ref[0] = tok_ref[rows, :]
        pack_ref[1] = sibling_ref[rows, :]


def grad_u_kernel(
    copies, index_ref, grad_ref, filt_spec_ref, up_ref, acts_ref, table_ref, spec_ref, du_ref, give_ref, rank_ref, cross
):
    length = table_ref.shape[0]
    shards, chans, tokens = grad_ref.shape
    signal = jnp.concatenate([grad_ref[i] for i in range(shards)], axis=1)
    for cols in blocks(table_ref):
        half = (cols.stop - cols.start) // 2
        spec = dot(signal, table_ref[:, cols])
        spec_ref[:, cols] = spec
        cross[:, cols] = cross_spectrum(cols.start == 0, spec, filt_spec_ref[:, cols], half, 1.0 / length)
    grad_u = dot_nt(cross[...], table_ref[...]).astype(BF16)
    du_ref[...] = grad_u
    for i in range(shards // 2):
        give_ref[i] = du_ref[:, part(own_index(index_ref, 2 * i + 1), tokens)]
    rank = dot(up_ref[:, part(own_index(index_ref, 0), chans)], grad_u).astype(BF16)
    both = [jnp.concatenate([rank[:, i * tokens : (i + 1) * tokens], acts_ref[...]], axis=0) for i in range(shards)]
    for i in range(shards):
        for j in range(copies):
            rank_ref[i * copies + j] = both[i]


def du_pack_kernel(index_ref, du_ref, got_ref, *pack_refs):
    tokens = got_ref.shape[2]
    for i, pack_ref in enumerate(pack_refs):
        pack_ref[0] = du_ref[:, part(own_index(index_ref, 2 * (i + 1)), tokens)]
        pack_ref[1] = got_ref[i + 1]


def rank_kernel(groups, scale, index_ref, parts_ref, tok_ref, du_ref, rank_ref, acts_ref, adapter_ref):
    rank = rank_ref.shape[0]
    shards = parts_ref.shape[0] // groups
    width = tok_ref.shape[0]
    acts, total = [], None
    for i in range(shards):
        both = parts_ref[i * groups].astype(F32)
        for j in range(1, groups):
            both = both + parts_ref[i * groups + j].astype(F32)
        acts.append(both[rank:])
        total = both[:rank] if total is None else total + both[:rank]
    acts = jnp.concatenate(acts, axis=1).astype(BF16)
    acts_ref[...] = acts
    rank_grad = total.astype(BF16)
    rank_ref[...] = rank_grad
    adapter_ref[:, :width] = scale * dot_nt(rank_grad, tok_ref[...])
    adapter_ref[:, width:] = scale * dot_nt(acts, du_ref[...])


def chip_sum_kernel(own_ref, other_ref, out_ref):
    chans = out_ref.shape[1] - own_ref.shape[1]
    width = own_ref.shape[1] - chans
    out_ref[:, :width] = (own_ref[:, :width] + other_ref[:, :width]).astype(BF16)
    out_ref[:, width : width + chans] = own_ref[:, width:].astype(BF16)
    out_ref[:, width + chans :] = other_ref[:, width:].astype(BF16)


def filter_grad_kernel(index_ref, acts_ref, up_ref, spec_ref, table_ref, *refs):
    pack_refs, out_ref, signal, cross = refs[:-3], refs[-3], refs[-2], refs[-1]
    length = table_ref.shape[0]
    _, chans, tokens = pack_refs[0].shape
    for i, pack_ref in enumerate(pack_refs):
        for j in range(2):
            signal[:, part(own_index(index_ref, 2 * i + j), tokens)] = pack_ref[j]
    own_up = up_ref[:, part(own_index(index_ref, 0), chans)]
    act = (signal[...].astype(F32) + dot_tn(own_up, acts_ref[...])).astype(BF16)
    for cols in blocks(table_ref):
        half = (cols.stop - cols.start) // 2
        spec = dot(act, table_ref[:, cols])
        cross[:, cols] = cross_spectrum(cols.start == 0, spec_ref[:, cols], spec, half, 1.0 / length)
    out_ref[...] = dot_nt(cross[...], table_ref[...])


def input_grad_kernel(index_ref, du_ref, got_ref, down_ref, rank_ref, *refs):
    pack_refs, out_ref = refs[:-1], refs[-1]
    _, chans, tokens = got_ref.shape

    def put(offset, value):
        index = own_index(index_ref, offset)
        lift = dot_tn(down_ref[:, part(index, chans)], rank_ref[...])
        out_ref[part(index, chans), :] = (value.astype(F32) + lift).astype(BF16)

    put(0, du_ref[:, part(own_index(index_ref, 0), tokens)])
    put(1, got_ref[0])
    for i, pack_ref in enumerate(pack_refs):
        for j in range(2):
            put(2 * (i + 1) + j, pack_ref[j])


def adapter_sum_kernel(index_ref, *refs):
    part_refs, down_out, up_out, total, chunks = refs[:-4], refs[-4], refs[-3], refs[-2], refs[-1]
    width = down_out.shape[2]
    chans = (part_refs[0].shape[1] - width) // 2
    sums = [ref[:, :width].astype(F32) for ref in part_refs]
    while len(sums) > 1:
        sums = [sums[i] + sums[i + 1] for i in range(0, len(sums), 2)]
    down_out[:, 0, :] = sums[0]
    for i, ref in enumerate(part_refs):
        for j in range(2):
            block = ref[:, width + j * chans : width + (j + 1) * chans]
            chunks[:, part(own_index(index_ref, 2 * i + j), chans)] = block.astype(F32)
    up_out[:, 0, :] = chunks[...]


def dense_body(mesh, saved_input, out_grad, filters, adapter_down, adapter_up):
    shards, groups = mesh.shape["ctx"], mesh.shape["grp"]
    tok_input, tok_grad, filt = saved_input[0], out_grad[0], filters[0]
    down, up = adapter_down[:, 0, :], adapter_up[:, 0, :]
    rank, width = down.shape
    tokens = tok_input.shape[1]
    chans, length = filt.shape
    chips = shards // 2
    table = jnp.asarray(dft_table(length))
    index = lax.axis_index("ctx").reshape(1)
    scalar = pl.BlockSpec(memory_space=pltpu.SMEM)
    local = pl.BlockSpec(memory_space=pltpu.VMEM)
    product = 2 * chans * length * 2 * length

    def call(kernel, name, out_shape, args, scratch=(), flops=0, index_first=True):
        args = ((index,) if index_first else ()) + tuple(args)
        in_specs = [scalar if arg is index else local for arg in args]
        moved = sum(int(np.prod(o.shape)) * o.dtype.itemsize for o in jax.tree.leaves(out_shape))
        return pl.pallas_call(
            kernel,
            out_shape=out_shape,
            in_specs=in_specs,
            scratch_shapes=scratch,
            cost_estimate=pl.CostEstimate(flops=flops, bytes_accessed=moved, transcendentals=0),
            compiler_params=pltpu.CompilerParams(vmem_limit_bytes=VMEM_BYTES),
            name=name,
        )(*args)

    def send(value, offset):
        return lax.ppermute(value, "ctx", [(i, i ^ offset) for i in range(shards)])

    pack = shape((2, chans, tokens), BF16)
    chan_grad = lax.all_to_all(tok_grad.reshape(shards, chans, tokens), "ctx", 0, 0, tiled=True)
    sibling_input = send(tok_input, 1)
    acts_part, *input_packs = call(
        input_pack_kernel,
        "input_pack",
        (shape((rank, tokens), BF16),) + (pack,) * chips,
        (down, tok_input, sibling_input),
    )
    chan_packs = [input_packs[0]] + [send(input_packs[i], 2 * i) for i in range(1, chips)]
    filt_spec = call(
        filter_spec_kernel,
        "filter_spec",
        shape((chans, 2 * length), F32),
        (filt, table),
        flops=product,
        index_first=False,
    )
    grad_spec, chan_du, give, rank_parts = call(
        functools.partial(grad_u_kernel, groups),
        "grad_u",
        (
            shape((chans, 2 * length), F32),
            shape((chans, length), BF16),
            shape((chips, chans, tokens), BF16),
            shape((shards * groups, 2 * rank, tokens), BF16),
        ),
        (chan_grad, filt_spec, up, acts_part, table),
        scratch=[pltpu.VMEM((chans, 2 * length), BF16)],
        flops=2 * product,
    )
    rank_all = lax.all_to_all(rank_parts, ("ctx", "grp"), 0, 0, tiled=True)
    got = send(give, 1)
    du_packs = call(du_pack_kernel, "du_pack", (pack,) * (chips - 1), (chan_du, got))
    tok_packs = [send(du_packs[i], 2 * (i + 1)) for i in range(chips - 1)]

    rank_grad, acts, adapter_part = call(
        functools.partial(rank_kernel, groups, float(length) ** -0.5),
        "rank_grad",
        (shape((rank, tokens), BF16), shape((rank, length), BF16), shape((rank, width + chans), F32)),
        (rank_all, tok_input, chan_du),
    )
    chip_part = call(
        chip_sum_kernel,
        "chip_sum",
        shape((rank, width + 2 * chans), BF16),
        (adapter_part, send(adapter_part, 1)),
        index_first=False,
    )
    chip_parts = [chip_part] + [send(chip_part, 2 * i) for i in range(1, chips)]
    filt_grad = call(
        filter_grad_kernel,
        "filter_grad",
        shape((chans, length), F32),
        (acts, up, grad_spec, table, *chan_packs),
        scratch=[pltpu.VMEM((chans, length), BF16), pltpu.VMEM((chans, 2 * length), BF16)],
        flops=2 * product,
    )
    grad_input = call(
        input_grad_kernel, "input_grad", shape((width, tokens), BF16), (chan_du, got, down, rank_grad, *tok_packs)
    )
    grad_down, grad_up = call(
        adapter_sum_kernel,
        "adapter_sum",
        (shape((rank, 1, width), F32),) * 2,
        chip_parts,
        scratch=[pltpu.VMEM((rank, width), F32)] * 2,
    )
    return grad_input[None], filt_grad[None], grad_down, grad_up


def split_radix(points):
    radix_low = 1
    while (
        points % (radix_low * 2) == 0
        and radix_low * 2 * (radix_low * 2) <= points
        and (points // (radix_low * 2) % 2 == 0)
    ):
        radix_low = radix_low * 2
    return (radix_low, points // radix_low)


def angle_table(height, across, period):
    index_down = lax.broadcasted_iota(jnp.int32, (height, across), 0)
    index_across = lax.broadcasted_iota(jnp.int32, (height, across), 1)
    phase = (index_down * index_across % period).astype(jnp.float32) * (2.0 * math.pi / period)
    return (jnp.cos(phase), jnp.sin(phase))


def make_tables(points):
    radix_low, radix_high = split_radix(points)
    cos_one, sin_one = angle_table(radix_high, radix_high // 2, radix_high)
    first = jnp.concatenate([cos_one, -sin_one], axis=0)
    first_high = first.astype(jnp.bfloat16)
    first_low = (first - first_high.astype(jnp.float32)).astype(jnp.bfloat16)
    twist = angle_table(radix_high, radix_low, points)
    cos_two, sin_two = angle_table(radix_low, radix_low, radix_low)
    second_fwd = jnp.concatenate(
        [jnp.concatenate([cos_two, sin_two], axis=1), jnp.concatenate([-sin_two, cos_two], axis=1)],
        axis=0,
    )
    second_inv = jnp.concatenate(
        [jnp.concatenate([cos_two, -sin_two], axis=1), jnp.concatenate([sin_two, cos_two], axis=1)],
        axis=0,
    )
    last_inv = jnp.concatenate([cos_one, -sin_one], axis=0)
    return (
        radix_low,
        radix_high,
        first,
        first_high,
        first_low,
        twist,
        second_fwd,
        second_inv,
        last_inv,
    )


def forward_dft(signal, tables):
    radix_low, radix_high, first, first_high, first_low, twist, second_fwd, second_inv, last_inv = (
        tables
    )
    channels = signal.shape[0]
    blocks = signal.reshape(channels, radix_high // 2, radix_low)
    if signal.dtype == jnp.bfloat16:
        section_one = jnp.einsum(
            "kn,cnp->ckp", first_high, blocks, preferred_element_type=jnp.float32
        )
        section_one = section_one + jnp.einsum(
            "kn,cnp->ckp", first_low, blocks, preferred_element_type=jnp.float32
        )
    else:
        section_one = jnp.einsum("kn,cnp->ckp", first, blocks, precision=HIGH)
    real_one = section_one[:, :radix_high]
    imag_one = section_one[:, radix_high:]
    cos_twist, sin_twist = twist
    real_two = real_one * cos_twist + imag_one * sin_twist
    imag_two = imag_one * cos_twist - real_one * sin_twist
    joined = jnp.concatenate([real_two, imag_two], axis=2)
    spectrum = jnp.einsum("jq,ckq->cjk", second_fwd, joined, precision=HIGH)
    return (spectrum[:, :radix_low], spectrum[:, radix_low:])


def inverse_dft(spectrum, tables):
    radix_low, radix_high, first, first_high, first_low, twist, second_fwd, second_inv, last_inv = (
        tables
    )
    spec_real, spec_imag = spectrum
    channels = spec_real.shape[0]
    joined = jnp.concatenate([spec_real, spec_imag], axis=1)
    section_one = jnp.einsum("pq,cqk->cpk", second_inv, joined, precision=HIGH)
    real_one = section_one[:, :radix_low]
    imag_one = section_one[:, radix_low:]
    cos_twist = twist[0].T
    sin_twist = twist[1].T
    real_two = real_one * cos_twist - imag_one * sin_twist
    imag_two = real_one * sin_twist + imag_one * cos_twist
    stacked = jnp.concatenate([real_two, imag_two], axis=2)
    signal = jnp.einsum("kn,cpk->cnp", last_inv, stacked, precision=HIGH)
    return signal.reshape(channels, -1) / float(radix_low * radix_high)


def conj_product(spec_left, spec_right):
    left_real, left_imag = spec_left
    right_real, right_imag = spec_right
    return (
        left_real * right_real + left_imag * right_imag,
        left_imag * right_real - left_real * right_imag,
    )


def staged_body(saved_input, out_grad, filters, adapter_down, adapter_up):
    tok_input = saved_input[0]
    tok_grad = out_grad[0]
    down_rows = adapter_down[:, 0, :]
    up_float = adapter_up[:, 0, :].astype(jnp.float32)
    rank_part = jnp.dot(down_rows, tok_input, preferred_element_type=jnp.float32)
    rank_acts = lax.psum(rank_part, "grp")
    tok_act = (
        tok_input.astype(jnp.float32) + jnp.einsum("rc,rt->ct", up_float, rank_acts, precision=HIGH)
    ).astype(jnp.bfloat16)
    chan_act, chan_grad = (
        lax.all_to_all(tok_act, "ctx", split_axis=0, concat_axis=1, tiled=True),
        lax.all_to_all(tok_grad, "ctx", split_axis=0, concat_axis=1, tiled=True),
    )
    length = chan_act.shape[1]
    tables = make_tables(2 * length)
    act_spec = forward_dft(chan_act, tables)
    grad_spec = forward_dft(chan_grad, tables)
    kern_spec = forward_dft(filters[0], tables)
    chan_du = inverse_dft(conj_product(grad_spec, kern_spec), tables).astype(jnp.bfloat16)
    filt_grad = inverse_dft(conj_product(grad_spec, act_spec), tables)
    tok_du = lax.all_to_all(chan_du, "ctx", split_axis=1, concat_axis=0, tiled=True)
    du_float = tok_du.astype(jnp.float32)
    rank_grad = lax.psum(jnp.einsum("rc,ct->rt", up_float, du_float, precision=HIGH), "grp")
    grad_input = (
        du_float + jnp.einsum("rc,rt->ct", down_rows.astype(jnp.float32), rank_grad, precision=HIGH)
    ).astype(jnp.bfloat16)
    down_part = jnp.einsum("rt,ct->rc", rank_grad, tok_input.astype(jnp.float32), precision=HIGH)
    up_part = jnp.einsum("rt,ct->rc", rank_acts, du_float, precision=HIGH)
    down_sum, up_sum = lax.psum((down_part, up_part), "ctx")
    factor = float(length) ** (-0.5)
    return (
        grad_input[None],
        filt_grad[None],
        (factor * down_sum)[:, None, :],
        (factor * up_sum)[:, None, :],
    )


def body(mesh, saved_input, out_grad, filters, adapter_down, adapter_up):
    length = filters.shape[2]
    shards = mesh.shape["ctx"]
    if 2 * length * length <= TABLE_ENTRIES and shards > 1 and shards & (shards - 1) == 0:
        return dense_body(mesh, saved_input, out_grad, filters, adapter_down, adapter_up)
    return staged_body(saved_input, out_grad, filters, adapter_down, adapter_up)


def solution(mesh):
    placed = (
        P("grp", None, "ctx"),
        P("grp", None, "ctx"),
        P("grp", "ctx", None),
        P(None, "grp", None),
        P(None, "grp", None),
    )
    return jax.shard_map(
        functools.partial(body, mesh),
        mesh=mesh,
        in_specs=placed,
        out_specs=(
            P("grp", None, "ctx"),
            P("grp", "ctx", None),
            P(None, "grp", None),
            P(None, "grp", None),
        ),
        check_vma=False,
    )
```

profile of v0, /device:TPU:0, one launch (start us, length us, event | category | flops | bytes accessed | tf_op | source)
XLA Modules:
  0.0 63.1 jit_solution(1435019461600387371)
XLA Ops:
  0.6 0.5 collective-permute-start
  1.1 4.8 %all-to-all-start = ((bf16[8,256,128]{2,1,0:T(8,128)(2,1)}), bf16[8,256,128]{2,1,0:T(8,128)(2,1)S(1)}, u32[]{:S(2)}, u32[]{:S(2)}) async-start(bf16[8,256,128]{2,1,0:T(8,128)(2,1)} %bitcast.17), calls=%async_computation | async-start | bytes 1048576 | tf_op jit(solution)/shard_map/all_to_all | solution.py:221
  6.0 2.2 %copy-done = bf16[1024,2048]{1,0:T(8,128)(2,1)S(1)} copy-done((bf16[1024,2048]{1,0:T(8,128)(2,1)S(1)}, bf16[1024,2048]{1,0:T(8,128)(2,1)}, u32[]{:S(2)}) %copy-start) | copy-done | bytes 4194328
  8.2 1.2 %copy-done.6 = f32[1,256,1024]{2,1,0:T(8,128)S(1)} copy-done((f32[1,256,1024]{2,1,0:T(8,128)S(1)}, f32[1,256,1024]{2,1,0:T(8,128)}, u32[]{:S(2)}) %copy-start.6) | copy-done | bytes 1048600
  9.4 1.2 %filter_spec.1.filt_spec_ref = f32[256,2048]{1,0:T(8,128)S(1)} custom-call(f32[256,1024]{1,0:T(8,128)S(1)} %bitcast.11, bf16[1024,2048]{1,0:T(8,128)(2,1)S(1)} %copy-done), custom_call_target="tpu_custom_call" | custom-call | flops 1073741824 | bytes 2097152 | tf_op jit(solution)/shard_map/filter_spec/pallas_call | solution.py:207
  10.7 0.0 collective-permute-done.sibling_ref
  10.7 1.3 %input_pack.1 = (bf16[16,128]{1,0:T(8,128)(2,1)S(1)}, bf16[2,256,128]{2,1,0:T(8,128)(2,1)S(1)}, bf16[2,256,128]{2,1,0:T(8,128)(2,1)S(1)}, bf16[2,256,128]{2,1,0:T(8,128)(2,1)S(1)}, bf16[2,256,128]{2,1,0:T(8,128)(2,1)S(1)}) custom-call(s32[1]{0:T(128)} %bitcast.index_ref, bf16[16,2048]{1,0:T(8,128)(2,1)S(1)} %bitcast.12, bf16[2048,128]{1,0:T(8,128)(2,1)S(1)} %bitcast.9, ...), custom_call_target="tpu_custom_call" | custom-call | bytes 528384 | tf_op jit(solution)/shard_map/input_pack/pallas_call | solution.py:207
  11.9 0.0 copy-start.11
  11.9 0.7 %copy-done.11 = bf16[2,256,128]{2,1,0:T(8,128)(2,1)} copy-done((bf16[2,256,128]{2,1,0:T(8,128)(2,1)}, bf16[2,256,128]{2,1,0:T(8,128)(2,1)S(1)}, u32[]{:S(2)}) %copy-start.11) | copy-done | bytes 131096
  12.6 0.7 %copy-done.15 = bf16[2,256,128]{2,1,0:T(8,128)(2,1)} copy-done((bf16[2,256,128]{2,1,0:T(8,128)(2,1)}, bf16[2,256,128]{2,1,0:T(8,128)(2,1)S(1)}, u32[]{:S(2)}) %copy-start.15) | copy-done | bytes 131096
  13.3 0.7 %copy-done.16 = bf16[2,256,128]{2,1,0:T(8,128)(2,1)} copy-done((bf16[2,256,128]{2,1,0:T(8,128)(2,1)}, bf16[2,256,128]{2,1,0:T(8,128)(2,1)S(1)}, u32[]{:S(2)}) %copy-start.16) | copy-done | bytes 131096
  13.9 0.7 %copy-done.17 = bf16[2,256,128]{2,1,0:T(8,128)(2,1)} copy-done((bf16[2,256,128]{2,1,0:T(8,128)(2,1)}, bf16[2,256,128]{2,1,0:T(8,128)(2,1)S(1)}, u32[]{:S(2)}) %copy-start.17) | copy-done | bytes 131096
  14.6 1.2 %all-to-all-done.grad_ref = bf16[8,256,128]{2,1,0:T(8,128)(2,1)S(1)} async-done(((bf16[8,256,128]{2,1,0:T(8,128)(2,1)}), bf16[8,256,128]{2,1,0:T(8,128)(2,1)S(1)}, u32[]{:S(2)}, u32[]{:S(2)}) %all-to-all-start) | async-done | bytes 524320 | tf_op jit(solution)/shard_map/all_to_all | solution.py:221
  15.7 0.8 %copy-done.7 = bf16[8,256,128]{2,1,0:T(8,128)(2,1)} copy-done((bf16[8,256,128]{2,1,0:T(8,128)(2,1)}, bf16[8,256,128]{2,1,0:T(8,128)(2,1)S(1)}, u32[]{:S(2)}) %copy-start.7) | copy-done | bytes 524312
  16.5 2.2 %copy-done.1 = bf16[1024,2048]{1,0:T(8,128)(2,1)S(1)} copy-done((bf16[1024,2048]{1,0:T(8,128)(2,1)S(1)}, bf16[1024,2048]{1,0:T(8,128)(2,1)}, u32[]{:S(2)}) %copy-start.1) | copy-done | bytes 4194328
  18.7 1.0 %copy-done.8 = bf16[8,256,128]{2,1,0:T(8,128)(2,1)S(1)} copy-done((bf16[8,256,128]{2,1,0:T(8,128)(2,1)S(1)}, bf16[8,256,128]{2,1,0:T(8,128)(2,1)}, u32[]{:S(2)}) %copy-start.8) | copy-done | bytes 524312
  19.8 2.6 %grad_u.1 = (f32[256,2048]{1,0:T(8,128)S(1)}, bf16[256,1024]{1,0:T(8,128)(2,1)S(1)}, bf16[4,256,128]{2,1,0:T(8,128)(2,1)S(1)}, bf16[32,32,128]{2,1,0:T(8,128)(2,1)S(1)}) custom-call(s32[1]{0:T(128)} %bitcast.index_ref, bf16[8,256,128]{2,1,0:T(8,128)(2,1)S(1)} %copy-done.8, f32[256,2048]{1,0:T(8,128)S(1)} %filter_spec.1.filt_spec_ref, ...), custom_call_target="tpu_custom_call" | custom-call | flops 2147483648 | bytes 3145728 | tf_op jit(solution)/shard_map/grad_u/pallas_call | solution.py:207
  22.3 1.4 %copy-done.4 = f32[256,2048]{1,0:T(8,128)} copy-done((f32[256,2048]{1,0:T(8,128)}, f32[256,2048]{1,0:T(8,128)S(1)}, u32[]{:S(2)}) %copy-start.4) | copy-done | bytes 2097176
  23.7 0.7 %copy-done.9 = bf16[32,32,128]{2,1,0:T(8,128)(2,1)} copy-done((bf16[32,32,128]{2,1,0:T(8,128)(2,1)}, bf16[32,32,128]{2,1,0:T(8,128)(2,1)S(1)}, u32[]{:S(2)}) %copy-start.9) | copy-done | bytes 262168
  24.4 0.7 %copy-done.14 = bf16[4,256,128]{2,1,0:T(8,128)(2,1)} copy-done((bf16[4,256,128]{2,1,0:T(8,128)(2,1)}, bf16[4,256,128]{2,1,0:T(8,128)(2,1)S(1)}, u32[]{:S(2)}) %copy-start.14) | copy-done | bytes 262168
  25.1 5.2 %all-to-all-start.1 = ((bf16[32,32,128]{2,1,0:T(8,128)(2,1)}), bf16[32,32,128]{2,1,0:T(8,128)(2,1)S(1)}, u32[]{:S(2)}, u32[]{:S(2)}) async-start(bf16[32,32,128]{2,1,0:T(8,128)(2,1)} %copy-done.9), calls=%async_computation.1 | async-start | bytes 524288 | tf_op jit(solution)/shard_map/all_to_all | solution.py:251
  30.3 0.3 collective-permute-start.1
  30.6 9.9 %all-to-all-done.1.parts_ref = bf16[32,32,128]{2,1,0:T(8,128)(2,1)S(1)} async-done(((bf16[32,32,128]{2,1,0:T(8,128)(2,1)}), bf16[32,32,128]{2,1,0:T(8,128)(2,1)S(1)}, u32[]{:S(2)}, u32[]{:S(2)}) %all-to-all-start.1) | async-done | bytes 262176 | tf_op jit(solution)/shard_map/all_to_all | solution.py:251
  40.5 0.4 rank_grad.1
  40.9 0.4 collective-permute-start.8
  41.3 0.9 %collective-permute-start.5 = (bf16[2,256,128]{2,1,0:T(8,128)(2,1)}, bf16[2,256,128]{2,1,0:T(8,128)(2,1)S(1)}, u32[]{:S(2)}, u32[]{:S(2)}) collective-permute-start(bf16[2,256,128]{2,1,0:T(8,128)(2,1)} %copy-done.17), channel_id=1, source_target_pairs={{0,8},{4,12},{8,0},{12,4},{16,24},{20,28},{24,16},{28,20},{1,9},{5... | collective-permute-start | bytes 393224 | tf_op jit(solution)/shard_map/ppermute | solution.py:218
  42.2 0.6 collective-permute-start.6
  42.7 2.0 %collective-permute-start.7 = (bf16[2,256,128]{2,1,0:T(8,128)(2,1)}, bf16[2,256,128]{2,1,0:T(8,128)(2,1)S(1)}, u32[]{:S(2)}, u32[]{:S(2)}) collective-permute-start(bf16[2,256,128]{2,1,0:T(8,128)(2,1)} %copy-done.15), channel_id=1, source_target_pairs={{0,24},{4,28},{8,16},{12,20},{16,8},{20,12},{24,0},{28,4},{1,25},{... | collective-permute-start | bytes 393224 | tf_op jit(solution)/shard_map/ppermute | solution.py:218
  44.8 0.0 collective-permute-done.1.got_ref
  44.8 1.0 %du_pack.1 = (bf16[2,256,128]{2,1,0:T(8,128)(2,1)S(1)}, bf16[2,256,128]{2,1,0:T(8,128)(2,1)S(1)}, bf16[2,256,128]{2,1,0:T(8,128)(2,1)S(1)}) custom-call(s32[1]{0:T(128)} %bitcast.index_ref, bf16[256,1024]{1,0:T(8,128)(2,1)S(1)} %get-tuple-element.22.du_ref, bf16[4,256,128]{2,1,0:T(8,128)(2,1)} %collective-permute-done.1.got_ref), custom_call_target="tpu_custom_call" | custom-call | bytes 393216 | tf_op jit(solution)/shard_map/du_pack/pallas_call | solution.py:207
  45.8 1.0 %collective-permute-start.2 = (bf16[2,256,128]{2,1,0:T(8,128)(2,1)S(1)}, bf16[2,256,128]{2,1,0:T(8,128)(2,1)S(1)}, u32[]{:S(2)}, u32[]{:S(2)}) collective-permute-start(bf16[2,256,128]{2,1,0:T(8,128)(2,1)S(1)} %get-tuple-element.26), channel_id=1, source_target_pairs={{0,8},{4,12},{8,0},{12,4},{16,24},{20,28},{24,16},{28,20},{1,9},{5... | collective-permute-start | bytes 393224 | tf_op jit(solution)/shard_map/ppermute | solution.py:218
  46.7 0.0 collective-permute-done.8.other_ref
  46.7 0.6 collective-permute-start.3
  47.3 0.5 collective-permute-done.5.refs_1_
  47.8 1.6 %collective-permute-start.4 = (bf16[2,256,128]{2,1,0:T(8,128)(2,1)S(1)}, bf16[2,256,128]{2,1,0:T(8,128)(2,1)S(1)}, u32[]{:S(2)}, u32[]{:S(2)}) collective-permute-start(bf16[2,256,128]{2,1,0:T(8,128)(2,1)S(1)} %get-tuple-element.28), channel_id=1, source_target_pairs={{0,24},{4,28},{8,16},{12,20},{16,8},{20,12},{24,0},{28,4},{1,25},{... | collective-permute-start | bytes 393224 | tf_op jit(solution)/shard_map/ppermute | solution.py:218
  49.4 0.9 %collective-permute-done.6.refs_2_ = bf16[2,256,128]{2,1,0:T(8,128)(2,1)S(1)} collective-permute-done((bf16[2,256,128]{2,1,0:T(8,128)(2,1)}, bf16[2,256,128]{2,1,0:T(8,128)(2,1)S(1)}, u32[]{:S(2)}, u32[]{:S(2)}) %collective-permute-start.6) | collective-permute-done | bytes 131104 | tf_op jit(solution)/shard_map/ppermute | solution.py:218
  50.3 1.6 %collective-permute-start.11 = (bf16[16,2560]{1,0:T(8,128)(2,1)S(1)}, bf16[16,2560]{1,0:T(8,128)(2,1)S(1)}, u32[]{:S(2)}, u32[]{:S(2)}) collective-permute-start(bf16[16,2560]{1,0:T(8,128)(2,1)S(1)} %chip_sum.1.refs_0_), channel_id=1, source_target_pairs={{0,24},{4,28},{8,16},{12,20},{16,8},{20,12},{24,0},{28,4},{1,25},{... | collective-permute-start | bytes 245768 | tf_op jit(solution)/shard_map/ppermute | solution.py:218
  51.9 0.0 collective-permute-done.7.refs_3_
  51.9 1.7 %collective-permute-start.10 = (bf16[16,2560]{1,0:T(8,128)(2,1)S(1)}, bf16[16,2560]{1,0:T(8,128)(2,1)S(1)}, u32[]{:S(2)}, u32[]{:S(2)}) collective-permute-start(bf16[16,2560]{1,0:T(8,128)(2,1)S(1)} %chip_sum.1.refs_0_), channel_id=1, source_target_pairs={{0,16},{4,20},{8,24},{12,28},{16,0},{20,4},{24,8},{28,12},{1,17},{... | collective-permute-start | bytes 245768 | tf_op jit(solution)/shard_map/ppermute | solution.py:218
  53.6 0.0 collective-permute-done.2.refs_0_
  53.6 0.8 %collective-permute-start.9 = (bf16[16,2560]{1,0:T(8,128)(2,1)S(1)}, bf16[16,2560]{1,0:T(8,128)(2,1)S(1)}, u32[]{:S(2)}, u32[]{:S(2)}) collective-permute-start(bf16[16,2560]{1,0:T(8,128)(2,1)S(1)} %chip_sum.1.refs_0_), channel_id=1, source_target_pairs={{0,8},{4,12},{8,0},{12,4},{16,24},{20,28},{24,16},{28,20},{1,9},{5... | collective-permute-start | bytes 245768 | tf_op jit(solution)/shard_map/ppermute | solution.py:218
  54.4 2.2 %copy-done.2 = bf16[1024,2048]{1,0:T(8,128)(2,1)S(1)} copy-done((bf16[1024,2048]{1,0:T(8,128)(2,1)S(1)}, bf16[1024,2048]{1,0:T(8,128)(2,1)}, u32[]{:S(2)}) %copy-start.2) | copy-done | bytes 4194328
  56.6 3.6 %filter_grad.1 = f32[256,1024]{1,0:T(8,128)} custom-call(s32[1]{0:T(128)} %bitcast.index_ref, bf16[16,1024]{1,0:T(8,128)(2,1)S(1)} %get-tuple-element.29.acts_ref, bf16[16,2048]{1,0:T(8,128)(2,1)S(1)} %bitcast.15, f32[256,2048]{1,0:T(8,128)S(1)} %copy-done.5, bf16[1024,2048]{1,0:T(8,128)(2,1)S(1)} %copy-done.2, bf16[2,256,128]{2,1,0:T(8,128)(2,1)S(1)} %copy-done.12, ...), custom_call_target="tpu_custom_call" | custom-call | flops 2147483648 | bytes 1048576 | tf_op jit(solution)/shard_map/filter_grad/pallas_call | solution.py:207
  60.2 0.0 collective-permute-done.3.refs_1_
  60.2 0.0 collective-permute-done.4.refs_2_
  60.2 2.1 %input_grad.1 = bf16[2048,128]{1,0:T(8,128)(2,1)} custom-call(s32[1]{0:T(128)} %bitcast.index_ref, bf16[256,1024]{1,0:T(8,128)(2,1)S(1)} %get-tuple-element.22.du_ref, bf16[4,256,128]{2,1,0:T(8,128)(2,1)} %collective-permute-done.1.got_ref, bf16[16,2048]{1,0:T(8,128)(2,1)S(1)} %bitcast.13, bf16[16,128]{1,0:T(8,128)(2,1)S(1)} %get-tuple-element.25.rank_ref, ...), custom_call_target="tpu_custom_call" | custom-call | bytes 524288 | tf_op jit(solution)/shard_map/input_grad/pallas_call | solution.py:207
  62.3 0.0 collective-permute-done.9.refs_1_
  62.3 0.8 %adapter_sum.1 = (f32[16,1,2048]{2,1,0:T(1,128)}, f32[16,1,2048]{2,1,0:T(1,128)}) custom-call(s32[1]{0:T(128)} %bitcast.index_ref, bf16[16,2560]{1,0:T(8,128)(2,1)S(1)} %chip_sum.1.refs_0_, bf16[16,2560]{1,0:T(8,128)(2,1)S(1)} %collective-permute-done.9.refs_1_, bf16[16,2560]{1,0:T(8,128)(2,1)S(1)} %collective-permute-done.10.refs_2_, ...), custom_call_target="tpu_custom_call" | custom-call | bytes 262144 | tf_op jit(solution)/shard_map/adapter_sum/pallas_call | solution.py:207
  (25 shorter events, 0.1 us)
Async XLA Ops:
  0.6 10.0 %collective-permute-start = (bf16[2048,128]{1,0:T(8,128)(2,1)}, bf16[2048,128]{1,0:T(8,128)(2,1)}, u32[]{:S(2)}, u32[]{:S(2)}) collective-permute-start(bf16[2048,128]{1,0:T(8,128)(2,1)} %bitcast.8), channel_id=1, source_target_pairs={{0,4},{4,0},{8,12},{12,8},{16,20},{20,16},{24,28},{28,24},{1,5},{5... | collective-permute-start | bytes 1572872 | tf_op jit(solution)/shard_map/ppermute | solution.py:218
  1.1 14.6 %all-to-all-start = ((bf16[8,256,128]{2,1,0:T(8,128)(2,1)}), bf16[8,256,128]{2,1,0:T(8,128)(2,1)S(1)}, u32[]{:S(2)}, u32[]{:S(2)}) async-start(bf16[8,256,128]{2,1,0:T(8,128)(2,1)} %bitcast.17), calls=%async_computation | async-start | bytes 1048576 | tf_op jit(solution)/shard_map/all_to_all | solution.py:221
  6.0 2.2 %copy-start = (bf16[1024,2048]{1,0:T(8,128)(2,1)S(1)}, bf16[1024,2048]{1,0:T(8,128)(2,1)}, u32[]{:S(2)}) copy-start(bf16[1024,2048]{1,0:T(8,128)(2,1)} %constant.8.clone.table_ref) | copy-start | bytes 12582916
  8.2 1.2 %copy-start.6 = (f32[1,256,1024]{2,1,0:T(8,128)S(1)}, f32[1,256,1024]{2,1,0:T(8,128)}, u32[]{:S(2)}) copy-start(f32[1,256,1024]{2,1,0:T(8,128)} %param.8) | copy-start | bytes 3145732
  9.4 1.3 %copy-start.3 = (bf16[1,2048,128]{2,1,0:T(8,128)(2,1)S(1)}, bf16[1,2048,128]{2,1,0:T(8,128)(2,1)}, u32[]{:S(2)}) copy-start(bf16[1,2048,128]{2,1,0:T(8,128)(2,1)} %param.6) | copy-start | bytes 1572868
  9.4 1.3 %copy-start.10 = (bf16[16,1,2048]{2,0,1:T(8,128)(2,1)S(1)}, bf16[16,1,2048]{2,0,1:T(8,128)(2,1)}, u32[]{:S(2)}) copy-start(bf16[16,1,2048]{2,0,1:T(8,128)(2,1)} %param.9) | copy-start | bytes 196612
  9.4 7.1 %copy-start.13 = (bf16[16,1,2048]{2,0,1:T(8,128)(2,1)S(1)}, bf16[16,1,2048]{2,0,1:T(8,128)(2,1)}, u32[]{:S(2)}) copy-start(bf16[16,1,2048]{2,0,1:T(8,128)(2,1)} %param.10) | copy-start | bytes 196612
  11.9 0.7 %copy-start.11 = (bf16[2,256,128]{2,1,0:T(8,128)(2,1)}, bf16[2,256,128]{2,1,0:T(8,128)(2,1)S(1)}, u32[]{:S(2)}) copy-start(bf16[2,256,128]{2,1,0:T(8,128)(2,1)S(1)} %get-tuple-element.31.refs_0_) | copy-start | bytes 393220
  12.6 0.7 %copy-start.15 = (bf16[2,256,128]{2,1,0:T(8,128)(2,1)}, bf16[2,256,128]{2,1,0:T(8,128)(2,1)S(1)}, u32[]{:S(2)}) copy-start(bf16[2,256,128]{2,1,0:T(8,128)(2,1)S(1)} %get-tuple-element.34) | copy-start | bytes 393220
  13.3 0.7 %copy-start.16 = (bf16[2,256,128]{2,1,0:T(8,128)(2,1)}, bf16[2,256,128]{2,1,0:T(8,128)(2,1)S(1)}, u32[]{:S(2)}) copy-start(bf16[2,256,128]{2,1,0:T(8,128)(2,1)S(1)} %get-tuple-element.33) | copy-start | bytes 393220
  13.9 0.7 %copy-start.17 = (bf16[2,256,128]{2,1,0:T(8,128)(2,1)}, bf16[2,256,128]{2,1,0:T(8,128)(2,1)S(1)}, u32[]{:S(2)}) copy-start(bf16[2,256,128]{2,1,0:T(8,128)(2,1)S(1)} %get-tuple-element.32) | copy-start | bytes 393220
  15.7 0.8 %copy-start.7 = (bf16[8,256,128]{2,1,0:T(8,128)(2,1)}, bf16[8,256,128]{2,1,0:T(8,128)(2,1)S(1)}, u32[]{:S(2)}) copy-start(bf16[8,256,128]{2,1,0:T(8,128)(2,1)S(1)} %all-to-all-done.grad_ref) | copy-start | bytes 1572868
  16.5 2.2 %copy-start.1 = (bf16[1024,2048]{1,0:T(8,128)(2,1)S(1)}, bf16[1024,2048]{1,0:T(8,128)(2,1)}, u32[]{:S(2)}) copy-start(bf16[1024,2048]{1,0:T(8,128)(2,1)} %constant.8.clone.table_ref) | copy-start | bytes 12582916
  18.7 1.0 %copy-start.8 = (bf16[8,256,128]{2,1,0:T(8,128)(2,1)S(1)}, bf16[8,256,128]{2,1,0:T(8,128)(2,1)}, u32[]{:S(2)}) copy-start(bf16[8,256,128]{2,1,0:T(8,128)(2,1)} %copy-done.7) | copy-start | bytes 1572868
  22.3 1.4 %copy-start.4 = (f32[256,2048]{1,0:T(8,128)}, f32[256,2048]{1,0:T(8,128)S(1)}, u32[]{:S(2)}) copy-start(f32[256,2048]{1,0:T(8,128)S(1)} %get-tuple-element.30.spec_ref) | copy-start | bytes 6291460
  23.7 0.7 %copy-start.9 = (bf16[32,32,128]{2,1,0:T(8,128)(2,1)}, bf16[32,32,128]{2,1,0:T(8,128)(2,1)S(1)}, u32[]{:S(2)}) copy-start(bf16[32,32,128]{2,1,0:T(8,128)(2,1)S(1)} %get-tuple-element.24) | copy-start | bytes 786436
  24.4 0.7 %copy-start.14 = (bf16[4,256,128]{2,1,0:T(8,128)(2,1)}, bf16[4,256,128]{2,1,0:T(8,128)(2,1)S(1)}, u32[]{:S(2)}) copy-start(bf16[4,256,128]{2,1,0:T(8,128)(2,1)S(1)} %get-tuple-element.23) | copy-start | bytes 786436
  25.1 29.3 %copy-start.5 = (f32[256,2048]{1,0:T(8,128)S(1)}, f32[256,2048]{1,0:T(8,128)}, u32[]{:S(2)}) copy-start(f32[256,2048]{1,0:T(8,128)} %copy-done.4) | copy-start | bytes 6291460
  25.1 15.4 %all-to-all-start.1 = ((bf16[32,32,128]{2,1,0:T(8,128)(2,1)}), bf16[32,32,128]{2,1,0:T(8,128)(2,1)S(1)}, u32[]{:S(2)}, u32[]{:S(2)}) async-start(bf16[32,32,128]{2,1,0:T(8,128)(2,1)} %copy-done.9), calls=%async_computation.1 | async-start | bytes 524288 | tf_op jit(solution)/shard_map/all_to_all | solution.py:251
  30.3 14.5 %collective-permute-start.1 = (bf16[4,256,128]{2,1,0:T(8,128)(2,1)}, bf16[4,256,128]{2,1,0:T(8,128)(2,1)}, u32[]{:S(2)}, u32[]{:S(2)}) collective-permute-start(bf16[4,256,128]{2,1,0:T(8,128)(2,1)} %copy-done.14), channel_id=1, source_target_pairs={{0,4},{4,0},{8,12},{12,8},{16,20},{20,16},{24,28},{28,24},{1,5},{5... | collective-permute-start | bytes 786440 | tf_op jit(solution)/shard_map/ppermute | solution.py:218
  40.5 13.9 %copy-start.12 = (bf16[2,256,128]{2,1,0:T(8,128)(2,1)S(1)}, bf16[2,256,128]{2,1,0:T(8,128)(2,1)}, u32[]{:S(2)}) copy-start(bf16[2,256,128]{2,1,0:T(8,128)(2,1)} %copy-done.11) | copy-start | bytes 393220
  40.9 5.9 %collective-permute-start.8 = (f32[16,2304]{1,0:T(8,128)S(1)}, f32[16,2304]{1,0:T(8,128)S(1)}, u32[]{:S(2)}, u32[]{:S(2)}) collective-permute-start(f32[16,2304]{1,0:T(8,128)S(1)} %get-tuple-element.35.own_ref), channel_id=1, source_target_pairs={{0,4},{4,0},{8,12},{12,8},{16,20},{20,16},{24,28},{28,24},{1,5},{5... | collective-permute-start | bytes 442376 | tf_op jit(solution)/shard_map/ppermute | solution.py:218
  41.3 6.6 %collective-permute-start.5 = (bf16[2,256,128]{2,1,0:T(8,128)(2,1)}, bf16[2,256,128]{2,1,0:T(8,128)(2,1)S(1)}, u32[]{:S(2)}, u32[]{:S(2)}) collective-permute-start(bf16[2,256,128]{2,1,0:T(8,128)(2,1)} %copy-done.17), channel_id=1, source_target_pairs={{0,8},{4,12},{8,0},{12,4},{16,24},{20,28},{24,16},{28,20},{1,9},{5... | collective-permute-start | bytes 393224 | tf_op jit(solution)/shard_map/ppermute | solution.py:218
  42.2 8.1 %collective-permute-start.6 = (bf16[2,256,128]{2,1,0:T(8,128)(2,1)}, bf16[2,256,128]{2,1,0:T(8,128)(2,1)S(1)}, u32[]{:S(2)}, u32[]{:S(2)}) collective-permute-start(bf16[2,256,128]{2,1,0:T(8,128)(2,1)} %copy-done.16), channel_id=1, source_target_pairs={{0,16},{4,20},{8,24},{12,28},{16,0},{20,4},{24,8},{28,12},{1,17},{... | collective-permute-start | bytes 393224 | tf_op jit(solution)/shard_map/ppermute | solution.py:218
  42.7 9.2 %collective-permute-start.7 = (bf16[2,256,128]{2,1,0:T(8,128)(2,1)}, bf16[2,256,128]{2,1,0:T(8,128)(2,1)S(1)}, u32[]{:S(2)}, u32[]{:S(2)}) collective-permute-start(bf16[2,256,128]{2,1,0:T(8,128)(2,1)} %copy-done.15), channel_id=1, source_target_pairs={{0,24},{4,28},{8,16},{12,20},{16,8},{20,12},{24,0},{28,4},{1,25},{... | collective-permute-start | bytes 393224 | tf_op jit(solution)/shard_map/ppermute | solution.py:218
  45.8 7.8 %collective-permute-start.2 = (bf16[2,256,128]{2,1,0:T(8,128)(2,1)S(1)}, bf16[2,256,128]{2,1,0:T(8,128)(2,1)S(1)}, u32[]{:S(2)}, u32[]{:S(2)}) collective-permute-start(bf16[2,256,128]{2,1,0:T(8,128)(2,1)S(1)} %get-tuple-element.26), channel_id=1, source_target_pairs={{0,8},{4,12},{8,0},{12,4},{16,24},{20,28},{24,16},{28,20},{1,9},{5... | collective-permute-start | bytes 393224 | tf_op jit(solution)/shard_map/ppermute | solution.py:218
  46.7 13.5 %collective-permute-start.3 = (bf16[2,256,128]{2,1,0:T(8,128)(2,1)S(1)}, bf16[2,256,128]{2,1,0:T(8,128)(2,1)S(1)}, u32[]{:S(2)}, u32[]{:S(2)}) collective-permute-start(bf16[2,256,128]{2,1,0:T(8,128)(2,1)S(1)} %get-tuple-element.27), channel_id=1, source_target_pairs={{0,16},{4,20},{8,24},{12,28},{16,0},{20,4},{24,8},{28,12},{1,17},{... | collective-permute-start | bytes 393224 | tf_op jit(solution)/shard_map/ppermute | solution.py:218
  47.8 12.4 %collective-permute-start.4 = (bf16[2,256,128]{2,1,0:T(8,128)(2,1)S(1)}, bf16[2,256,128]{2,1,0:T(8,128)(2,1)S(1)}, u32[]{:S(2)}, u32[]{:S(2)}) collective-permute-start(bf16[2,256,128]{2,1,0:T(8,128)(2,1)S(1)} %get-tuple-element.28), channel_id=1, source_target_pairs={{0,24},{4,28},{8,16},{12,20},{16,8},{20,12},{24,0},{28,4},{1,25},{... | collective-permute-start | bytes 393224 | tf_op jit(solution)/shard_map/ppermute | solution.py:218
  50.3 12.0 %collective-permute-start.11 = (bf16[16,2560]{1,0:T(8,128)(2,1)S(1)}, bf16[16,2560]{1,0:T(8,128)(2,1)S(1)}, u32[]{:S(2)}, u32[]{:S(2)}) collective-permute-start(bf16[16,2560]{1,0:T(8,128)(2,1)S(1)} %chip_sum.1.refs_0_), channel_id=1, source_target_pairs={{0,24},{4,28},{8,16},{12,20},{16,8},{20,12},{24,0},{28,4},{1,25},{... | collective-permute-start | bytes 245768 | tf_op jit(solution)/shard_map/ppermute | solution.py:218
  51.9 10.4 %collective-permute-start.10 = (bf16[16,2560]{1,0:T(8,128)(2,1)S(1)}, bf16[16,2560]{1,0:T(8,128)(2,1)S(1)}, u32[]{:S(2)}, u32[]{:S(2)}) collective-permute-start(bf16[16,2560]{1,0:T(8,128)(2,1)S(1)} %chip_sum.1.refs_0_), channel_id=1, source_target_pairs={{0,16},{4,20},{8,24},{12,28},{16,0},{20,4},{24,8},{28,12},{1,17},{... | collective-permute-start | bytes 245768 | tf_op jit(solution)/shard_map/ppermute | solution.py:218
  53.6 8.7 %collective-permute-start.9 = (bf16[16,2560]{1,0:T(8,128)(2,1)S(1)}, bf16[16,2560]{1,0:T(8,128)(2,1)S(1)}, u32[]{:S(2)}, u32[]{:S(2)}) collective-permute-start(bf16[16,2560]{1,0:T(8,128)(2,1)S(1)} %chip_sum.1.refs_0_), channel_id=1, source_target_pairs={{0,8},{4,12},{8,0},{12,4},{16,24},{20,28},{24,16},{28,20},{1,9},{5... | collective-permute-start | bytes 245768 | tf_op jit(solution)/shard_map/ppermute | solution.py:218
  54.4 2.2 %copy-start.2 = (bf16[1024,2048]{1,0:T(8,128)(2,1)S(1)}, bf16[1024,2048]{1,0:T(8,128)(2,1)}, u32[]{:S(2)}) copy-start(bf16[1024,2048]{1,0:T(8,128)(2,1)} %constant.8.clone.table_ref) | copy-start | bytes 12582916
where the time goes:
time: 63.6 us; the launch traced here: 63.1 us
  starting transfers between devices  21.9 us (34%)
  local copies, waits for them, and re-layouts  15 us (24%)
  Pallas kernels  13 us (20%)
  waiting for transfers between devices  12.4 us (19%)
  between operations  0.72 us (1%)
    unnamed x36, local copies, waits for them, and re-layouts  15 us
    pallas_call x9, Pallas kernels, call(): pl.pallas_call(kernel, out_shape=out_shape, in_specs=in_specs, scratch_sh...  13 us
    ppermute x12, starting transfers between devices, send(): return lax.ppermute(value, 'ctx', [(i, i ^ offset) for i in range(shards)])  11.9 us
    all_to_all x1, waiting for transfers between devices, dense_body(): rank_all = lax.all_to_all(rank_parts, ('ctx', 'grp'), 0, 0, tiled=True)  9.88 us
    all_to_all x1, starting transfers between devices, dense_body(): rank_all = lax.all_to_all(rank_parts, ('ctx', 'grp'), 0, 0, tiled=True)  5.18 us
    all_to_all x1, starting transfers between devices, dense_body(): lax.all_to_all(tok_grad.reshape(shards, chans, tokens), 'ctx', 0, 0, tile...  4.83 us
    ppermute x12, waiting for transfers between devices, send(): return lax.ppermute(value, 'ctx', [(i, i ^ offset) for i in range(shards)])  1.42 us
  transfers between devices with their start and end apart: 14, of which 4 were waited for; matrix products, arithmetic and copies ran while one was open for 0% of the time, Pallas kernels for 15%

commit v1 on v0

--- a/solution.py
+++ b/solution.py
@@ -74,8 +74,7 @@
     out_ref[...] = dot(filt_ref[...].astype(BF16), table_ref[...])
 
 
-def input_pack_kernel(index_ref, down_ref, tok_ref, sibling_ref, acts_ref, *pack_refs):
-    acts_ref[...] = dot(down_ref[...], tok_ref[...]).astype(BF16)
+def grad_pack_kernel(index_ref, tok_ref, sibling_ref, *pack_refs):
     chans = pack_refs[0].shape[1]
     for i, pack_ref in enumerate(pack_refs):
         rows = part(own_index(index_ref, 2 * i), chans)
@@ -83,15 +82,27 @@
         pack_ref[1] = sibling_ref[rows, :]
 
 
-def grad_u_kernel(
-    copies, index_ref, grad_ref, filt_spec_ref, up_ref, acts_ref, table_ref, spec_ref, du_ref, give_ref, rank_ref, cross
-):
+def input_pack_kernel(index_ref, down_ref, tok_ref, sibling_ref, acts_ref, *pack_refs):
+    acts_ref[...] = dot(down_ref[...], tok_ref[...]).astype(BF16)
+    grad_pack_kernel(index_ref, tok_ref, sibling_ref, *pack_refs)
+
+
+def unpack(index_ref, pack_refs, signal):
+    tokens = pack_refs[0].shape[2]
+    for i, pack_ref in enumerate(pack_refs):
+        for j in range(2):
+            signal[:, part(own_index(index_ref, 2 * i + j), tokens)] = pack_ref[j]
+
+
+def grad_u_kernel(copies, chips, index_ref, filt_spec_ref, up_ref, acts_ref, table_ref, *refs):
+    pack_refs, (spec_ref, du_ref, give_ref, rank_ref, signal, cross) = refs[:chips], refs[chips:]
     length = table_ref.shape[0]
-    shards, chans, tokens = grad_ref.shape
-    signal = jnp.concatenate([grad_ref[i] for i in range(shards)], axis=1)
+    shards = 2 * chips
+    _, chans, tokens = pack_refs[0].shape
+    unpack(index_ref, pack_refs, signal)
     for cols in blocks(table_ref):
         half = (cols.stop - cols.start) // 2
-        spec = dot(signal, table_ref[:, cols])
+        spec = dot(signal[...], table_ref[:, cols])
         spec_ref[:, cols] = spec
         cross[:, cols] = cross_spectrum(cols.start == 0, spec, filt_spec_ref[:, cols], half, 1.0 / length)
     grad_u = dot_nt(cross[...], table_ref[...]).astype(BF16)
@@ -143,9 +154,7 @@
     pack_refs, out_ref, signal, cross = refs[:-3], refs[-3], refs[-2], refs[-1]
     length = table_ref.shape[0]
     _, chans, tokens = pack_refs[0].shape
-    for i, pack_ref in enumerate(pack_refs):
-        for j in range(2):
-            signal[:, part(own_index(index_ref, 2 * i + j), tokens)] = pack_ref[j]
+    unpack(index_ref, pack_refs, signal)
     own_up = up_ref[:, part(own_index(index_ref, 0), chans)]
     act = (signal[...].astype(F32) + dot_tn(own_up, acts_ref[...])).astype(BF16)
     for cols in blocks(table_ref):
@@ -218,8 +227,11 @@
         return lax.ppermute(value, "ctx", [(i, i ^ offset) for i in range(shards)])
 
     pack = shape((2, chans, tokens), BF16)
-    chan_grad = lax.all_to_all(tok_grad.reshape(shards, chans, tokens), "ctx", 0, 0, tiled=True)
+    sibling_grad = send(tok_grad, 1)
     sibling_input = send(tok_input, 1)
+    grad_packs = call(grad_pack_kernel, "grad_pack", (pack,) * chips, (tok_grad, sibling_grad))
+    grad_packs, tok_input = lax.optimization_barrier((grad_packs, tok_input))
+    chan_grad = [grad_packs[0]] + [send(grad_packs[i], 2 * i) for i in range(1, chips)]
     acts_part, *input_packs = call(
         input_pack_kernel,
         "input_pack",
@@ -236,7 +248,7 @@
         index_first=False,
     )
     grad_spec, chan_du, give, rank_parts = call(
-        functools.partial(grad_u_kernel, groups),
+        functools.partial(grad_u_kernel, groups, chips),
         "grad_u",
         (
             shape((chans, 2 * length), F32),
@@ -244,10 +256,11 @@
             shape((chips, chans, tokens), BF16),
             shape((shards * groups, 2 * rank, tokens), BF16),
         ),
-        (chan_grad, filt_spec, up, acts_part, table),
-        scratch=[pltpu.VMEM((chans, 2 * length), BF16)],
+        (filt_spec, up, acts_part, table, *chan_grad),
+        scratch=[pltpu.VMEM((chans, length), BF16), pltpu.VMEM((chans, 2 * length), BF16)],
         flops=2 * product,
     )
+    rank_parts, chan_packs = lax.optimization_barrier((rank_parts, chan_packs))
     rank_all = lax.all_to_all(rank_parts, ("ctx", "grp"), 0, 0, tiled=True)
     got = send(give, 1)
     du_packs = call(du_pack_kernel, "du_pack", (pack,) * (chips - 1), (chan_du, got))

time: 63.6 us -> 58.3 us (0.917)
  local copies, waits for them, and re-layouts: 15 us -> 10.7 us
  waiting for transfers between devices: 12.4 us -> 13.5 us
  Pallas kernels: 13 us -> 12 us
  starting transfers between devices: 21.9 us -> 21 us
    all_to_all x1 -> x0, starting transfers between devices: 4.83 us -> none  [dense_body(): lax.all_to_all(tok_grad.reshape(shards, chans, tokens), 'ctx', 0, 0, tile...]
    unnamed x36, local copies, waits for them, and re-layouts: 15 us -> 10.7 us
    ppermute x12 -> x16, starting transfers between devices: 11.9 us -> 16.1 us  [send(): return lax.ppermute(value, 'ctx', [(i, i ^ offset) for i in range(shards)])]
    ppermute x12 -> x16, waiting for transfers between devices: 1.42 us -> 3.59 us  [send(): return lax.ppermute(value, 'ctx', [(i, i ^ offset) for i in range(shards)])]
    all_to_all x1 -> x0, waiting for transfers between devices: 1.15 us -> none  [dense_body(): lax.all_to_all(tok_grad.reshape(shards, chans, tokens), 'ctx', 0, 0, tile...]
    pallas_call x9 -> x10, Pallas kernels: 13 us -> 12 us  [call(): pl.pallas_call(kernel, out_shape=out_shape, in_specs=in_specs, scratch_sh...]
  transfers between devices with their start and end apart: 14 -> 17, of which waited for: 4 -> 4; matrix products, arithmetic and copies ran while one was open for 0% -> 0% of each run, Pallas kernels for 15% -> 19%
where the time goes in v1:
time: 58.3 us; the launch traced here: 57.9 us
  starting transfers between devices  21 us (36%)
  waiting for transfers between devices  13.5 us (23%)
  Pallas kernels  12 us (21%)
  local copies, waits for them, and re-layouts  10.7 us (18%)
  between operations  0.75 us (1%)
    ppermute x16, starting transfers between devices, send(): return lax.ppermute(value, 'ctx', [(i, i ^ offset) for i in range(shards)])  16.1 us
    pallas_call x10, Pallas kernels, call(): pl.pallas_call(kernel, out_shape=out_shape, in_specs=in_specs, scratch_sh...  12 us
    unnamed x36, local copies, waits for them, and re-layouts  10.7 us
    all_to_all x1, waiting for transfers between devices, dense_body(): rank_all = lax.all_to_all(rank_parts, ('ctx', 'grp'), 0, 0, tiled=True)  9.88 us
    all_to_all x1, starting transfers between devices, dense_body(): rank_all = lax.all_to_all(rank_parts, ('ctx', 'grp'), 0, 0, tiled=True)  4.84 us
    ppermute x16, waiting for transfers between devices, send(): return lax.ppermute(value, 'ctx', [(i, i ^ offset) for i in range(shards)])  3.59 us
  transfers between devices with their start and end apart: 17, of which 4 were waited for; matrix products, arithmetic and copies ran while one was open for 0% of the time, Pallas kernels for 19%

profile of v1, /device:TPU:0, one launch (start us, length us, event | category | flops | bytes accessed | tf_op | source)
XLA Modules:
  0.0 57.9 jit_solution(16190201989459713120)
XLA Ops:
  0.6 0.5 collective-permute-start
  1.1 0.1 collective-permute-start.1
  1.2 1.7 %collective-permute-done.sibling_ref = bf16[2048,128]{1,0:T(8,128)(2,1)S(1)} collective-permute-done((bf16[2048,128]{1,0:T(8,128)(2,1)}, bf16[2048,128]{1,0:T(8,128)(2,1)S(1)}, u32[]{:S(2)}, u32[]{:S(2)}) %collective-permute-start) | collective-permute-done | bytes 524320 | tf_op jit(solution)/shard_map/ppermute | solution.py:227
  2.9 1.0 %copy-done.5 = bf16[1,2048,128]{2,1,0:T(8,128)(2,1)S(1)} copy-done((bf16[1,2048,128]{2,1,0:T(8,128)(2,1)S(1)}, bf16[1,2048,128]{2,1,0:T(8,128)(2,1)}, u32[]{:S(2)}) %copy-start.5) | copy-done | bytes 524312
  4.0 2.9 %collective-permute-start.2 = (bf16[2,256,128]{2,1,0:T(8,128)(2,1)S(1)}, bf16[2,256,128]{2,1,0:T(8,128)(2,1)S(1)}, u32[]{:S(2)}, u32[]{:S(2)}) collective-permute-start(bf16[2,256,128]{2,1,0:T(8,128)(2,1)S(1)} %get-tuple-element.42), channel_id=1, source_target_pairs={{0,8},{4,12},{8,0},{12,4},{16,24},{20,28},{24,16},{28,20},{1,9},{5... | collective-permute-start | bytes 393224 | tf_op jit(solution)/shard_map/ppermute | solution.py:227
  6.9 1.5 %collective-permute-start.3 = (bf16[2,256,128]{2,1,0:T(8,128)(2,1)S(1)}, bf16[2,256,128]{2,1,0:T(8,128)(2,1)S(1)}, u32[]{:S(2)}, u32[]{:S(2)}) collective-permute-start(bf16[2,256,128]{2,1,0:T(8,128)(2,1)S(1)} %get-tuple-element.43), channel_id=1, source_target_pairs={{0,16},{4,20},{8,24},{12,28},{16,0},{20,4},{24,8},{28,12},{1,17},{... | collective-permute-start | bytes 393224 | tf_op jit(solution)/shard_map/ppermute | solution.py:227
  8.4 0.0 collective-permute-start.4
  8.4 2.2 %copy-done = bf16[1024,2048]{1,0:T(8,128)(2,1)S(1)} copy-done((bf16[1024,2048]{1,0:T(8,128)(2,1)S(1)}, bf16[1024,2048]{1,0:T(8,128)(2,1)}, u32[]{:S(2)}) %copy-start) | copy-done | bytes 4194328
  10.6 1.2 %copy-done.4 = f32[1,256,1024]{2,1,0:T(8,128)S(1)} copy-done((f32[1,256,1024]{2,1,0:T(8,128)S(1)}, f32[1,256,1024]{2,1,0:T(8,128)}, u32[]{:S(2)}) %copy-start.4) | copy-done | bytes 1048600
  11.9 1.2 %filter_spec.1.filt_spec_ref = f32[256,2048]{1,0:T(8,128)S(1)} custom-call(f32[256,1024]{1,0:T(8,128)S(1)} %bitcast.11, bf16[1024,2048]{1,0:T(8,128)(2,1)S(1)} %copy-done), custom_call_target="tpu_custom_call" | custom-call | flops 1073741824 | bytes 2097152 | tf_op jit(solution)/shard_map/filter_spec/pallas_call | solution.py:216
  13.1 0.0 collective-permute-done.1.sibling_ref
  13.2 0.2 input_pack.1
  13.3 0.7 %copy-done.8 = bf16[2,256,128]{2,1,0:T(8,128)(2,1)} copy-done((bf16[2,256,128]{2,1,0:T(8,128)(2,1)}, bf16[2,256,128]{2,1,0:T(8,128)(2,1)S(1)}, u32[]{:S(2)}) %copy-start.8) | copy-done | bytes 131096
  14.0 1.9 %collective-permute-start.6 = (bf16[2,256,128]{2,1,0:T(8,128)(2,1)S(1)}, bf16[2,256,128]{2,1,0:T(8,128)(2,1)S(1)}, u32[]{:S(2)}, u32[]{:S(2)}) collective-permute-start(bf16[2,256,128]{2,1,0:T(8,128)(2,1)S(1)} %get-tuple-element.49), channel_id=1, source_target_pairs={{0,8},{4,12},{8,0},{12,4},{16,24},{20,28},{24,16},{28,20},{1,9},{5... | collective-permute-start | bytes 393224 | tf_op jit(solution)/shard_map/ppermute | solution.py:227
  15.9 1.5 %collective-permute-start.7 = (bf16[2,256,128]{2,1,0:T(8,128)(2,1)S(1)}, bf16[2,256,128]{2,1,0:T(8,128)(2,1)S(1)}, u32[]{:S(2)}, u32[]{:S(2)}) collective-permute-start(bf16[2,256,128]{2,1,0:T(8,128)(2,1)S(1)} %get-tuple-element.50), channel_id=1, source_target_pairs={{0,16},{4,20},{8,24},{12,28},{16,0},{20,4},{24,8},{28,12},{1,17},{... | collective-permute-start | bytes 393224 | tf_op jit(solution)/shard_map/ppermute | solution.py:227
  17.5 0.0 collective-permute-done.2.refs_1_
  17.5 0.0 collective-permute-start.8
  17.5 0.0 collective-permute-done.3.refs_2_
  17.5 0.0 collective-permute-done.4.refs_3_
  17.5 2.7 %grad_u.1 = (f32[256,2048]{1,0:T(8,128)S(1)}, bf16[256,1024]{1,0:T(8,128)(2,1)S(1)}, bf16[4,256,128]{2,1,0:T(8,128)(2,1)S(1)}, bf16[32,32,128]{2,1,0:T(8,128)(2,1)S(1)}) custom-call(s32[1]{0:T(128)} %bitcast.index_ref, f32[256,2048]{1,0:T(8,128)S(1)} %filter_spec.1.filt_spec_ref, bf16[16,2048]{1,0:T(8,128)(2,1)S(1)} %bitcast.16, ...), custom_call_target="tpu_custom_call" | custom-call | flops 2147483648 | bytes 3145728 | tf_op jit(solution)/shard_map/grad_u/pallas_call | solution.py:216
  20.2 0.7 %copy-done.6 = bf16[32,32,128]{2,1,0:T(8,128)(2,1)} copy-done((bf16[32,32,128]{2,1,0:T(8,128)(2,1)}, bf16[32,32,128]{2,1,0:T(8,128)(2,1)S(1)}, u32[]{:S(2)}) %copy-start.6) | copy-done | bytes 262168
  20.9 0.7 %copy-done.17 = bf16[4,256,128]{2,1,0:T(8,128)(2,1)} copy-done((bf16[4,256,128]{2,1,0:T(8,128)(2,1)}, bf16[4,256,128]{2,1,0:T(8,128)(2,1)S(1)}, u32[]{:S(2)}) %copy-start.17) | copy-done | bytes 262168
  21.6 0.0 collective-permute-done.6.refs_1_
  21.6 0.7 %copy-done.10 = bf16[2,256,128]{2,1,0:T(8,128)(2,1)} copy-done((bf16[2,256,128]{2,1,0:T(8,128)(2,1)}, bf16[2,256,128]{2,1,0:T(8,128)(2,1)S(1)}, u32[]{:S(2)}) %copy-start.10) | copy-done | bytes 131096
  22.3 1.5 %collective-permute-done.7.refs_2_ = bf16[2,256,128]{2,1,0:T(8,128)(2,1)S(1)} collective-permute-done((bf16[2,256,128]{2,1,0:T(8,128)(2,1)S(1)}, bf16[2,256,128]{2,1,0:T(8,128)(2,1)S(1)}, u32[]{:S(2)}, u32[]{:S(2)}) %collective-permute-start.7) | collective-permute-done | bytes 131104 | tf_op jit(solution)/shard_map/ppermute | solution.py:227
  23.7 0.7 %copy-done.12 = bf16[2,256,128]{2,1,0:T(8,128)(2,1)} copy-done((bf16[2,256,128]{2,1,0:T(8,128)(2,1)}, bf16[2,256,128]{2,1,0:T(8,128)(2,1)S(1)}, u32[]{:S(2)}) %copy-start.12) | copy-done | bytes 131096
  24.4 0.6 %copy-done.14 = bf16[2,256,128]{2,1,0:T(8,128)(2,1)} copy-done((bf16[2,256,128]{2,1,0:T(8,128)(2,1)}, bf16[2,256,128]{2,1,0:T(8,128)(2,1)S(1)}, u32[]{:S(2)}) %copy-start.14) | copy-done | bytes 131096
  25.0 4.8 %all-to-all-start = ((bf16[32,32,128]{2,1,0:T(8,128)(2,1)}), bf16[32,32,128]{2,1,0:T(8,128)(2,1)S(1)}, u32[]{:S(2)}, u32[]{:S(2)}) async-start(bf16[32,32,128]{2,1,0:T(8,128)(2,1)} %copy-done.6), calls=%async_computation | async-start | bytes 524288 | tf_op jit(solution)/shard_map/all_to_all | solution.py:264
  29.9 0.3 collective-permute-start.5
  30.2 9.9 %all-to-all-done.parts_ref = bf16[32,32,128]{2,1,0:T(8,128)(2,1)S(1)} async-done(((bf16[32,32,128]{2,1,0:T(8,128)(2,1)}), bf16[32,32,128]{2,1,0:T(8,128)(2,1)S(1)}, u32[]{:S(2)}, u32[]{:S(2)}) %all-to-all-start) | async-done | bytes 262176 | tf_op jit(solution)/shard_map/all_to_all | solution.py:264
  40.1 0.4 rank_grad.1
  40.5 0.4 collective-permute-start.12
  40.9 1.0 %du_pack.1 = (bf16[2,256,128]{2,1,0:T(8,128)(2,1)S(1)}, bf16[2,256,128]{2,1,0:T(8,128)(2,1)S(1)}, bf16[2,256,128]{2,1,0:T(8,128)(2,1)S(1)}) custom-call(s32[1]{0:T(128)} %bitcast.index_ref, bf16[256,1024]{1,0:T(8,128)(2,1)S(1)} %get-tuple-element.45.du_ref, bf16[4,256,128]{2,1,0:T(8,128)(2,1)} %collective-permute-done.5.got_ref), custom_call_target="tpu_custom_call" | custom-call | bytes 393216 | tf_op jit(solution)/shard_map/du_pack/pallas_call | solution.py:216
  41.9 1.0 %collective-permute-start.9 = (bf16[2,256,128]{2,1,0:T(8,128)(2,1)S(1)}, bf16[2,256,128]{2,1,0:T(8,128)(2,1)S(1)}, u32[]{:S(2)}, u32[]{:S(2)}) collective-permute-start(bf16[2,256,128]{2,1,0:T(8,128)(2,1)S(1)} %get-tuple-element.54), channel_id=1, source_target_pairs={{0,8},{4,12},{8,0},{12,4},{16,24},{20,28},{24,16},{28,20},{1,9},{5... | collective-permute-start | bytes 393224 | tf_op jit(solution)/shard_map/ppermute | solution.py:227
  42.9 0.6 collective-permute-start.10
  43.4 2.1 %collective-permute-start.11 = (bf16[2,256,128]{2,1,0:T(8,128)(2,1)S(1)}, bf16[2,256,128]{2,1,0:T(8,128)(2,1)S(1)}, u32[]{:S(2)}, u32[]{:S(2)}) collective-permute-start(bf16[2,256,128]{2,1,0:T(8,128)(2,1)S(1)} %get-tuple-element.56), channel_id=1, source_target_pairs={{0,24},{4,28},{8,16},{12,20},{16,8},{20,12},{24,0},{28,4},{1,25},{... | collective-permute-start | bytes 393224 | tf_op jit(solution)/shard_map/ppermute | solution.py:227
  45.5 0.0 collective-permute-done.12.other_ref
  45.5 0.9 %collective-permute-start.15 = (bf16[16,2560]{1,0:T(8,128)(2,1)S(1)}, bf16[16,2560]{1,0:T(8,128)(2,1)S(1)}, u32[]{:S(2)}, u32[]{:S(2)}) collective-permute-start(bf16[16,2560]{1,0:T(8,128)(2,1)S(1)} %chip_sum.1.refs_0_), channel_id=1, source_target_pairs={{0,24},{4,28},{8,16},{12,20},{16,8},{20,12},{24,0},{28,4},{1,25},{... | collective-permute-start | bytes 245768 | tf_op jit(solution)/shard_map/ppermute | solution.py:227
  46.4 1.5 %collective-permute-start.14 = (bf16[16,2560]{1,0:T(8,128)(2,1)S(1)}, bf16[16,2560]{1,0:T(8,128)(2,1)S(1)}, u32[]{:S(2)}, u32[]{:S(2)}) collective-permute-start(bf16[16,2560]{1,0:T(8,128)(2,1)S(1)} %chip_sum.1.refs_0_), channel_id=1, source_target_pairs={{0,16},{4,20},{8,24},{12,28},{16,0},{20,4},{24,8},{28,12},{1,17},{... | collective-permute-start | bytes 245768 | tf_op jit(solution)/shard_map/ppermute | solution.py:227
  47.9 0.4 collective-permute-done.9.refs_0_
  48.3 0.9 %collective-permute-start.13 = (bf16[16,2560]{1,0:T(8,128)(2,1)S(1)}, bf16[16,2560]{1,0:T(8,128)(2,1)S(1)}, u32[]{:S(2)}, u32[]{:S(2)}) collective-permute-start(bf16[16,2560]{1,0:T(8,128)(2,1)S(1)} %chip_sum.1.refs_0_), channel_id=1, source_target_pairs={{0,8},{4,12},{8,0},{12,4},{16,24},{20,28},{24,16},{28,20},{1,9},{5... | collective-permute-start | bytes 245768 | tf_op jit(solution)/shard_map/ppermute | solution.py:227
  49.2 0.0 copy-start.2
  49.2 2.2 %copy-done.2 = bf16[1024,2048]{1,0:T(8,128)(2,1)S(1)} copy-done((bf16[1024,2048]{1,0:T(8,128)(2,1)S(1)}, bf16[1024,2048]{1,0:T(8,128)(2,1)}, u32[]{:S(2)}) %copy-start.2) | copy-done | bytes 4194328
  51.4 3.6 %filter_grad.1 = f32[256,1024]{1,0:T(8,128)} custom-call(s32[1]{0:T(128)} %bitcast.index_ref, bf16[16,1024]{1,0:T(8,128)(2,1)S(1)} %get-tuple-element.57.acts_ref, bf16[16,2048]{1,0:T(8,128)(2,1)S(1)} %bitcast.17, f32[256,2048]{1,0:T(8,128)S(1)} %get-tuple-element.58.spec_ref, bf16[1024,2048]{1,0:T(8,128)(2,1)S(1)} %copy-done.2, ...), custom_call_target="tpu_custom_call" | custom-call | flops 2147483648 | bytes 1048576 | tf_op jit(solution)/shard_map/filter_grad/pallas_call | solution.py:216
  55.0 2.1 %input_grad.1 = bf16[2048,128]{1,0:T(8,128)(2,1)} custom-call(s32[1]{0:T(128)} %bitcast.index_ref, bf16[256,1024]{1,0:T(8,128)(2,1)S(1)} %get-tuple-element.45.du_ref, bf16[4,256,128]{2,1,0:T(8,128)(2,1)} %collective-permute-done.5.got_ref, bf16[16,2048]{1,0:T(8,128)(2,1)S(1)} %bitcast.15, bf16[16,128]{1,0:T(8,128)(2,1)S(1)} %get-tuple-element.53.rank_ref, ...), custom_call_target="tpu_custom_call" | custom-call | bytes 524288 | tf_op jit(solution)/shard_map/input_grad/pallas_call | solution.py:216
  57.1 0.0 collective-permute-done.14.refs_2_
  57.1 0.0 collective-permute-done.13.refs_1_
  57.1 0.8 %adapter_sum.1 = (f32[16,1,2048]{2,1,0:T(1,128)}, f32[16,1,2048]{2,1,0:T(1,128)}) custom-call(s32[1]{0:T(128)} %bitcast.index_ref, bf16[16,2560]{1,0:T(8,128)(2,1)S(1)} %chip_sum.1.refs_0_, bf16[16,2560]{1,0:T(8,128)(2,1)S(1)} %collective-permute-done.13.refs_1_, bf16[16,2560]{1,0:T(8,128)(2,1)S(1)} %collective-permute-done.14.refs_2_, ...), custom_call_target="tpu_custom_call" | custom-call | bytes 262144 | tf_op jit(solution)/shard_map/adapter_sum/pallas_call | solution.py:216
  (32 shorter events, 0.1 us)
Async XLA Ops:
  0.6 2.3 %collective-permute-start = (bf16[2048,128]{1,0:T(8,128)(2,1)}, bf16[2048,128]{1,0:T(8,128)(2,1)S(1)}, u32[]{:S(2)}, u32[]{:S(2)}) collective-permute-start(bf16[2048,128]{1,0:T(8,128)(2,1)} %bitcast.12), channel_id=1, source_target_pairs={{0,4},{4,0},{8,12},{12,8},{16,20},{20,16},{24,28},{28,24},{1,5},{5... | collective-permute-start | bytes 1572872 | tf_op jit(solution)/shard_map/ppermute | solution.py:227
  1.1 12.0 %collective-permute-start.1 = (bf16[2048,128]{1,0:T(8,128)(2,1)}, bf16[2048,128]{1,0:T(8,128)(2,1)S(1)}, u32[]{:S(2)}, u32[]{:S(2)}) collective-permute-start(bf16[2048,128]{1,0:T(8,128)(2,1)} %bitcast.8), channel_id=1, source_target_pairs={{0,4},{4,0},{8,12},{12,8},{16,20},{20,16},{24,28},{28,24},{1,5},{5... | collective-permute-start | bytes 1572872 | tf_op jit(solution)/shard_map/ppermute | solution.py:227
  2.9 1.0 %copy-start.5 = (bf16[1,2048,128]{2,1,0:T(8,128)(2,1)S(1)}, bf16[1,2048,128]{2,1,0:T(8,128)(2,1)}, u32[]{:S(2)}) copy-start(bf16[1,2048,128]{2,1,0:T(8,128)(2,1)} %param.7) | copy-start | bytes 1572868
  4.0 13.5 %collective-permute-start.2 = (bf16[2,256,128]{2,1,0:T(8,128)(2,1)S(1)}, bf16[2,256,128]{2,1,0:T(8,128)(2,1)S(1)}, u32[]{:S(2)}, u32[]{:S(2)}) collective-permute-start(bf16[2,256,128]{2,1,0:T(8,128)(2,1)S(1)} %get-tuple-element.42), channel_id=1, source_target_pairs={{0,8},{4,12},{8,0},{12,4},{16,24},{20,28},{24,16},{28,20},{1,9},{5... | collective-permute-start | bytes 393224 | tf_op jit(solution)/shard_map/ppermute | solution.py:227
  6.9 10.6 %collective-permute-start.3 = (bf16[2,256,128]{2,1,0:T(8,128)(2,1)S(1)}, bf16[2,256,128]{2,1,0:T(8,128)(2,1)S(1)}, u32[]{:S(2)}, u32[]{:S(2)}) collective-permute-start(bf16[2,256,128]{2,1,0:T(8,128)(2,1)S(1)} %get-tuple-element.43), channel_id=1, source_target_pairs={{0,16},{4,20},{8,24},{12,28},{16,0},{20,4},{24,8},{28,12},{1,17},{... | collective-permute-start | bytes 393224 | tf_op jit(solution)/shard_map/ppermute | solution.py:227
  8.4 9.1 %collective-permute-start.4 = (bf16[2,256,128]{2,1,0:T(8,128)(2,1)S(1)}, bf16[2,256,128]{2,1,0:T(8,128)(2,1)S(1)}, u32[]{:S(2)}, u32[]{:S(2)}) collective-permute-start(bf16[2,256,128]{2,1,0:T(8,128)(2,1)S(1)} %get-tuple-element.44), channel_id=1, source_target_pairs={{0,24},{4,28},{8,16},{12,20},{16,8},{20,12},{24,0},{28,4},{1,25},{... | collective-permute-start | bytes 393224 | tf_op jit(solution)/shard_map/ppermute | solution.py:227
  8.4 2.2 %copy-start = (bf16[1024,2048]{1,0:T(8,128)(2,1)S(1)}, bf16[1024,2048]{1,0:T(8,128)(2,1)}, u32[]{:S(2)}) copy-start(bf16[1024,2048]{1,0:T(8,128)(2,1)} %constant.8.clone.table_ref) | copy-start | bytes 12582916
  10.6 1.2 %copy-start.4 = (f32[1,256,1024]{2,1,0:T(8,128)S(1)}, f32[1,256,1024]{2,1,0:T(8,128)}, u32[]{:S(2)}) copy-start(f32[1,256,1024]{2,1,0:T(8,128)} %param.8) | copy-start | bytes 3145732
  11.9 1.3 %copy-start.3 = (bf16[1,2048,128]{2,1,0:T(8,128)(2,1)S(1)}, bf16[1,2048,128]{2,1,0:T(8,128)(2,1)}, u32[]{:S(2)}) copy-start(bf16[1,2048,128]{2,1,0:T(8,128)(2,1)} %param.6) | copy-start | bytes 1572868
  11.9 1.3 %copy-start.7 = (bf16[16,1,2048]{2,0,1:T(8,128)(2,1)S(1)}, bf16[16,1,2048]{2,0,1:T(8,128)(2,1)}, u32[]{:S(2)}) copy-start(bf16[16,1,2048]{2,0,1:T(8,128)(2,1)} %param.9) | copy-start | bytes 196612
  11.9 5.6 %copy-start.1 = (bf16[1024,2048]{1,0:T(8,128)(2,1)S(1)}, bf16[1024,2048]{1,0:T(8,128)(2,1)}, u32[]{:S(2)}) copy-start(bf16[1024,2048]{1,0:T(8,128)(2,1)} %constant.8.clone.table_ref) | copy-start | bytes 12582916
  11.9 5.6 %copy-start.16 = (bf16[16,1,2048]{2,0,1:T(8,128)(2,1)S(1)}, bf16[16,1,2048]{2,0,1:T(8,128)(2,1)}, u32[]{:S(2)}) copy-start(bf16[16,1,2048]{2,0,1:T(8,128)(2,1)} %param.10) | copy-start | bytes 196612
  13.3 0.7 %copy-start.8 = (bf16[2,256,128]{2,1,0:T(8,128)(2,1)}, bf16[2,256,128]{2,1,0:T(8,128)(2,1)S(1)}, u32[]{:S(2)}) copy-start(bf16[2,256,128]{2,1,0:T(8,128)(2,1)S(1)} %get-tuple-element.59.refs_0_) | copy-start | bytes 393220
  14.0 7.6 %collective-permute-start.6 = (bf16[2,256,128]{2,1,0:T(8,128)(2,1)S(1)}, bf16[2,256,128]{2,1,0:T(8,128)(2,1)S(1)}, u32[]{:S(2)}, u32[]{:S(2)}) collective-permute-start(bf16[2,256,128]{2,1,0:T(8,128)(2,1)S(1)} %get-tuple-element.49), channel_id=1, source_target_pairs={{0,8},{4,12},{8,0},{12,4},{16,24},{20,28},{24,16},{28,20},{1,9},{5... | collective-permute-start | bytes 393224 | tf_op jit(solution)/shard_map/ppermute | solution.py:227
  15.9 7.8 %collective-permute-start.7 = (bf16[2,256,128]{2,1,0:T(8,128)(2,1)S(1)}, bf16[2,256,128]{2,1,0:T(8,128)(2,1)S(1)}, u32[]{:S(2)}, u32[]{:S(2)}) collective-permute-start(bf16[2,256,128]{2,1,0:T(8,128)(2,1)S(1)} %get-tuple-element.50), channel_id=1, source_target_pairs={{0,16},{4,20},{8,24},{12,28},{16,0},{20,4},{24,8},{28,12},{1,17},{... | collective-permute-start | bytes 393224 | tf_op jit(solution)/shard_map/ppermute | solution.py:227
  17.5 6.9 %collective-permute-start.8 = (bf16[2,256,128]{2,1,0:T(8,128)(2,1)S(1)}, bf16[2,256,128]{2,1,0:T(8,128)(2,1)S(1)}, u32[]{:S(2)}, u32[]{:S(2)}) collective-permute-start(bf16[2,256,128]{2,1,0:T(8,128)(2,1)S(1)} %get-tuple-element.51), channel_id=1, source_target_pairs={{0,24},{4,28},{8,16},{12,20},{16,8},{20,12},{24,0},{28,4},{1,25},{... | collective-permute-start | bytes 393224 | tf_op jit(solution)/shard_map/ppermute | solution.py:227
  20.2 0.7 %copy-start.6 = (bf16[32,32,128]{2,1,0:T(8,128)(2,1)}, bf16[32,32,128]{2,1,0:T(8,128)(2,1)S(1)}, u32[]{:S(2)}) copy-start(bf16[32,32,128]{2,1,0:T(8,128)(2,1)S(1)} %get-tuple-element.52) | copy-start | bytes 786436
  20.9 0.7 %copy-start.17 = (bf16[4,256,128]{2,1,0:T(8,128)(2,1)}, bf16[4,256,128]{2,1,0:T(8,128)(2,1)S(1)}, u32[]{:S(2)}) copy-start(bf16[4,256,128]{2,1,0:T(8,128)(2,1)S(1)} %get-tuple-element.46) | copy-start | bytes 786436
  21.6 0.7 %copy-start.10 = (bf16[2,256,128]{2,1,0:T(8,128)(2,1)}, bf16[2,256,128]{2,1,0:T(8,128)(2,1)S(1)}, u32[]{:S(2)}) copy-start(bf16[2,256,128]{2,1,0:T(8,128)(2,1)S(1)} %collective-permute-done.6.refs_1_) | copy-start | bytes 393220
  23.7 0.7 %copy-start.12 = (bf16[2,256,128]{2,1,0:T(8,128)(2,1)}, bf16[2,256,128]{2,1,0:T(8,128)(2,1)S(1)}, u32[]{:S(2)}) copy-start(bf16[2,256,128]{2,1,0:T(8,128)(2,1)S(1)} %collective-permute-done.7.refs_2_) | copy-start | bytes 393220
  24.4 0.6 %copy-start.14 = (bf16[2,256,128]{2,1,0:T(8,128)(2,1)}, bf16[2,256,128]{2,1,0:T(8,128)(2,1)S(1)}, u32[]{:S(2)}) copy-start(bf16[2,256,128]{2,1,0:T(8,128)(2,1)S(1)} %collective-permute-done.8.refs_3_) | copy-start | bytes 393220
  25.0 15.0 %all-to-all-start = ((bf16[32,32,128]{2,1,0:T(8,128)(2,1)}), bf16[32,32,128]{2,1,0:T(8,128)(2,1)S(1)}, u32[]{:S(2)}, u32[]{:S(2)}) async-start(bf16[32,32,128]{2,1,0:T(8,128)(2,1)} %copy-done.6), calls=%async_computation | async-start | bytes 524288 | tf_op jit(solution)/shard_map/all_to_all | solution.py:264
  29.9 11.0 %collective-permute-start.5 = (bf16[4,256,128]{2,1,0:T(8,128)(2,1)}, bf16[4,256,128]{2,1,0:T(8,128)(2,1)}, u32[]{:S(2)}, u32[]{:S(2)}) collective-permute-start(bf16[4,256,128]{2,1,0:T(8,128)(2,1)} %copy-done.17), channel_id=1, source_target_pairs={{0,4},{4,0},{8,12},{12,8},{16,20},{20,16},{24,28},{28,24},{1,5},{5... | collective-permute-start | bytes 786440 | tf_op jit(solution)/shard_map/ppermute | solution.py:227
  40.1 9.1 %copy-start.9 = (bf16[2,256,128]{2,1,0:T(8,128)(2,1)S(1)}, bf16[2,256,128]{2,1,0:T(8,128)(2,1)}, u32[]{:S(2)}) copy-start(bf16[2,256,128]{2,1,0:T(8,128)(2,1)} %copy-done.8) | copy-start | bytes 393220
  40.1 9.1 %copy-start.11 = (bf16[2,256,128]{2,1,0:T(8,128)(2,1)S(1)}, bf16[2,256,128]{2,1,0:T(8,128)(2,1)}, u32[]{:S(2)}) copy-start(bf16[2,256,128]{2,1,0:T(8,128)(2,1)} %copy-done.10) | copy-start | bytes 393220
  40.1 9.1 %copy-start.13 = (bf16[2,256,128]{2,1,0:T(8,128)(2,1)S(1)}, bf16[2,256,128]{2,1,0:T(8,128)(2,1)}, u32[]{:S(2)}) copy-start(bf16[2,256,128]{2,1,0:T(8,128)(2,1)} %copy-done.12) | copy-start | bytes 393220
  40.1 9.1 %copy-start.15 = (bf16[2,256,128]{2,1,0:T(8,128)(2,1)S(1)}, bf16[2,256,128]{2,1,0:T(8,128)(2,1)}, u32[]{:S(2)}) copy-start(bf16[2,256,128]{2,1,0:T(8,128)(2,1)} %copy-done.14) | copy-start | bytes 393220
  40.5 5.0 %collective-permute-start.12 = (f32[16,2304]{1,0:T(8,128)S(1)}, f32[16,2304]{1,0:T(8,128)S(1)}, u32[]{:S(2)}, u32[]{:S(2)}) collective-permute-start(f32[16,2304]{1,0:T(8,128)S(1)} %get-tuple-element.63.own_ref), channel_id=1, source_target_pairs={{0,4},{4,0},{8,12},{12,8},{16,20},{20,16},{24,28},{28,24},{1,5},{5... | collective-permute-start | bytes 442376 | tf_op jit(solution)/shard_map/ppermute | solution.py:227
  41.9 6.4 %collective-permute-start.9 = (bf16[2,256,128]{2,1,0:T(8,128)(2,1)S(1)}, bf16[2,256,128]{2,1,0:T(8,128)(2,1)S(1)}, u32[]{:S(2)}, u32[]{:S(2)}) collective-permute-start(bf16[2,256,128]{2,1,0:T(8,128)(2,1)S(1)} %get-tuple-element.54), channel_id=1, source_target_pairs={{0,8},{4,12},{8,0},{12,4},{16,24},{20,28},{24,16},{28,20},{1,9},{5... | collective-permute-start | bytes 393224 | tf_op jit(solution)/shard_map/ppermute | solution.py:227
  42.9 12.2 %collective-permute-start.10 = (bf16[2,256,128]{2,1,0:T(8,128)(2,1)S(1)}, bf16[2,256,128]{2,1,0:T(8,128)(2,1)S(1)}, u32[]{:S(2)}, u32[]{:S(2)}) collective-permute-start(bf16[2,256,128]{2,1,0:T(8,128)(2,1)S(1)} %get-tuple-element.55), channel_id=1, source_target_pairs={{0,16},{4,20},{8,24},{12,28},{16,0},{20,4},{24,8},{28,12},{1,17},{... | collective-permute-start | bytes 393224 | tf_op jit(solution)/shard_map/ppermute | solution.py:227
  43.4 11.6 %collective-permute-start.11 = (bf16[2,256,128]{2,1,0:T(8,128)(2,1)S(1)}, bf16[2,256,128]{2,1,0:T(8,128)(2,1)S(1)}, u32[]{:S(2)}, u32[]{:S(2)}) collective-permute-start(bf16[2,256,128]{2,1,0:T(8,128)(2,1)S(1)} %get-tuple-element.56), channel_id=1, source_target_pairs={{0,24},{4,28},{8,16},{12,20},{16,8},{20,12},{24,0},{28,4},{1,25},{... | collective-permute-start | bytes 393224 | tf_op jit(solution)/shard_map/ppermute | solution.py:227
  45.5 11.6 %collective-permute-start.15 = (bf16[16,2560]{1,0:T(8,128)(2,1)S(1)}, bf16[16,2560]{1,0:T(8,128)(2,1)S(1)}, u32[]{:S(2)}, u32[]{:S(2)}) collective-permute-start(bf16[16,2560]{1,0:T(8,128)(2,1)S(1)} %chip_sum.1.refs_0_), channel_id=1, source_target_pairs={{0,24},{4,28},{8,16},{12,20},{16,8},{20,12},{24,0},{28,4},{1,25},{... | collective-permute-start | bytes 245768 | tf_op jit(solution)/shard_map/ppermute | solution.py:227
  46.4 10.7 %collective-permute-start.14 = (bf16[16,2560]{1,0:T(8,128)(2,1)S(1)}, bf16[16,2560]{1,0:T(8,128)(2,1)S(1)}, u32[]{:S(2)}, u32[]{:S(2)}) collective-permute-start(bf16[16,2560]{1,0:T(8,128)(2,1)S(1)} %chip_sum.1.refs_0_), channel_id=1, source_target_pairs={{0,16},{4,20},{8,24},{12,28},{16,0},{20,4},{24,8},{28,12},{1,17},{... | collective-permute-start | bytes 245768 | tf_op jit(solution)/shard_map/ppermute | solution.py:227
  48.3 8.8 %collective-permute-start.13 = (bf16[16,2560]{1,0:T(8,128)(2,1)S(1)}, bf16[16,2560]{1,0:T(8,128)(2,1)S(1)}, u32[]{:S(2)}, u32[]{:S(2)}) collective-permute-start(bf16[16,2560]{1,0:T(8,128)(2,1)S(1)} %chip_sum.1.refs_0_), channel_id=1, source_target_pairs={{0,8},{4,12},{8,0},{12,4},{16,24},{20,28},{24,16},{28,20},{1,9},{5... | collective-permute-start | bytes 245768 | tf_op jit(solution)/shard_map/ppermute | solution.py:227
  49.2 2.2 %copy-start.2 = (bf16[1024,2048]{1,0:T(8,128)(2,1)S(1)}, bf16[1024,2048]{1,0:T(8,128)(2,1)}, u32[]{:S(2)}) copy-start(bf16[1024,2048]{1,0:T(8,128)(2,1)} %constant.8.clone.table_ref) | copy-start | bytes 12582916

commit v2 on v1

--- a/solution.py
+++ b/solution.py
@@ -15,7 +15,7 @@
 F32 = jnp.float32
 TABLE_ENTRIES = 1 << 22
 HALF = 256
-VMEM_BYTES = 20 * 1024 * 1024
+VMEM_BYTES = 16 << 20
 
 
 @functools.lru_cache(maxsize=None)
@@ -45,8 +45,8 @@
     return jax.ShapeDtypeStruct(dims, kind)
 
 
-def own_index(index_ref, offset):
-    return jnp.bitwise_xor(index_ref[0], offset)
+def own_index(offset):
+    return jnp.bitwise_xor(lax.axis_index("ctx"), offset)
 
 
 def part(index, size):
@@ -70,76 +70,96 @@
     return [slice(i, i + width) for i in range(0, period, width)]
 
 
-def filter_spec_kernel(filt_ref, table_ref, out_ref):
-    out_ref[...] = dot(filt_ref[...].astype(BF16), table_ref[...])
-
-
-def grad_pack_kernel(index_ref, tok_ref, sibling_ref, *pack_refs):
+def pack_kernel(tok_ref, sibling_ref, *pack_refs):
     chans = pack_refs[0].shape[1]
     for i, pack_ref in enumerate(pack_refs):
-        rows = part(own_index(index_ref, 2 * i), chans)
+        rows = part(own_index(2 * i), chans)
         pack_ref[0] = tok_ref[rows, :]
         pack_ref[1] = sibling_ref[rows, :]
 
 
-def input_pack_kernel(index_ref, down_ref, tok_ref, sibling_ref, acts_ref, *pack_refs):
-    acts_ref[...] = dot(down_ref[...], tok_ref[...]).astype(BF16)
-    grad_pack_kernel(index_ref, tok_ref, sibling_ref, *pack_refs)
-
-
-def unpack(index_ref, pack_refs, signal):
+def unpack(pack_refs, signal):
     tokens = pack_refs[0].shape[2]
     for i, pack_ref in enumerate(pack_refs):
         for j in range(2):
-            signal[:, part(own_index(index_ref, 2 * i + j), tokens)] = pack_ref[j]
-
-
-def grad_u_kernel(copies, chips, index_ref, filt_spec_ref, up_ref, acts_ref, table_ref, *refs):
-    pack_refs, (spec_ref, du_ref, give_ref, rank_ref, signal, cross) = refs[:chips], refs[chips:]
+            signal[:, part(own_index(2 * i + j), tokens)] = pack_ref[j]
+
+
+def filter_spec_kernel(filt_ref, tok_ref, table_ref, down_ref, spec_ref, acts_ref):
+    spec_ref[...] = dot(filt_ref[...].astype(BF16), table_ref[...])
+    acts_ref[...] = dot(down_ref[...], tok_ref[...]).astype(BF16)
+
+
+def grad_u_kernel(filt_spec_ref, up_ref, acts_ref, table_ref, *refs):
+    pack_refs, (spec_ref, keep_ref, give_ref, signal, cross, du, rank) = refs[:-7], refs[-7:]
     length = table_ref.shape[0]
-    shards = 2 * chips
+    chips = len(pack_refs)
     _, chans, tokens = pack_refs[0].shape
-    unpack(index_ref, pack_refs, signal)
+    ranks = up_ref.shape[0]
+    unpack(pack_refs, signal)
     for cols in blocks(table_ref):
         half = (cols.stop - cols.start) // 2
         spec = dot(signal[...], table_ref[:, cols])
         spec_ref[:, cols] = spec
         cross[:, cols] = cross_spectrum(cols.start == 0, spec, filt_spec_ref[:, cols], half, 1.0 / length)
     grad_u = dot_nt(cross[...], table_ref[...]).astype(BF16)
-    du_ref[...] = grad_u
-    for i in range(shards // 2):
-        give_ref[i] = du_ref[:, part(own_index(index_ref, 2 * i + 1), tokens)]
-    rank = dot(up_ref[:, part(own_index(index_ref, 0), chans)], grad_u).astype(BF16)
-    both = [jnp.concatenate([rank[:, i * tokens : (i + 1) * tokens], acts_ref[...]], axis=0) for i in range(shards)]
-    for i in range(shards):
-        for j in range(copies):
-            rank_ref[i * copies + j] = both[i]
-
-
-def du_pack_kernel(index_ref, du_ref, got_ref, *pack_refs):
-    tokens = got_ref.shape[2]
+    du[...] = grad_u
+    rank[...] = dot(up_ref[:, part(own_index(0), chans)], grad_u).astype(BF16)
+    low = chips * chans
+    for i in range(chips):
+        for j, out_ref in enumerate((keep_ref, give_ref)):
+            cols = part(own_index(2 * i + j), tokens)
+            out_ref[i * chans : (i + 1) * chans] = du[:, cols]
+            out_ref[low + i * ranks : low + (i + 1) * ranks] = rank[:, cols]
+    for out_ref in (keep_ref, give_ref):
+        out_ref[low + chips * ranks :] = acts_ref[...]
+
+
+def core_sum_kernel(chips, ranks, keep_ref, got_ref, out_ref):
+    rows = chips * ranks
+    low = keep_ref.shape[0] - rows - ranks
+    total = keep_ref[low : low + rows].astype(F32) + got_ref[low : low + rows].astype(F32)
+    out_ref[:rows] = total.astype(BF16)
+    out_ref[rows : rows + ranks] = keep_ref[low + rows :]
+    out_ref[rows + ranks :] = got_ref[low + rows :]
+
+
+def pairwise(values):
+    while len(values) > 1:
+        values = [values[i] + values[i + 1] for i in range(0, len(values), 2)]
+    return values[0]
+
+
+def du_pack_kernel(groups, chans, ranks, keep_ref, got_ref, *refs):
+    total = pairwise([ref[...].astype(F32) for ref in refs[:groups]]).astype(BF16)
+    own_ref, pack_refs = refs[groups], refs[groups + 1 :]
+    rows = (1 + len(pack_refs)) * ranks
+    own_ref[:ranks] = total[:ranks]
+    own_ref[ranks:] = total[rows:]
     for i, pack_ref in enumerate(pack_refs):
-        pack_ref[0] = du_ref[:, part(own_index(index_ref, 2 * (i + 1)), tokens)]
-        pack_ref[1] = got_ref[i + 1]
-
-
-def rank_kernel(groups, scale, index_ref, parts_ref, tok_ref, du_ref, rank_ref, acts_ref, adapter_ref):
-    rank = rank_ref.shape[0]
-    shards = parts_ref.shape[0] // groups
+        block = slice((i + 1) * chans, (i + 2) * chans)
+        pack_ref[:chans] = keep_ref[block]
+        pack_ref[chans : 2 * chans] = got_ref[block]
+        pack_ref[2 * chans : 2 * chans + ranks] = total[(i + 1) * ranks : (i + 2) * ranks]
+        pack_ref[2 * chans + ranks :] = total[rows:]
+
+
+def rank_kernel(scale, chans, tok_ref, keep_ref, give_ref, own_ref, *refs):
+    pack_refs, (rank_ref, acts_ref, adapter_ref) = refs[:-3], refs[-3:]
+    ranks, tokens = rank_ref.shape
     width = tok_ref.shape[0]
-    acts, total = [], None
-    for i in range(shards):
-        both = parts_ref[i * groups].astype(F32)
-        for j in range(1, groups):
-            both = both + parts_ref[i * groups + j].astype(F32)
-        acts.append(both[rank:])
-        total = both[:rank] if total is None else total + both[:rank]
-    acts = jnp.concatenate(acts, axis=1).astype(BF16)
-    acts_ref[...] = acts
-    rank_grad = total.astype(BF16)
+    tails = [own_ref[...]] + [ref[2 * chans :] for ref in pack_refs]
+    rank_grad = pairwise([tail[:ranks].astype(F32) for tail in tails]).astype(BF16)
     rank_ref[...] = rank_grad
     adapter_ref[:, :width] = scale * dot_nt(rank_grad, tok_ref[...])
-    adapter_ref[:, width:] = scale * dot_nt(acts, du_ref[...])
+    up = None
+    for i, tail in enumerate(tails):
+        for j, ref in enumerate((keep_ref, give_ref)):
+            act = tail[(1 + j) * ranks : (2 + j) * ranks]
+            acts_ref[:, part(own_index(2 * i + j), tokens)] = act
+            term = dot_nt(act, ref[i * chans : (i + 1) * chans])
+            up = term if up is None else up + term
+    adapter_ref[:, width:] = scale * up
 
 
 def chip_sum_kernel(own_ref, other_ref, out_ref):
@@ -150,12 +170,12 @@
     out_ref[:, width + chans :] = other_ref[:, width:].astype(BF16)
 
 
-def filter_grad_kernel(index_ref, acts_ref, up_ref, spec_ref, table_ref, *refs):
+def filter_grad_kernel(acts_ref, up_ref, spec_ref, table_ref, *refs):
     pack_refs, out_ref, signal, cross = refs[:-3], refs[-3], refs[-2], refs[-1]
     length = table_ref.shape[0]
-    _, chans, tokens = pack_refs[0].shape
-    unpack(index_ref, pack_refs, signal)
-    own_up = up_ref[:, part(own_index(index_ref, 0), chans)]
+    chans = pack_refs[0].shape[1]
+    unpack(pack_refs, signal)
+    own_up = up_ref[:, part(own_index(0), chans)]
     act = (signal[...].astype(F32) + dot_tn(own_up, acts_ref[...])).astype(BF16)
     for cols in blocks(table_ref):
         half = (cols.stop - cols.start) // 2
@@ -164,34 +184,31 @@
     out_ref[...] = dot_nt(cross[...], table_ref[...])
 
 
-def input_grad_kernel(index_ref, du_ref, got_ref, down_ref, rank_ref, *refs):
+def input_grad_kernel(keep_ref, got_ref, down_ref, rank_ref, *refs):
     pack_refs, out_ref = refs[:-1], refs[-1]
-    _, chans, tokens = got_ref.shape
+    chans = (pack_refs[0].shape[0] - 3 * rank_ref.shape[0]) // 2
 
     def put(offset, value):
-        index = own_index(index_ref, offset)
+        index = own_index(offset)
         lift = dot_tn(down_ref[:, part(index, chans)], rank_ref[...])
         out_ref[part(index, chans), :] = (value.astype(F32) + lift).astype(BF16)
 
-    put(0, du_ref[:, part(own_index(index_ref, 0), tokens)])
-    put(1, got_ref[0])
+    put(0, keep_ref[:chans])
+    put(1, got_ref[:chans])
     for i, pack_ref in enumerate(pack_refs):
         for j in range(2):
-            put(2 * (i + 1) + j, pack_ref[j])
-
-
-def adapter_sum_kernel(index_ref, *refs):
+            put(2 * (i + 1) + j, pack_ref[j * chans : (j + 1) * chans])
+
+
+def adapter_sum_kernel(*refs):
     part_refs, down_out, up_out, total, chunks = refs[:-4], refs[-4], refs[-3], refs[-2], refs[-1]
     width = down_out.shape[2]
     chans = (part_refs[0].shape[1] - width) // 2
-    sums = [ref[:, :width].astype(F32) for ref in part_refs]
-    while len(sums) > 1:
-        sums = [sums[i] + sums[i + 1] for i in range(0, len(sums), 2)]
-    down_out[:, 0, :] = sums[0]
+    down_out[:, 0, :] = pairwise([ref[:, :width].astype(F32) for ref in part_refs])
     for i, ref in enumerate(part_refs):
         for j in range(2):
             block = ref[:, width + j * chans : width + (j + 1) * chans]
-            chunks[:, part(own_index(index_ref, 2 * i + j), chans)] = block.astype(F32)
+            chunks[:, part(own_index(2 * i + j), chans)] = block.astype(F32)
     up_out[:, 0, :] = chunks[...]
 
 
@@ -204,80 +221,90 @@
     chans, length = filt.shape
     chips = shards // 2
     table = jnp.asarray(dft_table(length))
-    index = lax.axis_index("ctx").reshape(1)
-    scalar = pl.BlockSpec(memory_space=pltpu.SMEM)
     local = pl.BlockSpec(memory_space=pltpu.VMEM)
     product = 2 * chans * length * 2 * length
 
-    def call(kernel, name, out_shape, args, scratch=(), flops=0, index_first=True):
-        args = ((index,) if index_first else ()) + tuple(args)
-        in_specs = [scalar if arg is index else local for arg in args]
-        moved = sum(int(np.prod(o.shape)) * o.dtype.itemsize for o in jax.tree.leaves(out_shape))
+    def call(kernel, name, out_shape, args, scratch=(), flops=0):
+        outs = jax.tree.leaves(out_shape)
+        moved = sum(int(np.prod(o.shape)) * o.dtype.itemsize for o in outs)
+        out_specs = (local,) * len(outs) if isinstance(out_shape, tuple) else local
         return pl.pallas_call(
             kernel,
             out_shape=out_shape,
-            in_specs=in_specs,
+            in_specs=[local] * len(args),
+            out_specs=out_specs,
             scratch_shapes=scratch,
             cost_estimate=pl.CostEstimate(flops=flops, bytes_accessed=moved, transcendentals=0),
             compiler_params=pltpu.CompilerParams(vmem_limit_bytes=VMEM_BYTES),
             name=name,
         )(*args)
 
-    def send(value, offset):
-        return lax.ppermute(value, "ctx", [(i, i ^ offset) for i in range(shards)])
-
+    def send(value, offset, axis="ctx"):
+        return lax.ppermute(value, axis, [(i, i ^ offset) for i in range(mesh.shape[axis])])
+
+    def packed(own, sibling, name):
+        return call(pack_kernel, name, (pack,) * chips, (own, sibling))
+
+    def to_chips(packs):
+        return [packs[0]] + [send(packs[i], 2 * i) for i in range(1, chips)]
+
+    vmem = pltpu.VMEM
     pack = shape((2, chans, tokens), BF16)
     sibling_grad = send(tok_grad, 1)
     sibling_input = send(tok_input, 1)
-    grad_packs = call(grad_pack_kernel, "grad_pack", (pack,) * chips, (tok_grad, sibling_grad))
-    grad_packs, tok_input = lax.optimization_barrier((grad_packs, tok_input))
-    chan_grad = [grad_packs[0]] + [send(grad_packs[i], 2 * i) for i in range(1, chips)]
-    acts_part, *input_packs = call(
-        input_pack_kernel,
-        "input_pack",
-        (shape((rank, tokens), BF16),) + (pack,) * chips,
-        (down, tok_input, sibling_input),
-    )
-    chan_packs = [input_packs[0]] + [send(input_packs[i], 2 * i) for i in range(1, chips)]
-    filt_spec = call(
+    grad_packs = packed(tok_grad, sibling_grad, "grad_pack")
+    grad_packs, filt, tok_input = lax.optimization_barrier((grad_packs, filt, tok_input))
+    chan_grad = to_chips(grad_packs)
+    filt_spec, acts_part = call(
         filter_spec_kernel,
         "filter_spec",
-        shape((chans, 2 * length), F32),
-        (filt, table),
+        (shape((chans, 2 * length), F32), shape((rank, tokens), BF16)),
+        (filt, tok_input, table, down),
         flops=product,
-        index_first=False,
-    )
-    grad_spec, chan_du, give, rank_parts = call(
-        functools.partial(grad_u_kernel, groups, chips),
+    )
+    input_packs = packed(tok_input, sibling_input, "input_pack")
+    half_du = shape((chips * (chans + rank) + rank, tokens), BF16)
+    grad_spec, keep, give = call(
+        grad_u_kernel,
         "grad_u",
-        (
-            shape((chans, 2 * length), F32),
-            shape((chans, length), BF16),
-            shape((chips, chans, tokens), BF16),
-            shape((shards * groups, 2 * rank, tokens), BF16),
-        ),
+        (shape((chans, 2 * length), F32), half_du, half_du),
         (filt_spec, up, acts_part, table, *chan_grad),
-        scratch=[pltpu.VMEM((chans, length), BF16), pltpu.VMEM((chans, 2 * length), BF16)],
+        scratch=[
+            vmem((chans, length), BF16),
+            vmem((chans, 2 * length), BF16),
+            vmem((chans, length), BF16),
+            vmem((rank, length), BF16),
+        ],
         flops=2 * product,
     )
-    rank_parts, chan_packs = lax.optimization_barrier((rank_parts, chan_packs))
-    rank_all = lax.all_to_all(rank_parts, ("ctx", "grp"), 0, 0, tiled=True)
     got = send(give, 1)
-    du_packs = call(du_pack_kernel, "du_pack", (pack,) * (chips - 1), (chan_du, got))
+    input_packs, got = lax.optimization_barrier((input_packs, got))
+    core_part = call(
+        functools.partial(core_sum_kernel, chips, rank),
+        "core_sum",
+        shape(((chips + 2) * rank, tokens), BF16),
+        (keep, got),
+    )
+    chan_packs = to_chips(input_packs)
+    core_parts = [core_part] + [send(core_part, i, "grp") for i in range(1, groups)]
+    own_tail, *du_packs = call(
+        functools.partial(du_pack_kernel, groups, chans, rank),
+        "du_pack",
+        (shape((3 * rank, tokens), BF16),) + (shape((2 * chans + 3 * rank, tokens), BF16),) * (chips - 1),
+        (keep, got, *core_parts),
+    )
     tok_packs = [send(du_packs[i], 2 * (i + 1)) for i in range(chips - 1)]
-
     rank_grad, acts, adapter_part = call(
-        functools.partial(rank_kernel, groups, float(length) ** -0.5),
+        functools.partial(rank_kernel, float(length) ** -0.5, chans),
         "rank_grad",
         (shape((rank, tokens), BF16), shape((rank, length), BF16), shape((rank, width + chans), F32)),
-        (rank_all, tok_input, chan_du),
+        (tok_input, keep, give, own_tail, *tok_packs),
     )
     chip_part = call(
         chip_sum_kernel,
         "chip_sum",
         shape((rank, width + 2 * chans), BF16),
         (adapter_part, send(adapter_part, 1)),
-        index_first=False,
     )
     chip_parts = [chip_part] + [send(chip_part, 2 * i) for i in range(1, chips)]
     filt_grad = call(
@@ -285,11 +312,11 @@
         "filter_grad",
         shape((chans, length), F32),
         (acts, up, grad_spec, table, *chan_packs),
-        scratch=[pltpu.VMEM((chans, length), BF16), pltpu.VMEM((chans, 2 * length), BF16)],
+        scratch=[vmem((chans, length), BF16), vmem((chans, 2 * length), BF16)],
         flops=2 * product,
     )
     grad_input = call(
-        input_grad_kernel, "input_grad", shape((width, tokens), BF16), (chan_du, got, down, rank_grad, *tok_packs)
+        input_grad_kernel, "input_grad", shape((width, tokens), BF16), (keep, got, down, rank_grad, *tok_packs)
     )
     grad_down, grad_up = call(
         adapter_sum_kernel,
@@ -443,8 +470,9 @@
 
 def body(mesh, saved_input, out_grad, filters, adapter_down, adapter_up):
     length = filters.shape[2]
-    shards = mesh.shape["ctx"]
-    if 2 * length * length <= TABLE_ENTRIES and shards > 1 and shards & (shards - 1) == 0:
+    shards, groups = mesh.shape["ctx"], mesh.shape["grp"]
+    paired = shards > 1 and shards & (shards - 1) == 0 and groups & (groups - 1) == 0
+    if 2 * length * length <= TABLE_ENTRIES and paired:
         return dense_body(mesh, saved_input, out_grad, filters, adapter_down, adapter_up)
     return staged_body(saved_input, out_grad, filters, adapter_down, adapter_up)
 

time: 58.3 us -> 56.8 us (0.974)
  local copies, waits for them, and re-layouts: 10.7 us -> 7.2 us
  Pallas kernels: 12 us -> 10.2 us
  waiting for transfers between devices: 13.5 us -> 15.3 us
  starting transfers between devices: 21 us -> 22.5 us
    ppermute x16 -> x19, waiting for transfers between devices: 3.59 us -> 15.3 us  [send(): lax.ppermute(value, axis, [(i, i ^ offset) for i in range(mesh.shape[axis...]
    all_to_all x1 -> x0, waiting for transfers between devices: 9.88 us -> none  [dense_body(): rank_all = lax.all_to_all(rank_parts, ('ctx', 'grp'), 0, 0, tiled=True)]
    ppermute x16 -> x19, starting transfers between devices: 16.1 us -> 22.5 us  [send(): lax.ppermute(value, axis, [(i, i ^ offset) for i in range(mesh.shape[axis...]
    all_to_all x1 -> x0, starting transfers between devices: 4.84 us -> none  [dense_body(): rank_all = lax.all_to_all(rank_parts, ('ctx', 'grp'), 0, 0, tiled=True)]
    unnamed x36 -> x18, local copies, waits for them, and re-layouts: 10.7 us -> 7.2 us
    pallas_call x10 -> x11, Pallas kernels: 12 us -> 10.2 us  [call(): pl.pallas_call(kernel, out_shape=out_shape, in_specs=[local] * len(args),...]
  transfers between devices with their start and end apart: 17 -> 19, of which waited for: 4 -> 9; matrix products, arithmetic and copies ran while one was open for 0% -> 0% of each run, Pallas kernels for 19% -> 16%
where the time goes in v2:
time: 56.8 us; the launch traced here: 55.9 us
  starting transfers between devices  22.5 us (40%)
  waiting for transfers between devices  15.3 us (27%)
  Pallas kernels  10.2 us (18%)
  local copies, waits for them, and re-layouts  7.2 us (13%)
  between operations  0.71 us (1%)
    ppermute x19, starting transfers between devices, send(): lax.ppermute(value, axis, [(i, i ^ offset) for i in range(mesh.shape[axis...  22.5 us
    ppermute x19, waiting for transfers between devices, send(): lax.ppermute(value, axis, [(i, i ^ offset) for i in range(mesh.shape[axis...  15.3 us
    pallas_call x11, Pallas kernels, call(): pl.pallas_call(kernel, out_shape=out_shape, in_specs=[local] * len(args),...  10.2 us
    unnamed x18, local copies, waits for them, and re-layouts  7.2 us
  transfers between devices with their start and end apart: 19, of which 9 were waited for; matrix products, arithmetic and copies ran while one was open for 0% of the time, Pallas kernels for 16%

profile of v2, /device:TPU:0, one launch (start us, length us, event | category | flops | bytes accessed | tf_op | source)
XLA Modules:
  0.0 55.9 jit_solution(5041311320364248580)
XLA Ops:
  0.6 0.5 collective-permute-start
  1.1 1.7 %collective-permute-done.sibling_ref = bf16[2048,128]{1,0:T(8,128)(2,1)S(1)} collective-permute-done((bf16[2048,128]{1,0:T(8,128)(2,1)}, bf16[2048,128]{1,0:T(8,128)(2,1)S(1)}, u32[]{:S(2)}, u32[]{:S(2)}) %collective-permute-start) | collective-permute-done | bytes 524320 | tf_op jit(solution)/shard_map/ppermute | solution.py:243
  2.9 1.0 %copy-done.5 = bf16[1,2048,128]{2,1,0:T(8,128)(2,1)S(1)} copy-done((bf16[1,2048,128]{2,1,0:T(8,128)(2,1)S(1)}, bf16[1,2048,128]{2,1,0:T(8,128)(2,1)}, u32[]{:S(2)}) %copy-start.5) | copy-done | bytes 524312
  4.0 2.9 %collective-permute-start.1 = (bf16[2,256,128]{2,1,0:T(8,128)(2,1)S(1)}, bf16[2,256,128]{2,1,0:T(8,128)(2,1)S(1)}, u32[]{:S(2)}, u32[]{:S(2)}) collective-permute-start(bf16[2,256,128]{2,1,0:T(8,128)(2,1)S(1)} %get-tuple-element.46), channel_id=1, source_target_pairs={{0,8},{4,12},{8,0},{12,4},{16,24},{20,28},{24,16},{28,20},{1,9},{5... | collective-permute-start | bytes 393224 | tf_op jit(solution)/shard_map/ppermute | solution.py:243
  6.9 1.5 %collective-permute-start.2 = (bf16[2,256,128]{2,1,0:T(8,128)(2,1)S(1)}, bf16[2,256,128]{2,1,0:T(8,128)(2,1)S(1)}, u32[]{:S(2)}, u32[]{:S(2)}) collective-permute-start(bf16[2,256,128]{2,1,0:T(8,128)(2,1)S(1)} %get-tuple-element.47), channel_id=1, source_target_pairs={{0,16},{4,20},{8,24},{12,28},{16,0},{20,4},{24,8},{28,12},{1,17},{... | collective-permute-start | bytes 393224 | tf_op jit(solution)/shard_map/ppermute | solution.py:243
  8.4 0.0 collective-permute-start.3
  8.4 0.0 collective-permute-start.4
  8.4 2.2 %copy-done = bf16[1024,2048]{1,0:T(8,128)(2,1)S(1)} copy-done((bf16[1024,2048]{1,0:T(8,128)(2,1)S(1)}, bf16[1024,2048]{1,0:T(8,128)(2,1)}, u32[]{:S(2)}) %copy-start) | copy-done | bytes 4194328
  10.6 1.0 %copy-done.2 = bf16[1,2048,128]{2,1,0:T(8,128)(2,1)S(1)} copy-done((bf16[1,2048,128]{2,1,0:T(8,128)(2,1)S(1)}, bf16[1,2048,128]{2,1,0:T(8,128)(2,1)}, u32[]{:S(2)}) %copy-start.2) | copy-done | bytes 524312
  11.7 1.2 %copy-done.4 = f32[1,256,1024]{2,1,0:T(8,128)S(1)} copy-done((f32[1,256,1024]{2,1,0:T(8,128)S(1)}, f32[1,256,1024]{2,1,0:T(8,128)}, u32[]{:S(2)}) %copy-start.4) | copy-done | bytes 1048600
  12.9 0.8 %copy-done.6 = bf16[16,1,2048]{2,0,1:T(8,128)(2,1)S(1)} copy-done((bf16[16,1,2048]{2,0,1:T(8,128)(2,1)S(1)}, bf16[16,1,2048]{2,0,1:T(8,128)(2,1)}, u32[]{:S(2)}) %copy-start.6) | copy-done | bytes 65560
  13.7 1.3 %filter_spec.1 = (f32[256,2048]{1,0:T(8,128)S(1)}, bf16[16,128]{1,0:T(8,128)(2,1)S(1)}) custom-call(f32[256,1024]{1,0:T(8,128)S(1)} %bitcast.11, bf16[2048,128]{1,0:T(8,128)(2,1)S(1)} %bitcast.8, bf16[1024,2048]{1,0:T(8,128)(2,1)S(1)} %copy-done, bf16[16,2048]{1,0:T(8,128)(2,1)S(1)} %bitcast.14), custom_call_target="tpu_custom_call" | custom-call | flops 1073741824 | bytes 2101248 | tf_op jit(solution)/shard_map/filter_spec/pallas_call | solution.py:231
  15.0 0.0 collective-permute-done.1.refs_1_
  15.1 0.0 collective-permute-done.2.refs_2_
  15.1 0.0 collective-permute-done.3.refs_3_
  15.1 0.9 %copy-done.1 = bf16[1024,2048]{1,0:T(8,128)(2,1)S(1)} copy-done((bf16[1024,2048]{1,0:T(8,128)(2,1)S(1)}, bf16[1024,2048]{1,0:T(8,128)(2,1)}, u32[]{:S(2)}) %copy-start.1) | copy-done | bytes 4194328
  15.9 2.8 %grad_u.1 = (f32[256,2048]{1,0:T(8,128)S(1)}, bf16[1104,128]{1,0:T(8,128)(2,1)S(1)}, bf16[1104,128]{1,0:T(8,128)(2,1)S(1)}) custom-call(f32[256,2048]{1,0:T(8,128)S(1)} %get-tuple-element.43.filt_spec_ref, bf16[16,2048]{1,0:T(8,128)(2,1)S(1)} %bitcast.16, bf16[16,128]{1,0:T(8,128)(2,1)S(1)} %get-tuple-element.44.acts_ref, bf16[1024,2048]{1,0:T(8,128)(2,1)S(1)} %copy-done.1, ...), custom_call_target="tpu_custom_call" | custom-call | flops 2147483648 | bytes 2662400 | tf_op jit(solution)/shard_map/grad_u/pallas_call | solution.py:231
  18.7 0.6 %collective-permute-start.5 = (bf16[1104,128]{1,0:T(8,128)(2,1)S(1)}, bf16[1104,128]{1,0:T(8,128)(2,1)S(1)}, u32[]{:S(2)}, u32[]{:S(2)}) collective-permute-start(bf16[1104,128]{1,0:T(8,128)(2,1)S(1)} %get-tuple-element.54.give_ref), channel_id=1, source_target_pairs={{0,4},{4,0},{8,12},{12,8},{16,20},{20,16},{24,28},{28,24},{1,5},{5... | collective-permute-start | bytes 847880 | tf_op jit(solution)/shard_map/ppermute | solution.py:243
  19.3 0.0 collective-permute-done.4.sibling_ref
  19.4 1.1 %collective-permute-done.5.got_ref = bf16[1104,128]{1,0:T(8,128)(2,1)S(1)} collective-permute-done((bf16[1104,128]{1,0:T(8,128)(2,1)S(1)}, bf16[1104,128]{1,0:T(8,128)(2,1)S(1)}, u32[]{:S(2)}, u32[]{:S(2)}) %collective-permute-start.5) | collective-permute-done | bytes 282656 | tf_op jit(solution)/shard_map/ppermute | solution.py:243
  20.5 2.0 %collective-permute-start.6 = (bf16[96,128]{1,0:T(8,128)(2,1)S(1)}, bf16[96,128]{1,0:T(8,128)(2,1)S(1)}, u32[]{:S(2)}, u32[]{:S(2)}) collective-permute-start(bf16[96,128]{1,0:T(8,128)(2,1)S(1)} %core_sum.1.refs_0_), channel_id=1, source_target_pairs={{0,1},{1,0},{2,3},{3,2},{4,5},{5,4},{6,7},{7,6},{8,9},{9,8},{10,11... | collective-permute-start | bytes 73736 | tf_op jit(solution)/shard_map/ppermute | solution.py:243
  22.6 2.6 %collective-permute-start.7 = (bf16[96,128]{1,0:T(8,128)(2,1)S(1)}, bf16[96,128]{1,0:T(8,128)(2,1)S(1)}, u32[]{:S(2)}, u32[]{:S(2)}) collective-permute-start(bf16[96,128]{1,0:T(8,128)(2,1)S(1)} %core_sum.1.refs_0_), channel_id=1, source_target_pairs={{0,2},{1,3},{2,0},{3,1},{4,6},{5,7},{6,4},{7,5},{8,10},{9,11},{10,... | collective-permute-start | bytes 73736 | tf_op jit(solution)/shard_map/ppermute | solution.py:243
  25.2 0.0 collective-permute-start.8
  25.2 0.0 collective-permute-done.6.refs_1_
  25.2 2.2 %collective-permute-done.7.refs_2_ = bf16[96,128]{1,0:T(8,128)(2,1)S(1)} collective-permute-done((bf16[96,128]{1,0:T(8,128)(2,1)S(1)}, bf16[96,128]{1,0:T(8,128)(2,1)S(1)}, u32[]{:S(2)}, u32[]{:S(2)}) %collective-permute-start.7) | collective-permute-done | bytes 24608 | tf_op jit(solution)/shard_map/ppermute | solution.py:243
  27.4 3.4 %collective-permute-done.8.refs_3_ = bf16[96,128]{1,0:T(8,128)(2,1)S(1)} collective-permute-done((bf16[96,128]{1,0:T(8,128)(2,1)S(1)}, bf16[96,128]{1,0:T(8,128)(2,1)S(1)}, u32[]{:S(2)}, u32[]{:S(2)}) %collective-permute-start.8) | collective-permute-done | bytes 24608 | tf_op jit(solution)/shard_map/ppermute | solution.py:243
  30.8 1.6 %collective-permute-start.10 = (bf16[560,128]{1,0:T(8,128)(2,1)S(1)}, bf16[560,128]{1,0:T(8,128)(2,1)S(1)}, u32[]{:S(2)}, u32[]{:S(2)}) collective-permute-start(bf16[560,128]{1,0:T(8,128)(2,1)S(1)} %get-tuple-element.58), channel_id=1, source_target_pairs={{0,16},{4,20},{8,24},{12,28},{16,0},{20,4},{24,8},{28,12},{1,17},{... | collective-permute-start | bytes 430088 | tf_op jit(solution)/shard_map/ppermute | solution.py:243
  32.4 1.4 %collective-permute-start.11 = (bf16[560,128]{1,0:T(8,128)(2,1)S(1)}, bf16[560,128]{1,0:T(8,128)(2,1)S(1)}, u32[]{:S(2)}, u32[]{:S(2)}) collective-permute-start(bf16[560,128]{1,0:T(8,128)(2,1)S(1)} %get-tuple-element.59), channel_id=1, source_target_pairs={{0,24},{4,28},{8,16},{12,20},{16,8},{20,12},{24,0},{28,4},{1,25},{... | collective-permute-start | bytes 430088 | tf_op jit(solution)/shard_map/ppermute | solution.py:243
  33.8 0.5 collective-permute-start.9
  34.4 3.4 %collective-permute-done.10.refs_1_ = bf16[560,128]{1,0:T(8,128)(2,1)S(1)} collective-permute-done((bf16[560,128]{1,0:T(8,128)(2,1)S(1)}, bf16[560,128]{1,0:T(8,128)(2,1)S(1)}, u32[]{:S(2)}, u32[]{:S(2)}) %collective-permute-start.10) | collective-permute-done | bytes 143392 | tf_op jit(solution)/shard_map/ppermute | solution.py:243
  37.7 1.1 %collective-permute-done.11.refs_2_ = bf16[560,128]{1,0:T(8,128)(2,1)S(1)} collective-permute-done((bf16[560,128]{1,0:T(8,128)(2,1)S(1)}, bf16[560,128]{1,0:T(8,128)(2,1)S(1)}, u32[]{:S(2)}, u32[]{:S(2)}) %collective-permute-start.11) | collective-permute-done | bytes 143392 | tf_op jit(solution)/shard_map/ppermute | solution.py:243
  38.9 0.7 %collective-permute-done.9.refs_0_ = bf16[560,128]{1,0:T(8,128)(2,1)S(1)} collective-permute-done((bf16[560,128]{1,0:T(8,128)(2,1)S(1)}, bf16[560,128]{1,0:T(8,128)(2,1)S(1)}, u32[]{:S(2)}, u32[]{:S(2)}) %collective-permute-start.9) | collective-permute-done | bytes 143392 | tf_op jit(solution)/shard_map/ppermute | solution.py:243
  39.5 0.4 rank_grad.1
  39.9 0.0 collective-permute-start.15
  40.0 1.6 %collective-permute-start.12 = (bf16[2,256,128]{2,1,0:T(8,128)(2,1)S(1)}, bf16[2,256,128]{2,1,0:T(8,128)(2,1)S(1)}, u32[]{:S(2)}, u32[]{:S(2)}) collective-permute-start(bf16[2,256,128]{2,1,0:T(8,128)(2,1)S(1)} %get-tuple-element.64), channel_id=1, source_target_pairs={{0,8},{4,12},{8,0},{12,4},{16,24},{20,28},{24,16},{28,20},{1,9},{5... | collective-permute-start | bytes 393224 | tf_op jit(solution)/shard_map/ppermute | solution.py:243
  41.5 1.4 %collective-permute-start.13 = (bf16[2,256,128]{2,1,0:T(8,128)(2,1)S(1)}, bf16[2,256,128]{2,1,0:T(8,128)(2,1)S(1)}, u32[]{:S(2)}, u32[]{:S(2)}) collective-permute-start(bf16[2,256,128]{2,1,0:T(8,128)(2,1)S(1)} %get-tuple-element.65), channel_id=1, source_target_pairs={{0,16},{4,20},{8,24},{12,28},{16,0},{20,4},{24,8},{28,12},{1,17},{... | collective-permute-start | bytes 393224 | tf_op jit(solution)/shard_map/ppermute | solution.py:243
  43.0 0.6 %collective-permute-start.14 = (bf16[2,256,128]{2,1,0:T(8,128)(2,1)S(1)}, bf16[2,256,128]{2,1,0:T(8,128)(2,1)S(1)}, u32[]{:S(2)}, u32[]{:S(2)}) collective-permute-start(bf16[2,256,128]{2,1,0:T(8,128)(2,1)S(1)} %get-tuple-element.66), channel_id=1, source_target_pairs={{0,24},{4,28},{8,16},{12,20},{16,8},{20,12},{24,0},{28,4},{1,25},{... | collective-permute-start | bytes 393224 | tf_op jit(solution)/shard_map/ppermute | solution.py:243
  43.6 1.6 %collective-permute-start.16 = (bf16[16,2560]{1,0:T(8,128)(2,1)S(1)}, bf16[16,2560]{1,0:T(8,128)(2,1)S(1)}, u32[]{:S(2)}, u32[]{:S(2)}) collective-permute-start(bf16[16,2560]{1,0:T(8,128)(2,1)S(1)} %chip_sum.1.refs_0_), channel_id=1, source_target_pairs={{0,8},{4,12},{8,0},{12,4},{16,24},{20,28},{24,16},{28,20},{1,9},{5... | collective-permute-start | bytes 245768 | tf_op jit(solution)/shard_map/ppermute | solution.py:243
  45.1 1.4 %collective-permute-start.17 = (bf16[16,2560]{1,0:T(8,128)(2,1)S(1)}, bf16[16,2560]{1,0:T(8,128)(2,1)S(1)}, u32[]{:S(2)}, u32[]{:S(2)}) collective-permute-start(bf16[16,2560]{1,0:T(8,128)(2,1)S(1)} %chip_sum.1.refs_0_), channel_id=1, source_target_pairs={{0,16},{4,20},{8,24},{12,28},{16,0},{20,4},{24,8},{28,12},{1,17},{... | collective-permute-start | bytes 245768 | tf_op jit(solution)/shard_map/ppermute | solution.py:243
  46.5 0.0 collective-permute-done.12.refs_1_
  46.5 2.1 %collective-permute-start.18 = (bf16[16,2560]{1,0:T(8,128)(2,1)S(1)}, bf16[16,2560]{1,0:T(8,128)(2,1)S(1)}, u32[]{:S(2)}, u32[]{:S(2)}) collective-permute-start(bf16[16,2560]{1,0:T(8,128)(2,1)S(1)} %chip_sum.1.refs_0_), channel_id=1, source_target_pairs={{0,24},{4,28},{8,16},{12,20},{16,8},{20,12},{24,0},{28,4},{1,25},{... | collective-permute-start | bytes 245768 | tf_op jit(solution)/shard_map/ppermute | solution.py:243
  48.7 1.5 %collective-permute-done.13.refs_2_ = bf16[2,256,128]{2,1,0:T(8,128)(2,1)S(1)} collective-permute-done((bf16[2,256,128]{2,1,0:T(8,128)(2,1)S(1)}, bf16[2,256,128]{2,1,0:T(8,128)(2,1)S(1)}, u32[]{:S(2)}, u32[]{:S(2)}) %collective-permute-start.13) | collective-permute-done | bytes 131104 | tf_op jit(solution)/shard_map/ppermute | solution.py:243
  50.1 0.1 collective-permute-done.14.refs_3_
  50.3 3.7 %filter_grad.1 = f32[256,1024]{1,0:T(8,128)} custom-call(bf16[16,1024]{1,0:T(8,128)(2,1)S(1)} %get-tuple-element.61.acts_ref, bf16[16,2048]{1,0:T(8,128)(2,1)S(1)} %bitcast.17, f32[256,2048]{1,0:T(8,128)S(1)} %get-tuple-element.62.spec_ref, bf16[1024,2048]{1,0:T(8,128)(2,1)S(1)} %copy-done.1, bf16[2,256,128]{2,1,0:T(8,128)(2,1)S(1)} %get-tuple-element.63.refs_0_, ...), custom_call_target="tpu_custom_call" | custom-call | flops 2147483648 | bytes 1048576 | tf_op jit(solution)/shard_map/filter_grad/pallas_call | solution.py:231
  53.9 1.1 %input_grad.1 = bf16[2048,128]{1,0:T(8,128)(2,1)} custom-call(bf16[1104,128]{1,0:T(8,128)(2,1)S(1)} %get-tuple-element.49.keep_ref, bf16[1104,128]{1,0:T(8,128)(2,1)S(1)} %collective-permute-done.5.got_ref, bf16[16,2048]{1,0:T(8,128)(2,1)S(1)} %bitcast.15, bf16[16,128]{1,0:T(8,128)(2,1)S(1)} %get-tuple-element.60.rank_ref, ...), custom_call_target="tpu_custom_call" | custom-call | bytes 524288 | tf_op jit(solution)/shard_map/input_grad/pallas_call | solution.py:231
  55.1 0.0 collective-permute-done.16.refs_1_
  55.1 0.0 collective-permute-done.17.refs_2_
  55.1 0.8 %adapter_sum.1 = (f32[16,1,2048]{2,1,0:T(1,128)}, f32[16,1,2048]{2,1,0:T(1,128)}) custom-call(bf16[16,2560]{1,0:T(8,128)(2,1)S(1)} %chip_sum.1.refs_0_, bf16[16,2560]{1,0:T(8,128)(2,1)S(1)} %collective-permute-done.16.refs_1_, bf16[16,2560]{1,0:T(8,128)(2,1)S(1)} %collective-permute-done.17.refs_2_, bf16[16,2560]{1,0:T(8,128)(2,1)S(1)} %collective-permute-done.18.refs_3_), custom_call_target="tpu_custom_call" | custom-call | bytes 262144 | tf_op jit(solution)/shard_map/adapter_sum/pallas_call | solution.py:231
  (19 shorter events, 0.2 us)
Async XLA Ops:
  0.6 2.3 %collective-permute-start = (bf16[2048,128]{1,0:T(8,128)(2,1)}, bf16[2048,128]{1,0:T(8,128)(2,1)S(1)}, u32[]{:S(2)}, u32[]{:S(2)}) collective-permute-start(bf16[2048,128]{1,0:T(8,128)(2,1)} %bitcast.12), channel_id=1, source_target_pairs={{0,4},{4,0},{8,12},{12,8},{16,20},{20,16},{24,28},{28,24},{1,5},{5... | collective-permute-start | bytes 1572872 | tf_op jit(solution)/shard_map/ppermute | solution.py:243
  2.9 1.0 %copy-start.5 = (bf16[1,2048,128]{2,1,0:T(8,128)(2,1)S(1)}, bf16[1,2048,128]{2,1,0:T(8,128)(2,1)}, u32[]{:S(2)}) copy-start(bf16[1,2048,128]{2,1,0:T(8,128)(2,1)} %param.7) | copy-start | bytes 1572868
  4.0 11.1 %collective-permute-start.1 = (bf16[2,256,128]{2,1,0:T(8,128)(2,1)S(1)}, bf16[2,256,128]{2,1,0:T(8,128)(2,1)S(1)}, u32[]{:S(2)}, u32[]{:S(2)}) collective-permute-start(bf16[2,256,128]{2,1,0:T(8,128)(2,1)S(1)} %get-tuple-element.46), channel_id=1, source_target_pairs={{0,8},{4,12},{8,0},{12,4},{16,24},{20,28},{24,16},{28,20},{1,9},{5... | collective-permute-start | bytes 393224 | tf_op jit(solution)/shard_map/ppermute | solution.py:243
  6.9 8.2 %collective-permute-start.2 = (bf16[2,256,128]{2,1,0:T(8,128)(2,1)S(1)}, bf16[2,256,128]{2,1,0:T(8,128)(2,1)S(1)}, u32[]{:S(2)}, u32[]{:S(2)}) collective-permute-start(bf16[2,256,128]{2,1,0:T(8,128)(2,1)S(1)} %get-tuple-element.47), channel_id=1, source_target_pairs={{0,16},{4,20},{8,24},{12,28},{16,0},{20,4},{24,8},{28,12},{1,17},{... | collective-permute-start | bytes 393224 | tf_op jit(solution)/shard_map/ppermute | solution.py:243
  8.4 6.6 %collective-permute-start.3 = (bf16[2,256,128]{2,1,0:T(8,128)(2,1)S(1)}, bf16[2,256,128]{2,1,0:T(8,128)(2,1)S(1)}, u32[]{:S(2)}, u32[]{:S(2)}) collective-permute-start(bf16[2,256,128]{2,1,0:T(8,128)(2,1)S(1)} %get-tuple-element.48), channel_id=1, source_target_pairs={{0,24},{4,28},{8,16},{12,20},{16,8},{20,12},{24,0},{28,4},{1,25},{... | collective-permute-start | bytes 393224 | tf_op jit(solution)/shard_map/ppermute | solution.py:243
  8.4 10.9 %collective-permute-start.4 = (bf16[2048,128]{1,0:T(8,128)(2,1)}, bf16[2048,128]{1,0:T(8,128)(2,1)S(1)}, u32[]{:S(2)}, u32[]{:S(2)}) collective-permute-start(bf16[2048,128]{1,0:T(8,128)(2,1)} %bitcast.7), channel_id=1, source_target_pairs={{0,4},{4,0},{8,12},{12,8},{16,20},{20,16},{24,28},{28,24},{1,5},{5... | collective-permute-start | bytes 1572872 | tf_op jit(solution)/shard_map/ppermute | solution.py:243
  8.4 2.2 %copy-start = (bf16[1024,2048]{1,0:T(8,128)(2,1)S(1)}, bf16[1024,2048]{1,0:T(8,128)(2,1)}, u32[]{:S(2)}) copy-start(bf16[1024,2048]{1,0:T(8,128)(2,1)} %constant.2.clone.table_ref) | copy-start | bytes 12582916
  10.6 1.0 %copy-start.2 = (bf16[1,2048,128]{2,1,0:T(8,128)(2,1)S(1)}, bf16[1,2048,128]{2,1,0:T(8,128)(2,1)}, u32[]{:S(2)}) copy-start(bf16[1,2048,128]{2,1,0:T(8,128)(2,1)} %param.6) | copy-start | bytes 1572868
  11.7 1.2 %copy-start.4 = (f32[1,256,1024]{2,1,0:T(8,128)S(1)}, f32[1,256,1024]{2,1,0:T(8,128)}, u32[]{:S(2)}) copy-start(f32[1,256,1024]{2,1,0:T(8,128)} %param.8) | copy-start | bytes 3145732
  12.9 0.8 %copy-start.6 = (bf16[16,1,2048]{2,0,1:T(8,128)(2,1)S(1)}, bf16[16,1,2048]{2,0,1:T(8,128)(2,1)}, u32[]{:S(2)}) copy-start(bf16[16,1,2048]{2,0,1:T(8,128)(2,1)} %param.9) | copy-start | bytes 196612
  13.7 2.2 %copy-start.1 = (bf16[1024,2048]{1,0:T(8,128)(2,1)S(1)}, bf16[1024,2048]{1,0:T(8,128)(2,1)}, u32[]{:S(2)}) copy-start(bf16[1024,2048]{1,0:T(8,128)(2,1)} %constant.2.clone.table_ref) | copy-start | bytes 12582916
  13.7 2.2 %copy-start.8 = (bf16[16,1,2048]{2,0,1:T(8,128)(2,1)S(1)}, bf16[16,1,2048]{2,0,1:T(8,128)(2,1)}, u32[]{:S(2)}) copy-start(bf16[16,1,2048]{2,0,1:T(8,128)(2,1)} %param.10) | copy-start | bytes 196612
  15.9 3.4 %copy-start.3 = (bf16[1,2048,128]{2,1,0:T(8,128)(2,1)S(1)}, bf16[1,2048,128]{2,1,0:T(8,128)(2,1)}, u32[]{:S(2)}) copy-start(bf16[1,2048,128]{2,1,0:T(8,128)(2,1)} %param.6) | copy-start | bytes 1572868
  18.7 1.8 %collective-permute-start.5 = (bf16[1104,128]{1,0:T(8,128)(2,1)S(1)}, bf16[1104,128]{1,0:T(8,128)(2,1)S(1)}, u32[]{:S(2)}, u32[]{:S(2)}) collective-permute-start(bf16[1104,128]{1,0:T(8,128)(2,1)S(1)} %get-tuple-element.54.give_ref), channel_id=1, source_target_pairs={{0,4},{4,0},{8,12},{12,8},{16,20},{20,16},{24,28},{28,24},{1,5},{5... | collective-permute-start | bytes 847880 | tf_op jit(solution)/shard_map/ppermute | solution.py:243
  20.5 4.6 %collective-permute-start.6 = (bf16[96,128]{1,0:T(8,128)(2,1)S(1)}, bf16[96,128]{1,0:T(8,128)(2,1)S(1)}, u32[]{:S(2)}, u32[]{:S(2)}) collective-permute-start(bf16[96,128]{1,0:T(8,128)(2,1)S(1)} %core_sum.1.refs_0_), channel_id=1, source_target_pairs={{0,1},{1,0},{2,3},{3,2},{4,5},{5,4},{6,7},{7,6},{8,9},{9,8},{10,11... | collective-permute-start | bytes 73736 | tf_op jit(solution)/shard_map/ppermute | solution.py:243
  22.6 4.8 %collective-permute-start.7 = (bf16[96,128]{1,0:T(8,128)(2,1)S(1)}, bf16[96,128]{1,0:T(8,128)(2,1)S(1)}, u32[]{:S(2)}, u32[]{:S(2)}) collective-permute-start(bf16[96,128]{1,0:T(8,128)(2,1)S(1)} %core_sum.1.refs_0_), channel_id=1, source_target_pairs={{0,2},{1,3},{2,0},{3,1},{4,6},{5,7},{6,4},{7,5},{8,10},{9,11},{10,... | collective-permute-start | bytes 73736 | tf_op jit(solution)/shard_map/ppermute | solution.py:243
  25.2 5.6 %collective-permute-start.8 = (bf16[96,128]{1,0:T(8,128)(2,1)S(1)}, bf16[96,128]{1,0:T(8,128)(2,1)S(1)}, u32[]{:S(2)}, u32[]{:S(2)}) collective-permute-start(bf16[96,128]{1,0:T(8,128)(2,1)S(1)} %core_sum.1.refs_0_), channel_id=1, source_target_pairs={{0,3},{1,2},{2,1},{3,0},{4,7},{5,6},{6,5},{7,4},{8,11},{9,10},{10,... | collective-permute-start | bytes 73736 | tf_op jit(solution)/shard_map/ppermute | solution.py:243
  30.8 6.9 %collective-permute-start.10 = (bf16[560,128]{1,0:T(8,128)(2,1)S(1)}, bf16[560,128]{1,0:T(8,128)(2,1)S(1)}, u32[]{:S(2)}, u32[]{:S(2)}) collective-permute-start(bf16[560,128]{1,0:T(8,128)(2,1)S(1)} %get-tuple-element.58), channel_id=1, source_target_pairs={{0,16},{4,20},{8,24},{12,28},{16,0},{20,4},{24,8},{28,12},{1,17},{... | collective-permute-start | bytes 430088 | tf_op jit(solution)/shard_map/ppermute | solution.py:243
  32.4 6.5 %collective-permute-start.11 = (bf16[560,128]{1,0:T(8,128)(2,1)S(1)}, bf16[560,128]{1,0:T(8,128)(2,1)S(1)}, u32[]{:S(2)}, u32[]{:S(2)}) collective-permute-start(bf16[560,128]{1,0:T(8,128)(2,1)S(1)} %get-tuple-element.59), channel_id=1, source_target_pairs={{0,24},{4,28},{8,16},{12,20},{16,8},{20,12},{24,0},{28,4},{1,25},{... | collective-permute-start | bytes 430088 | tf_op jit(solution)/shard_map/ppermute | solution.py:243
  33.8 5.7 %collective-permute-start.9 = (bf16[560,128]{1,0:T(8,128)(2,1)S(1)}, bf16[560,128]{1,0:T(8,128)(2,1)S(1)}, u32[]{:S(2)}, u32[]{:S(2)}) collective-permute-start(bf16[560,128]{1,0:T(8,128)(2,1)S(1)} %get-tuple-element.57), channel_id=1, source_target_pairs={{0,8},{4,12},{8,0},{12,4},{16,24},{20,28},{24,16},{28,20},{1,9},{5... | collective-permute-start | bytes 430088 | tf_op jit(solution)/shard_map/ppermute | solution.py:243
  39.9 3.6 %collective-permute-start.15 = (f32[16,2304]{1,0:T(8,128)S(1)}, f32[16,2304]{1,0:T(8,128)S(1)}, u32[]{:S(2)}, u32[]{:S(2)}) collective-permute-start(f32[16,2304]{1,0:T(8,128)S(1)} %get-tuple-element.67.own_ref), channel_id=1, source_target_pairs={{0,4},{4,0},{8,12},{12,8},{16,20},{20,16},{24,28},{28,24},{1,5},{5... | collective-permute-start | bytes 442376 | tf_op jit(solution)/shard_map/ppermute | solution.py:243
  40.0 6.6 %collective-permute-start.12 = (bf16[2,256,128]{2,1,0:T(8,128)(2,1)S(1)}, bf16[2,256,128]{2,1,0:T(8,128)(2,1)S(1)}, u32[]{:S(2)}, u32[]{:S(2)}) collective-permute-start(bf16[2,256,128]{2,1,0:T(8,128)(2,1)S(1)} %get-tuple-element.64), channel_id=1, source_target_pairs={{0,8},{4,12},{8,0},{12,4},{16,24},{20,28},{24,16},{28,20},{1,9},{5... | collective-permute-start | bytes 393224 | tf_op jit(solution)/shard_map/ppermute | solution.py:243
  41.5 8.6 %collective-permute-start.13 = (bf16[2,256,128]{2,1,0:T(8,128)(2,1)S(1)}, bf16[2,256,128]{2,1,0:T(8,128)(2,1)S(1)}, u32[]{:S(2)}, u32[]{:S(2)}) collective-permute-start(bf16[2,256,128]{2,1,0:T(8,128)(2,1)S(1)} %get-tuple-element.65), channel_id=1, source_target_pairs={{0,16},{4,20},{8,24},{12,28},{16,0},{20,4},{24,8},{28,12},{1,17},{... | collective-permute-start | bytes 393224 | tf_op jit(solution)/shard_map/ppermute | solution.py:243
  43.0 7.3 %collective-permute-start.14 = (bf16[2,256,128]{2,1,0:T(8,128)(2,1)S(1)}, bf16[2,256,128]{2,1,0:T(8,128)(2,1)S(1)}, u32[]{:S(2)}, u32[]{:S(2)}) collective-permute-start(bf16[2,256,128]{2,1,0:T(8,128)(2,1)S(1)} %get-tuple-element.66), channel_id=1, source_target_pairs={{0,24},{4,28},{8,16},{12,20},{16,8},{20,12},{24,0},{28,4},{1,25},{... | collective-permute-start | bytes 393224 | tf_op jit(solution)/shard_map/ppermute | solution.py:243
  43.6 11.5 %collective-permute-start.16 = (bf16[16,2560]{1,0:T(8,128)(2,1)S(1)}, bf16[16,2560]{1,0:T(8,128)(2,1)S(1)}, u32[]{:S(2)}, u32[]{:S(2)}) collective-permute-start(bf16[16,2560]{1,0:T(8,128)(2,1)S(1)} %chip_sum.1.refs_0_), channel_id=1, source_target_pairs={{0,8},{4,12},{8,0},{12,4},{16,24},{20,28},{24,16},{28,20},{1,9},{5... | collective-permute-start | bytes 245768 | tf_op jit(solution)/shard_map/ppermute | solution.py:243
  45.1 10.0 %collective-permute-start.17 = (bf16[16,2560]{1,0:T(8,128)(2,1)S(1)}, bf16[16,2560]{1,0:T(8,128)(2,1)S(1)}, u32[]{:S(2)}, u32[]{:S(2)}) collective-permute-start(bf16[16,2560]{1,0:T(8,128)(2,1)S(1)} %chip_sum.1.refs_0_), channel_id=1, source_target_pairs={{0,16},{4,20},{8,24},{12,28},{16,0},{20,4},{24,8},{28,12},{1,17},{... | collective-permute-start | bytes 245768 | tf_op jit(solution)/shard_map/ppermute | solution.py:243
  46.5 8.6 %collective-permute-start.18 = (bf16[16,2560]{1,0:T(8,128)(2,1)S(1)}, bf16[16,2560]{1,0:T(8,128)(2,1)S(1)}, u32[]{:S(2)}, u32[]{:S(2)}) collective-permute-start(bf16[16,2560]{1,0:T(8,128)(2,1)S(1)} %chip_sum.1.refs_0_), channel_id=1, source_target_pairs={{0,24},{4,28},{8,16},{12,20},{16,8},{20,12},{24,0},{28,4},{1,25},{... | collective-permute-start | bytes 245768 | tf_op jit(solution)/shard_map/ppermute | solution.py:243
  50.3 3.7 %copy-start.7 = (bf16[16,1,2048]{2,0,1:T(8,128)(2,1)S(1)}, bf16[16,1,2048]{2,0,1:T(8,128)(2,1)}, u32[]{:S(2)}) copy-start(bf16[16,1,2048]{2,0,1:T(8,128)(2,1)} %param.9) | copy-start | bytes 196612

commit v3 on v2

--- a/solution.py
+++ b/solution.py
@@ -50,7 +50,7 @@
 
 
 def part(index, size):
-    return pl.ds(pl.multiple_of(index * size, size), size)
+    return pl.ds(index * size if isinstance(index, int) else pl.multiple_of(index * size, size), size)
 
 
 def cross_spectrum(first, left, right, half, scale):
@@ -70,7 +70,8 @@
     return [slice(i, i + width) for i in range(0, period, width)]
 
 
-def pack_kernel(tok_ref, sibling_ref, *pack_refs):
+def pack_kernel(chips, tok_ref, sibling_ref, *refs):
+    pack_refs = refs[-chips:]
     chans = pack_refs[0].shape[1]
     for i, pack_ref in enumerate(pack_refs):
         rows = part(own_index(2 * i), chans)
@@ -85,43 +86,35 @@
             signal[:, part(own_index(2 * i + j), tokens)] = pack_ref[j]
 
 
-def filter_spec_kernel(filt_ref, tok_ref, table_ref, down_ref, spec_ref, acts_ref):
+def filter_spec_kernel(filt_ref, table_ref, spec_ref):
     spec_ref[...] = dot(filt_ref[...].astype(BF16), table_ref[...])
-    acts_ref[...] = dot(down_ref[...], tok_ref[...]).astype(BF16)
-
-
-def grad_u_kernel(filt_spec_ref, up_ref, acts_ref, table_ref, *refs):
-    pack_refs, (spec_ref, keep_ref, give_ref, signal, cross, du, rank) = refs[:-7], refs[-7:]
+
+
+def rank_acts_kernel(down_ref, tok_ref, out_ref):
+    out_ref[...] = dot(down_ref[...], tok_ref[...]).astype(BF16)
+
+
+def grad_u_kernel(groups, filt_spec_ref, up_ref, acts_ref, table_ref, *refs):
+    pack_refs, (spec_ref, keep_ref, give_ref, rank_ref, signal, cross, du) = refs[:-7], refs[-7:]
     length = table_ref.shape[0]
     chips = len(pack_refs)
     _, chans, tokens = pack_refs[0].shape
-    ranks = up_ref.shape[0]
     unpack(pack_refs, signal)
     for cols in blocks(table_ref):
         half = (cols.stop - cols.start) // 2
         spec = dot(signal[...], table_ref[:, cols])
-        spec_ref[:, cols] = spec
+        spec_ref[:, cols] = spec.astype(BF16)
         cross[:, cols] = cross_spectrum(cols.start == 0, spec, filt_spec_ref[:, cols], half, 1.0 / length)
     grad_u = dot_nt(cross[...], table_ref[...]).astype(BF16)
     du[...] = grad_u
-    rank[...] = dot(up_ref[:, part(own_index(0), chans)], grad_u).astype(BF16)
-    low = chips * chans
+    rank = dot(up_ref[:, part(own_index(0), chans)], grad_u).astype(BF16)
+    for i in range(2 * chips):
+        for j in range(groups):
+            rank_ref[i * groups + j, : rank.shape[0]] = rank[:, i * tokens : (i + 1) * tokens]
+            rank_ref[i * groups + j, rank.shape[0] :] = acts_ref[...]
     for i in range(chips):
         for j, out_ref in enumerate((keep_ref, give_ref)):
-            cols = part(own_index(2 * i + j), tokens)
-            out_ref[i * chans : (i + 1) * chans] = du[:, cols]
-            out_ref[low + i * ranks : low + (i + 1) * ranks] = rank[:, cols]
-    for out_ref in (keep_ref, give_ref):
-        out_ref[low + chips * ranks :] = acts_ref[...]
-
-
-def core_sum_kernel(chips, ranks, keep_ref, got_ref, out_ref):
-    rows = chips * ranks
-    low = keep_ref.shape[0] - rows - ranks
-    total = keep_ref[low : low + rows].astype(F32) + got_ref[low : low + rows].astype(F32)
-    out_ref[:rows] = total.astype(BF16)
-    out_ref[rows : rows + ranks] = keep_ref[low + rows :]
-    out_ref[rows + ranks :] = got_ref[low + rows :]
+            out_ref[i] = du[:, part(own_index(2 * i + j), tokens)]
 
 
 def pairwise(values):
@@ -130,34 +123,30 @@
     return values[0]
 
 
-def du_pack_kernel(groups, chans, ranks, keep_ref, got_ref, *refs):
-    total = pairwise([ref[...].astype(F32) for ref in refs[:groups]]).astype(BF16)
-    own_ref, pack_refs = refs[groups], refs[groups + 1 :]
-    rows = (1 + len(pack_refs)) * ranks
-    own_ref[:ranks] = total[:ranks]
-    own_ref[ranks:] = total[rows:]
+def du_pack_kernel(keep_ref, got_ref, *pack_refs):
     for i, pack_ref in enumerate(pack_refs):
-        block = slice((i + 1) * chans, (i + 2) * chans)
-        pack_ref[:chans] = keep_ref[block]
-        pack_ref[chans : 2 * chans] = got_ref[block]
-        pack_ref[2 * chans : 2 * chans + ranks] = total[(i + 1) * ranks : (i + 2) * ranks]
-        pack_ref[2 * chans + ranks :] = total[rows:]
-
-
-def rank_kernel(scale, chans, tok_ref, keep_ref, give_ref, own_ref, *refs):
-    pack_refs, (rank_ref, acts_ref, adapter_ref) = refs[:-3], refs[-3:]
+        pack_ref[0] = keep_ref[i + 1]
+        pack_ref[1] = got_ref[i + 1]
+
+
+def rank_kernel(groups, scale, parts_ref, tok_ref, keep_ref, give_ref, rank_ref, acts_ref, adapter_ref):
     ranks, tokens = rank_ref.shape
     width = tok_ref.shape[0]
-    tails = [own_ref[...]] + [ref[2 * chans :] for ref in pack_refs]
-    rank_grad = pairwise([tail[:ranks].astype(F32) for tail in tails]).astype(BF16)
+    shards = parts_ref.shape[0] // groups
+    total = None
+    for i in range(shards):
+        both = parts_ref[i * groups].astype(F32)
+        for j in range(1, groups):
+            both = both + parts_ref[i * groups + j].astype(F32)
+        acts_ref[:, i * tokens : (i + 1) * tokens] = both[ranks:].astype(BF16)
+        total = both[:ranks] if total is None else total + both[:ranks]
+    rank_grad = total.astype(BF16)
     rank_ref[...] = rank_grad
     adapter_ref[:, :width] = scale * dot_nt(rank_grad, tok_ref[...])
     up = None
-    for i, tail in enumerate(tails):
+    for i in range(shards // 2):
         for j, ref in enumerate((keep_ref, give_ref)):
-            act = tail[(1 + j) * ranks : (2 + j) * ranks]
-            acts_ref[:, part(own_index(2 * i + j), tokens)] = act
-            term = dot_nt(act, ref[i * chans : (i + 1) * chans])
+            term = dot_nt(acts_ref[:, part(own_index(2 * i + j), tokens)], ref[i])
             up = term if up is None else up + term
     adapter_ref[:, width:] = scale * up
 
@@ -171,7 +160,7 @@
 
 
 def filter_grad_kernel(acts_ref, up_ref, spec_ref, table_ref, *refs):
-    pack_refs, out_ref, signal, cross = refs[:-3], refs[-3], refs[-2], refs[-1]
+    pack_refs, (out_ref, signal, cross, out, sems) = refs[:-5], refs[-5:]
     length = table_ref.shape[0]
     chans = pack_refs[0].shape[1]
     unpack(pack_refs, signal)
@@ -180,24 +169,31 @@
     for cols in blocks(table_ref):
         half = (cols.stop - cols.start) // 2
         spec = dot(act, table_ref[:, cols])
-        cross[:, cols] = cross_spectrum(cols.start == 0, spec_ref[:, cols], spec, half, 1.0 / length)
-    out_ref[...] = dot_nt(cross[...], table_ref[...])
+        cross[:, cols] = cross_spectrum(cols.start == 0, spec_ref[:, cols].astype(F32), spec, half, 1.0 / length)
+    copies = []
+    for i in range(sems.shape[0]):
+        lags = part(i, length // sems.shape[0])
+        out[:, lags] = dot_nt(cross[...], table_ref[lags, :])
+        copies.append(pltpu.make_async_copy(out.at[:, lags], out_ref.at[:, lags], sems.at[i]))
+        copies[-1].start()
+    for copy in copies:
+        copy.wait()
 
 
 def input_grad_kernel(keep_ref, got_ref, down_ref, rank_ref, *refs):
     pack_refs, out_ref = refs[:-1], refs[-1]
-    chans = (pack_refs[0].shape[0] - 3 * rank_ref.shape[0]) // 2
+    chans = keep_ref.shape[1]
 
     def put(offset, value):
         index = own_index(offset)
         lift = dot_tn(down_ref[:, part(index, chans)], rank_ref[...])
         out_ref[part(index, chans), :] = (value.astype(F32) + lift).astype(BF16)
 
-    put(0, keep_ref[:chans])
-    put(1, got_ref[:chans])
+    put(0, keep_ref[0])
+    put(1, got_ref[0])
     for i, pack_ref in enumerate(pack_refs):
         for j in range(2):
-            put(2 * (i + 1) + j, pack_ref[j * chans : (j + 1) * chans])
+            put(2 * (i + 1) + j, pack_ref[j])
 
 
 def adapter_sum_kernel(*refs):
@@ -224,14 +220,15 @@
     local = pl.BlockSpec(memory_space=pltpu.VMEM)
     product = 2 * chans * length * 2 * length
 
-    def call(kernel, name, out_shape, args, scratch=(), flops=0):
+    def call(kernel, name, out_shape, args, scratch=(), flops=0, early=0, far_out=False):
         outs = jax.tree.leaves(out_shape)
         moved = sum(int(np.prod(o.shape)) * o.dtype.itemsize for o in outs)
-        out_specs = (local,) * len(outs) if isinstance(out_shape, tuple) else local
+        out_spec = pl.BlockSpec(memory_space=pl.ANY) if far_out else local
+        out_specs = (out_spec,) * len(outs) if isinstance(out_shape, tuple) else out_spec
         return pl.pallas_call(
             kernel,
             out_shape=out_shape,
-            in_specs=[local] * len(args),
+            in_specs=[local] * (len(args) - early) + [pl.BlockSpec(memory_space=pl.ANY)] * early,
             out_specs=out_specs,
             scratch_shapes=scratch,
             cost_estimate=pl.CostEstimate(flops=flops, bytes_accessed=moved, transcendentals=0),
@@ -242,8 +239,9 @@
     def send(value, offset, axis="ctx"):
         return lax.ppermute(value, axis, [(i, i ^ offset) for i in range(mesh.shape[axis])])
 
-    def packed(own, sibling, name):
-        return call(pack_kernel, name, (pack,) * chips, (own, sibling))
+    def packed(own, sibling, name, early=(), flops=0):
+        kernel = functools.partial(pack_kernel, chips)
+        return call(kernel, name, (pack,) * chips, (own, sibling, *early), early=len(early), flops=flops)
 
     def to_chips(packs):
         return [packs[0]] + [send(packs[i], 2 * i) for i in range(1, chips)]
@@ -252,59 +250,44 @@
     pack = shape((2, chans, tokens), BF16)
     sibling_grad = send(tok_grad, 1)
     sibling_input = send(tok_input, 1)
-    grad_packs = packed(tok_grad, sibling_grad, "grad_pack")
-    grad_packs, filt, tok_input = lax.optimization_barrier((grad_packs, filt, tok_input))
+    ahead = 4 * product
+    first = call(lambda out_ref: out_ref.__setitem__(Ellipsis, jnp.zeros_like(out_ref)), "first", shape((8, 128), F32), (), flops=ahead)
+    grad_packs = packed(tok_grad, sibling_grad, "grad_pack", (first,), ahead)
     chan_grad = to_chips(grad_packs)
-    filt_spec, acts_part = call(
-        filter_spec_kernel,
-        "filter_spec",
-        (shape((chans, 2 * length), F32), shape((rank, tokens), BF16)),
-        (filt, tok_input, table, down),
-        flops=product,
-    )
-    input_packs = packed(tok_input, sibling_input, "input_pack")
-    half_du = shape((chips * (chans + rank) + rank, tokens), BF16)
-    grad_spec, keep, give = call(
-        grad_u_kernel,
+    everyone = shards * groups
+    acts_part = call(rank_acts_kernel, "rank_acts", shape((rank, tokens), BF16), (down, tok_input))
+    filt_spec = call(filter_spec_kernel, "filter_spec", shape((chans, 2 * length), F32), (filt, table), flops=product)
+    half_du = shape((chips, chans, tokens), BF16)
+    grad_spec, keep, give, rank_parts = call(
+        functools.partial(grad_u_kernel, groups),
         "grad_u",
-        (shape((chans, 2 * length), F32), half_du, half_du),
+        (shape((chans, 2 * length), BF16), half_du, half_du, shape((everyone, 2 * rank, tokens), BF16)),
         (filt_spec, up, acts_part, table, *chan_grad),
-        scratch=[
-            vmem((chans, length), BF16),
-            vmem((chans, 2 * length), BF16),
-            vmem((chans, length), BF16),
-            vmem((rank, length), BF16),
-        ],
-        flops=2 * product,
-    )
+        scratch=[vmem((chans, length), BF16), vmem((chans, 2 * length), BF16), vmem((chans, length), BF16)],
+    )
+    chan_packs = to_chips(packed(tok_input, sibling_input, "input_pack"))
+    rank_parts, chan_packs = lax.optimization_barrier((rank_parts, chan_packs))
+    all_parts = lax.all_to_all(rank_parts, ("ctx", "grp"), 0, 0, tiled=True)
     got = send(give, 1)
-    input_packs, got = lax.optimization_barrier((input_packs, got))
-    core_part = call(
-        functools.partial(core_sum_kernel, chips, rank),
-        "core_sum",
-        shape(((chips + 2) * rank, tokens), BF16),
-        (keep, got),
-    )
-    chan_packs = to_chips(input_packs)
-    core_parts = [core_part] + [send(core_part, i, "grp") for i in range(1, groups)]
-    own_tail, *du_packs = call(
-        functools.partial(du_pack_kernel, groups, chans, rank),
-        "du_pack",
-        (shape((3 * rank, tokens), BF16),) + (shape((2 * chans + 3 * rank, tokens), BF16),) * (chips - 1),
-        (keep, got, *core_parts),
-    )
+    du_packs = call(du_pack_kernel, "du_pack", (pack,) * (chips - 1), (keep, got))
     tok_packs = [send(du_packs[i], 2 * (i + 1)) for i in range(chips - 1)]
+    all_parts, tok_packs = lax.optimization_barrier((all_parts, tok_packs))
     rank_grad, acts, adapter_part = call(
-        functools.partial(rank_kernel, float(length) ** -0.5, chans),
+        functools.partial(rank_kernel, groups, float(length) ** -0.5),
         "rank_grad",
         (shape((rank, tokens), BF16), shape((rank, length), BF16), shape((rank, width + chans), F32)),
-        (tok_input, keep, give, own_tail, *tok_packs),
-    )
+        (all_parts, tok_input, keep, give),
+        flops=ahead,
+    )
+    grad_input = call(
+        input_grad_kernel, "input_grad", shape((width, tokens), BF16), (keep, got, down, rank_grad, *tok_packs)
+    )
+    other_part, grad_input = lax.optimization_barrier((send(adapter_part, 1), grad_input))
     chip_part = call(
         chip_sum_kernel,
         "chip_sum",
         shape((rank, width + 2 * chans), BF16),
-        (adapter_part, send(adapter_part, 1)),
+        (adapter_part, other_part),
     )
     chip_parts = [chip_part] + [send(chip_part, 2 * i) for i in range(1, chips)]
     filt_grad = call(
@@ -312,11 +295,14 @@
         "filter_grad",
         shape((chans, length), F32),
         (acts, up, grad_spec, table, *chan_packs),
-        scratch=[vmem((chans, length), BF16), vmem((chans, 2 * length), BF16)],
+        scratch=[
+            vmem((chans, length), BF16),
+            vmem((chans, 2 * length), BF16),
+            vmem((chans, length), F32),
+            pltpu.SemaphoreType.DMA((4,)),
+        ],
         flops=2 * product,
-    )
-    grad_input = call(
-        input_grad_kernel, "input_grad", shape((width, tokens), BF16), (keep, got, down, rank_grad, *tok_packs)
+        far_out=True,
     )
     grad_down, grad_up = call(
         adapter_sum_kernel,

time: 56.8 us -> 48.1 us (0.85); the launches traced: 55.9 us -> 47.9 us
  local copies, waits for them, and re-layouts: 7.2 us -> 0.04 us
  waiting for transfers between devices: 15.3 us -> 12.9 us
  Pallas kernels: 10.2 us -> 11 us
  starting transfers between devices: 22.5 us -> 23.2 us
    unnamed x18, local copies, waits for them, and re-layouts: 7.2 us -> 0.04 us
    all_to_all x0 -> x1, starting transfers between devices: none -> 4.92 us  [dense_body(): all_parts = lax.all_to_all(rank_parts, ('ctx', 'grp'), 0, 0, tiled=True)]
    ppermute x19 -> x16, starting transfers between devices: 22.5 us -> 18.2 us  [send(): lax.ppermute(value, axis, [(i, i ^ offset) for i in range(mesh.shape[axis...]
    ppermute x19 -> x16, waiting for transfers between devices: 15.3 us -> 12.9 us  [send(): lax.ppermute(value, axis, [(i, i ^ offset) for i in range(mesh.shape[axis...]
    pallas_call x11 -> x12, Pallas kernels: 10.2 us -> 11 us  [call(): pl.pallas_call(kernel, out_shape=out_shape, in_specs=[local] * (len(args)...]
  transfers between devices with their start and end apart: 19 -> 17, of which waited for: 9 -> 8; matrix products, arithmetic and copies ran while one was open for 0% -> 0% of each run, Pallas kernels for 16% -> 20%
where the time goes in v3:
time: 48.1 us; the launch traced here: 47.9 us
  starting transfers between devices  23.2 us (48%)
  waiting for transfers between devices  12.9 us (27%)
  Pallas kernels  11 us (23%)
  between operations  0.75 us (2%)
    ppermute x16, starting transfers between devices, send(): lax.ppermute(value, axis, [(i, i ^ offset) for i in range(mesh.shape[axis...  18.2 us
    ppermute x16, waiting for transfers between devices, send(): lax.ppermute(value, axis, [(i, i ^ offset) for i in range(mesh.shape[axis...  12.9 us
    pallas_call x12, Pallas kernels, call(): pl.pallas_call(kernel, out_shape=out_shape, in_specs=[local] * (len(args)...  11 us
    all_to_all x1, starting transfers between devices, dense_body(): all_parts = lax.all_to_all(rank_parts, ('ctx', 'grp'), 0, 0, tiled=True)  4.92 us
  transfers between devices with their start and end apart: 17, of which 8 were waited for; matrix products, arithmetic and copies ran while one was open for 0% of the time, Pallas kernels for 20%

profile of v3, /device:TPU:0, one launch (start us, length us, event | category | flops | bytes accessed | tf_op | source)
XLA Modules:
  0.0 47.9 jit_solution(15678890007533659546)
XLA Ops:
  0.6 0.5 %collective-permute-start = (bf16[2048,128]{1,0:T(8,128)(2,1)}, bf16[2048,128]{1,0:T(8,128)(2,1)S(1)}, u32[]{:S(2)}, u32[]{:S(2)}) collective-permute-start(bf16[2048,128]{1,0:T(8,128)(2,1)} %bitcast.16), channel_id=1, source_target_pairs={{0,4},{4,0},{8,12},{12,8},{16,20},{20,16},{24,28},{28,24},{1,5},{5... | collective-permute-start | bytes 1572872 | tf_op jit(solution)/shard_map/ppermute | solution.py:240
  1.2 0.1 collective-permute-start.4
  1.2 1.6 %collective-permute-done.sibling_ref = bf16[2048,128]{1,0:T(8,128)(2,1)S(1)} collective-permute-done((bf16[2048,128]{1,0:T(8,128)(2,1)}, bf16[2048,128]{1,0:T(8,128)(2,1)S(1)}, u32[]{:S(2)}, u32[]{:S(2)}) %collective-permute-start) | collective-permute-done | bytes 524320 | tf_op jit(solution)/shard_map/ppermute | solution.py:240
  2.9 0.0 copy-done.6
  2.9 2.9 %collective-permute-start.1 = (bf16[2,256,128]{2,1,0:T(8,128)(2,1)S(1)}, bf16[2,256,128]{2,1,0:T(8,128)(2,1)S(1)}, u32[]{:S(2)}, u32[]{:S(2)}) collective-permute-start(bf16[2,256,128]{2,1,0:T(8,128)(2,1)S(1)} %get-tuple-element.36), channel_id=1, source_target_pairs={{0,8},{4,12},{8,0},{12,4},{16,24},{20,28},{24,16},{28,20},{1,9},{5... | collective-permute-start | bytes 393224 | tf_op jit(solution)/shard_map/ppermute | solution.py:240
  5.9 1.5 %collective-permute-start.2 = (bf16[2,256,128]{2,1,0:T(8,128)(2,1)S(1)}, bf16[2,256,128]{2,1,0:T(8,128)(2,1)S(1)}, u32[]{:S(2)}, u32[]{:S(2)}) collective-permute-start(bf16[2,256,128]{2,1,0:T(8,128)(2,1)S(1)} %get-tuple-element.37), channel_id=1, source_target_pairs={{0,16},{4,20},{8,24},{12,28},{16,0},{20,4},{24,8},{28,12},{1,17},{... | collective-permute-start | bytes 393224 | tf_op jit(solution)/shard_map/ppermute | solution.py:240
  7.4 0.0 collective-permute-start.3
  7.4 0.0 collective-permute-done.4.sibling_ref
  7.5 0.0 copy-start.5
  7.5 2.0 %collective-permute-start.5 = (bf16[2,256,128]{2,1,0:T(8,128)(2,1)S(1)}, bf16[2,256,128]{2,1,0:T(8,128)(2,1)S(1)}, u32[]{:S(2)}, u32[]{:S(2)}) collective-permute-start(bf16[2,256,128]{2,1,0:T(8,128)(2,1)S(1)} %get-tuple-element.41), channel_id=1, source_target_pairs={{0,8},{4,12},{8,0},{12,4},{16,24},{20,28},{24,16},{28,20},{1,9},{5... | collective-permute-start | bytes 393224 | tf_op jit(solution)/shard_map/ppermute | solution.py:240
  9.5 1.5 %collective-permute-start.6 = (bf16[2,256,128]{2,1,0:T(8,128)(2,1)S(1)}, bf16[2,256,128]{2,1,0:T(8,128)(2,1)S(1)}, u32[]{:S(2)}, u32[]{:S(2)}) collective-permute-start(bf16[2,256,128]{2,1,0:T(8,128)(2,1)S(1)} %get-tuple-element.42), channel_id=1, source_target_pairs={{0,16},{4,20},{8,24},{12,28},{16,0},{20,4},{24,8},{28,12},{1,17},{... | collective-permute-start | bytes 393224 | tf_op jit(solution)/shard_map/ppermute | solution.py:240
  11.0 0.0 collective-permute-done.1.refs_1_
  11.0 2.2 %collective-permute-start.7 = (bf16[2,256,128]{2,1,0:T(8,128)(2,1)S(1)}, bf16[2,256,128]{2,1,0:T(8,128)(2,1)S(1)}, u32[]{:S(2)}, u32[]{:S(2)}) collective-permute-start(bf16[2,256,128]{2,1,0:T(8,128)(2,1)S(1)} %get-tuple-element.43), channel_id=1, source_target_pairs={{0,24},{4,28},{8,16},{12,20},{16,8},{20,12},{24,0},{28,4},{1,25},{... | collective-permute-start | bytes 393224 | tf_op jit(solution)/shard_map/ppermute | solution.py:240
  13.2 0.0 copy-done.4
  13.2 0.2 rank_acts.1.acts_ref
  13.3 0.0 copy-done.3
  13.3 0.0 copy-done
  13.4 1.3 %filter_spec.1.filt_spec_ref = f32[256,2048]{1,0:T(8,128)S(1)} custom-call(f32[256,1024]{1,0:T(8,128)S(1)} %bitcast.11, bf16[1024,2048]{1,0:T(8,128)(2,1)S(1)} %copy-done), custom_call_target="tpu_custom_call" | custom-call | flops 1073741824 | bytes 2097152 | tf_op jit(solution)/shard_map/filter_spec/pallas_call | solution.py:228
  14.6 0.0 collective-permute-done.2.refs_2_
  14.7 0.1 collective-permute-done.3.refs_3_
  14.8 3.6 %grad_u.1 = (bf16[256,2048]{1,0:T(8,128)(2,1)S(1)}, bf16[4,256,128]{2,1,0:T(8,128)(2,1)S(1)}, bf16[4,256,128]{2,1,0:T(8,128)(2,1)S(1)}, bf16[32,32,128]{2,1,0:T(8,128)(2,1)}) custom-call(f32[256,2048]{1,0:T(8,128)S(1)} %filter_spec.1.filt_spec_ref, bf16[16,2048]{1,0:T(8,128)(2,1)S(1)} %bitcast.14, bf16[16,128]{1,0:T(8,128)(2,1)S(1)} %rank_acts.1.acts_ref, ...), custom_call_target="tpu_custom_call" | custom-call | bytes 1835008 | tf_op jit(solution)/shard_map/grad_u/pallas_call | solution.py:228
  18.3 0.0 collective-permute-done.5.refs_1_
  18.3 1.2 %collective-permute-done.6.refs_2_ = bf16[2,256,128]{2,1,0:T(8,128)(2,1)S(1)} collective-permute-done((bf16[2,256,128]{2,1,0:T(8,128)(2,1)S(1)}, bf16[2,256,128]{2,1,0:T(8,128)(2,1)S(1)}, u32[]{:S(2)}, u32[]{:S(2)}) %collective-permute-start.6) | collective-permute-done | bytes 131104 | tf_op jit(solution)/shard_map/ppermute | solution.py:240
  19.6 0.0 collective-permute-done.7.refs_3_
  19.6 4.9 %all-to-all-start = ((bf16[32,32,128]{2,1,0:T(8,128)(2,1)}), bf16[32,32,128]{2,1,0:T(8,128)(2,1)S(1)}, u32[]{:S(2)}, u32[]{:S(2)}) async-start(bf16[32,32,128]{2,1,0:T(8,128)(2,1)} %get-tuple-element.44), calls=%async_computation | async-start | bytes 524288 | tf_op jit(solution)/shard_map/all_to_all | solution.py:270
  24.5 0.0 copy-done.7
  24.5 0.3 collective-permute-start.8
  24.8 1.3 %collective-permute-done.8.got_ref = bf16[4,256,128]{2,1,0:T(8,128)(2,1)S(1)} collective-permute-done((bf16[4,256,128]{2,1,0:T(8,128)(2,1)S(1)}, bf16[4,256,128]{2,1,0:T(8,128)(2,1)S(1)}, u32[]{:S(2)}, u32[]{:S(2)}) %collective-permute-start.8) | collective-permute-done | bytes 262176 | tf_op jit(solution)/shard_map/ppermute | solution.py:240
  26.1 1.8 %collective-permute-start.10 = (bf16[2,256,128]{2,1,0:T(8,128)(2,1)S(1)}, bf16[2,256,128]{2,1,0:T(8,128)(2,1)S(1)}, u32[]{:S(2)}, u32[]{:S(2)}) collective-permute-start(bf16[2,256,128]{2,1,0:T(8,128)(2,1)S(1)} %get-tuple-element.48), channel_id=1, source_target_pairs={{0,16},{4,20},{8,24},{12,28},{16,0},{20,4},{24,8},{28,12},{1,17},{... | collective-permute-start | bytes 393224 | tf_op jit(solution)/shard_map/ppermute | solution.py:240
  28.0 1.5 %collective-permute-start.11 = (bf16[2,256,128]{2,1,0:T(8,128)(2,1)S(1)}, bf16[2,256,128]{2,1,0:T(8,128)(2,1)S(1)}, u32[]{:S(2)}, u32[]{:S(2)}) collective-permute-start(bf16[2,256,128]{2,1,0:T(8,128)(2,1)S(1)} %get-tuple-element.49), channel_id=1, source_target_pairs={{0,24},{4,28},{8,16},{12,20},{16,8},{20,12},{24,0},{28,4},{1,25},{... | collective-permute-start | bytes 393224 | tf_op jit(solution)/shard_map/ppermute | solution.py:240
  29.4 0.3 collective-permute-start.9
  29.7 6.9 %collective-permute-done.10.refs_1_ = bf16[2,256,128]{2,1,0:T(8,128)(2,1)S(1)} collective-permute-done((bf16[2,256,128]{2,1,0:T(8,128)(2,1)S(1)}, bf16[2,256,128]{2,1,0:T(8,128)(2,1)S(1)}, u32[]{:S(2)}, u32[]{:S(2)}) %collective-permute-start.10) | collective-permute-done | bytes 131104 | tf_op jit(solution)/shard_map/ppermute | solution.py:240
  36.6 0.0 collective-permute-done.11.refs_2_
  36.6 0.3 collective-permute-done.9.refs_0_
  36.9 0.0 all-to-all-done.parts_ref
  36.9 0.4 rank_grad.1
  37.3 0.0 collective-permute-start.12
  37.4 1.1 %input_grad.1 = bf16[2048,128]{1,0:T(8,128)(2,1)} custom-call(bf16[4,256,128]{2,1,0:T(8,128)(2,1)S(1)} %get-tuple-element.45.keep_ref, bf16[4,256,128]{2,1,0:T(8,128)(2,1)S(1)} %collective-permute-done.8.got_ref, bf16[16,2048]{1,0:T(8,128)(2,1)S(1)} %bitcast.13, bf16[16,128]{1,0:T(8,128)(2,1)S(1)} %get-tuple-element.52.rank_ref, ...), custom_call_target="tpu_custom_call" | custom-call | bytes 524288 | tf_op jit(solution)/shard_map/input_grad/pallas_call | solution.py:228
  38.5 0.2 collective-permute-done.12.other_ref
  38.7 1.5 %collective-permute-start.13 = (bf16[16,2560]{1,0:T(8,128)(2,1)S(1)}, bf16[16,2560]{1,0:T(8,128)(2,1)S(1)}, u32[]{:S(2)}, u32[]{:S(2)}) collective-permute-start(bf16[16,2560]{1,0:T(8,128)(2,1)S(1)} %chip_sum.1.refs_0_), channel_id=1, source_target_pairs={{0,8},{4,12},{8,0},{12,4},{16,24},{20,28},{24,16},{28,20},{1,9},{5... | collective-permute-start | bytes 245768 | tf_op jit(solution)/shard_map/ppermute | solution.py:240
  40.3 1.5 %collective-permute-start.14 = (bf16[16,2560]{1,0:T(8,128)(2,1)S(1)}, bf16[16,2560]{1,0:T(8,128)(2,1)S(1)}, u32[]{:S(2)}, u32[]{:S(2)}) collective-permute-start(bf16[16,2560]{1,0:T(8,128)(2,1)S(1)} %chip_sum.1.refs_0_), channel_id=1, source_target_pairs={{0,16},{4,20},{8,24},{12,28},{16,0},{20,4},{24,8},{28,12},{1,17},{... | collective-permute-start | bytes 245768 | tf_op jit(solution)/shard_map/ppermute | solution.py:240
  41.8 0.5 %collective-permute-start.15 = (bf16[16,2560]{1,0:T(8,128)(2,1)S(1)}, bf16[16,2560]{1,0:T(8,128)(2,1)S(1)}, u32[]{:S(2)}, u32[]{:S(2)}) collective-permute-start(bf16[16,2560]{1,0:T(8,128)(2,1)S(1)} %chip_sum.1.refs_0_), channel_id=1, source_target_pairs={{0,24},{4,28},{8,16},{12,20},{16,8},{20,12},{24,0},{28,4},{1,25},{... | collective-permute-start | bytes 245768 | tf_op jit(solution)/shard_map/ppermute | solution.py:240
  42.3 0.0 copy-done.1
  42.3 3.5 %filter_grad.1 = f32[256,1024]{1,0:T(8,128)} custom-call(bf16[16,1024]{1,0:T(8,128)(2,1)S(1)} %get-tuple-element.57.acts_ref, bf16[16,2048]{1,0:T(8,128)(2,1)S(1)} %bitcast.15, bf16[256,2048]{1,0:T(8,128)(2,1)S(1)} %get-tuple-element.58.spec_ref, bf16[1024,2048]{1,0:T(8,128)(2,1)S(1)} %copy-done.1, bf16[2,256,128]{2,1,0:T(8,128)(2,1)S(1)} %get-tuple-element.59.refs_0_, ...), custom_call_target="tpu_custom_call" | custom-call | flops 2147483648 | bytes 1048576 | tf_op jit(solution)/shard_map/filter_grad/pallas_call | solution.py:228
  45.9 0.0 collective-permute-done.13.refs_1_
  45.9 0.0 collective-permute-done.14.refs_2_
  45.9 1.2 %collective-permute-done.15.refs_3_ = bf16[16,2560]{1,0:T(8,128)(2,1)S(1)} collective-permute-done((bf16[16,2560]{1,0:T(8,128)(2,1)S(1)}, bf16[16,2560]{1,0:T(8,128)(2,1)S(1)}, u32[]{:S(2)}, u32[]{:S(2)}) %collective-permute-start.15) | collective-permute-done | bytes 81952 | tf_op jit(solution)/shard_map/ppermute | solution.py:240
  47.1 0.8 %adapter_sum.1 = (f32[16,1,2048]{2,1,0:T(1,128)}, f32[16,1,2048]{2,1,0:T(1,128)}) custom-call(bf16[16,2560]{1,0:T(8,128)(2,1)S(1)} %chip_sum.1.refs_0_, bf16[16,2560]{1,0:T(8,128)(2,1)S(1)} %collective-permute-done.13.refs_1_, bf16[16,2560]{1,0:T(8,128)(2,1)S(1)} %collective-permute-done.14.refs_2_, bf16[16,2560]{1,0:T(8,128)(2,1)S(1)} %collective-permute-done.15.refs_3_), custom_call_target="tpu_custom_call" | custom-call | bytes 262144 | tf_op jit(solution)/shard_map/adapter_sum/pallas_call | solution.py:228
  (16 shorter events, 0.1 us)
Async XLA Ops:
  0.6 2.3 %collective-permute-start = (bf16[2048,128]{1,0:T(8,128)(2,1)}, bf16[2048,128]{1,0:T(8,128)(2,1)S(1)}, u32[]{:S(2)}, u32[]{:S(2)}) collective-permute-start(bf16[2048,128]{1,0:T(8,128)(2,1)} %bitcast.16), channel_id=1, source_target_pairs={{0,4},{4,0},{8,12},{12,8},{16,20},{20,16},{24,28},{28,24},{1,5},{5... | collective-permute-start | bytes 1572872 | tf_op jit(solution)/shard_map/ppermute | solution.py:240
  1.1 1.8 %copy-start.6 = (bf16[1,2048,128]{2,1,0:T(8,128)(2,1)S(1)}, bf16[1,2048,128]{2,1,0:T(8,128)(2,1)}, u32[]{:S(2)}) copy-start(bf16[1,2048,128]{2,1,0:T(8,128)(2,1)} %param.7) | copy-start | bytes 1572868
  1.2 6.3 %collective-permute-start.4 = (bf16[2048,128]{1,0:T(8,128)(2,1)}, bf16[2048,128]{1,0:T(8,128)(2,1)S(1)}, u32[]{:S(2)}, u32[]{:S(2)}) collective-permute-start(bf16[2048,128]{1,0:T(8,128)(2,1)} %bitcast.7), channel_id=1, source_target_pairs={{0,4},{4,0},{8,12},{12,8},{16,20},{20,16},{24,28},{28,24},{1,5},{5... | collective-permute-start | bytes 1572872 | tf_op jit(solution)/shard_map/ppermute | solution.py:240
  1.2 6.2 %copy-start.2 = (bf16[1,2048,128]{2,1,0:T(8,128)(2,1)S(1)}, bf16[1,2048,128]{2,1,0:T(8,128)(2,1)}, u32[]{:S(2)}) copy-start(bf16[1,2048,128]{2,1,0:T(8,128)(2,1)} %param.6) | copy-start | bytes 1572868
  1.2 11.9 %copy-start.4 = (bf16[16,1,2048]{2,0,1:T(8,128)(2,1)S(1)}, bf16[16,1,2048]{2,0,1:T(8,128)(2,1)}, u32[]{:S(2)}) copy-start(bf16[16,1,2048]{2,0,1:T(8,128)(2,1)} %param.9) | copy-start | bytes 196612
  1.2 12.1 %copy-start.3 = (f32[1,256,1024]{2,1,0:T(8,128)S(1)}, f32[1,256,1024]{2,1,0:T(8,128)}, u32[]{:S(2)}) copy-start(f32[1,256,1024]{2,1,0:T(8,128)} %param.8) | copy-start | bytes 3145732
  2.9 10.5 %copy-start = (bf16[1024,2048]{1,0:T(8,128)(2,1)S(1)}, bf16[1024,2048]{1,0:T(8,128)(2,1)}, u32[]{:S(2)}) copy-start(bf16[1024,2048]{1,0:T(8,128)(2,1)} %constant.2.clone.table_ref) | copy-start | bytes 12582916
  2.9 8.1 %collective-permute-start.1 = (bf16[2,256,128]{2,1,0:T(8,128)(2,1)S(1)}, bf16[2,256,128]{2,1,0:T(8,128)(2,1)S(1)}, u32[]{:S(2)}, u32[]{:S(2)}) collective-permute-start(bf16[2,256,128]{2,1,0:T(8,128)(2,1)S(1)} %get-tuple-element.36), channel_id=1, source_target_pairs={{0,8},{4,12},{8,0},{12,4},{16,24},{20,28},{24,16},{28,20},{1,9},{5... | collective-permute-start | bytes 393224 | tf_op jit(solution)/shard_map/ppermute | solution.py:240
  5.9 8.8 %collective-permute-start.2 = (bf16[2,256,128]{2,1,0:T(8,128)(2,1)S(1)}, bf16[2,256,128]{2,1,0:T(8,128)(2,1)S(1)}, u32[]{:S(2)}, u32[]{:S(2)}) collective-permute-start(bf16[2,256,128]{2,1,0:T(8,128)(2,1)S(1)} %get-tuple-element.37), channel_id=1, source_target_pairs={{0,16},{4,20},{8,24},{12,28},{16,0},{20,4},{24,8},{28,12},{1,17},{... | collective-permute-start | bytes 393224 | tf_op jit(solution)/shard_map/ppermute | solution.py:240
  7.4 7.4 %collective-permute-start.3 = (bf16[2,256,128]{2,1,0:T(8,128)(2,1)S(1)}, bf16[2,256,128]{2,1,0:T(8,128)(2,1)S(1)}, u32[]{:S(2)}, u32[]{:S(2)}) collective-permute-start(bf16[2,256,128]{2,1,0:T(8,128)(2,1)S(1)} %get-tuple-element.38), channel_id=1, source_target_pairs={{0,24},{4,28},{8,16},{12,20},{16,8},{20,12},{24,0},{28,4},{1,25},{... | collective-permute-start | bytes 393224 | tf_op jit(solution)/shard_map/ppermute | solution.py:240
  7.5 7.3 %copy-start.5 = (bf16[16,1,2048]{2,0,1:T(8,128)(2,1)S(1)}, bf16[16,1,2048]{2,0,1:T(8,128)(2,1)}, u32[]{:S(2)}) copy-start(bf16[16,1,2048]{2,0,1:T(8,128)(2,1)} %param.10) | copy-start | bytes 196612
  7.5 10.9 %collective-permute-start.5 = (bf16[2,256,128]{2,1,0:T(8,128)(2,1)S(1)}, bf16[2,256,128]{2,1,0:T(8,128)(2,1)S(1)}, u32[]{:S(2)}, u32[]{:S(2)}) collective-permute-start(bf16[2,256,128]{2,1,0:T(8,128)(2,1)S(1)} %get-tuple-element.41), channel_id=1, source_target_pairs={{0,8},{4,12},{8,0},{12,4},{16,24},{20,28},{24,16},{28,20},{1,9},{5... | collective-permute-start | bytes 393224 | tf_op jit(solution)/shard_map/ppermute | solution.py:240
  9.5 10.1 %collective-permute-start.6 = (bf16[2,256,128]{2,1,0:T(8,128)(2,1)S(1)}, bf16[2,256,128]{2,1,0:T(8,128)(2,1)S(1)}, u32[]{:S(2)}, u32[]{:S(2)}) collective-permute-start(bf16[2,256,128]{2,1,0:T(8,128)(2,1)S(1)} %get-tuple-element.42), channel_id=1, source_target_pairs={{0,16},{4,20},{8,24},{12,28},{16,0},{20,4},{24,8},{28,12},{1,17},{... | collective-permute-start | bytes 393224 | tf_op jit(solution)/shard_map/ppermute | solution.py:240
  11.0 8.6 %collective-permute-start.7 = (bf16[2,256,128]{2,1,0:T(8,128)(2,1)S(1)}, bf16[2,256,128]{2,1,0:T(8,128)(2,1)S(1)}, u32[]{:S(2)}, u32[]{:S(2)}) collective-permute-start(bf16[2,256,128]{2,1,0:T(8,128)(2,1)S(1)} %get-tuple-element.43), channel_id=1, source_target_pairs={{0,24},{4,28},{8,16},{12,20},{16,8},{20,12},{24,0},{28,4},{1,25},{... | collective-permute-start | bytes 393224 | tf_op jit(solution)/shard_map/ppermute | solution.py:240
  19.6 4.9 %copy-start.7 = (bf16[2,256,128]{2,1,0:T(8,128)(2,1)}, bf16[2,256,128]{2,1,0:T(8,128)(2,1)S(1)}, u32[]{:S(2)}) copy-start(bf16[2,256,128]{2,1,0:T(8,128)(2,1)S(1)} %collective-permute-done.7.refs_3_) | copy-start | bytes 393220
  19.6 17.4 %all-to-all-start = ((bf16[32,32,128]{2,1,0:T(8,128)(2,1)}), bf16[32,32,128]{2,1,0:T(8,128)(2,1)S(1)}, u32[]{:S(2)}, u32[]{:S(2)}) async-start(bf16[32,32,128]{2,1,0:T(8,128)(2,1)} %get-tuple-element.44), calls=%async_computation | async-start | bytes 524288 | tf_op jit(solution)/shard_map/all_to_all | solution.py:270
  24.5 1.6 %collective-permute-start.8 = (bf16[4,256,128]{2,1,0:T(8,128)(2,1)S(1)}, bf16[4,256,128]{2,1,0:T(8,128)(2,1)S(1)}, u32[]{:S(2)}, u32[]{:S(2)}) collective-permute-start(bf16[4,256,128]{2,1,0:T(8,128)(2,1)S(1)} %get-tuple-element.46.give_ref), channel_id=1, source_target_pairs={{0,4},{4,0},{8,12},{12,8},{16,20},{20,16},{24,28},{28,24},{1,5},{5... | collective-permute-start | bytes 786440 | tf_op jit(solution)/shard_map/ppermute | solution.py:240
  26.1 10.5 %collective-permute-start.10 = (bf16[2,256,128]{2,1,0:T(8,128)(2,1)S(1)}, bf16[2,256,128]{2,1,0:T(8,128)(2,1)S(1)}, u32[]{:S(2)}, u32[]{:S(2)}) collective-permute-start(bf16[2,256,128]{2,1,0:T(8,128)(2,1)S(1)} %get-tuple-element.48), channel_id=1, source_target_pairs={{0,16},{4,20},{8,24},{12,28},{16,0},{20,4},{24,8},{28,12},{1,17},{... | collective-permute-start | bytes 393224 | tf_op jit(solution)/shard_map/ppermute | solution.py:240
  28.0 8.6 %collective-permute-start.11 = (bf16[2,256,128]{2,1,0:T(8,128)(2,1)S(1)}, bf16[2,256,128]{2,1,0:T(8,128)(2,1)S(1)}, u32[]{:S(2)}, u32[]{:S(2)}) collective-permute-start(bf16[2,256,128]{2,1,0:T(8,128)(2,1)S(1)} %get-tuple-element.49), channel_id=1, source_target_pairs={{0,24},{4,28},{8,16},{12,20},{16,8},{20,12},{24,0},{28,4},{1,25},{... | collective-permute-start | bytes 393224 | tf_op jit(solution)/shard_map/ppermute | solution.py:240
  29.4 7.5 %collective-permute-start.9 = (bf16[2,256,128]{2,1,0:T(8,128)(2,1)S(1)}, bf16[2,256,128]{2,1,0:T(8,128)(2,1)S(1)}, u32[]{:S(2)}, u32[]{:S(2)}) collective-permute-start(bf16[2,256,128]{2,1,0:T(8,128)(2,1)S(1)} %get-tuple-element.47), channel_id=1, source_target_pairs={{0,8},{4,12},{8,0},{12,4},{16,24},{20,28},{24,16},{28,20},{1,9},{5... | collective-permute-start | bytes 393224 | tf_op jit(solution)/shard_map/ppermute | solution.py:240
  36.9 5.4 %copy-start.1 = (bf16[1024,2048]{1,0:T(8,128)(2,1)S(1)}, bf16[1024,2048]{1,0:T(8,128)(2,1)}, u32[]{:S(2)}) copy-start(bf16[1024,2048]{1,0:T(8,128)(2,1)} %constant.2.clone.table_ref) | copy-start | bytes 12582916
  36.9 5.4 %copy-start.8 = (bf16[2,256,128]{2,1,0:T(8,128)(2,1)S(1)}, bf16[2,256,128]{2,1,0:T(8,128)(2,1)}, u32[]{:S(2)}) copy-start(bf16[2,256,128]{2,1,0:T(8,128)(2,1)} %copy-done.7) | copy-start | bytes 393220
  37.3 1.4 %collective-permute-start.12 = (f32[16,2304]{1,0:T(8,128)S(1)}, f32[16,2304]{1,0:T(8,128)S(1)}, u32[]{:S(2)}, u32[]{:S(2)}) collective-permute-start(f32[16,2304]{1,0:T(8,128)S(1)} %get-tuple-element.51.own_ref), channel_id=1, source_target_pairs={{0,4},{4,0},{8,12},{12,8},{16,20},{20,16},{24,28},{28,24},{1,5},{5... | collective-permute-start | bytes 442376 | tf_op jit(solution)/shard_map/ppermute | solution.py:240
  38.7 7.1 %collective-permute-start.13 = (bf16[16,2560]{1,0:T(8,128)(2,1)S(1)}, bf16[16,2560]{1,0:T(8,128)(2,1)S(1)}, u32[]{:S(2)}, u32[]{:S(2)}) collective-permute-start(bf16[16,2560]{1,0:T(8,128)(2,1)S(1)} %chip_sum.1.refs_0_), channel_id=1, source_target_pairs={{0,8},{4,12},{8,0},{12,4},{16,24},{20,28},{24,16},{28,20},{1,9},{5... | collective-permute-start | bytes 245768 | tf_op jit(solution)/shard_map/ppermute | solution.py:240
  40.3 5.6 %collective-permute-start.14 = (bf16[16,2560]{1,0:T(8,128)(2,1)S(1)}, bf16[16,2560]{1,0:T(8,128)(2,1)S(1)}, u32[]{:S(2)}, u32[]{:S(2)}) collective-permute-start(bf16[16,2560]{1,0:T(8,128)(2,1)S(1)} %chip_sum.1.refs_0_), channel_id=1, source_target_pairs={{0,16},{4,20},{8,24},{12,28},{16,0},{20,4},{24,8},{28,12},{1,17},{... | collective-permute-start | bytes 245768 | tf_op jit(solution)/shard_map/ppermute | solution.py:240
  41.8 5.3 %collective-permute-start.15 = (bf16[16,2560]{1,0:T(8,128)(2,1)S(1)}, bf16[16,2560]{1,0:T(8,128)(2,1)S(1)}, u32[]{:S(2)}, u32[]{:S(2)}) collective-permute-start(bf16[16,2560]{1,0:T(8,128)(2,1)S(1)} %chip_sum.1.refs_0_), channel_id=1, source_target_pairs={{0,24},{4,28},{8,16},{12,20},{16,8},{20,12},{24,0},{28,4},{1,25},{... | collective-permute-start | bytes 245768 | tf_op jit(solution)/shard_map/ppermute | solution.py:240

commit v4 on v3

--- a/solution.py
+++ b/solution.py
@@ -49,6 +49,12 @@
     return jnp.bitwise_xor(lax.axis_index("ctx"), offset)
 
 
+def chip_offset(slot, other=0, device=None):
+    device = lax.axis_index("ctx") if device is None else device
+    odd = jnp.bitwise_and(device, 1) ^ other
+    return 2 * slot if slot not in (1, 2) else jnp.where(odd == 1, 2 * (3 - slot), 2 * slot)
+
+
 def part(index, size):
     return pl.ds(index * size if isinstance(index, int) else pl.multiple_of(index * size, size), size)
 
@@ -74,7 +80,7 @@
     pack_refs = refs[-chips:]
     chans = pack_refs[0].shape[1]
     for i, pack_ref in enumerate(pack_refs):
-        rows = part(own_index(2 * i), chans)
+        rows = part(own_index(chip_offset(i)), chans)
         pack_ref[0] = tok_ref[rows, :]
         pack_ref[1] = sibling_ref[rows, :]
 
@@ -83,7 +89,7 @@
     tokens = pack_refs[0].shape[2]
     for i, pack_ref in enumerate(pack_refs):
         for j in range(2):
-            signal[:, part(own_index(2 * i + j), tokens)] = pack_ref[j]
+            signal[:, part(own_index(chip_offset(i) ^ j), tokens)] = pack_ref[j]
 
 
 def filter_spec_kernel(filt_ref, table_ref, spec_ref):
@@ -114,7 +120,7 @@
             rank_ref[i * groups + j, rank.shape[0] :] = acts_ref[...]
     for i in range(chips):
         for j, out_ref in enumerate((keep_ref, give_ref)):
-            out_ref[i] = du[:, part(own_index(2 * i + j), tokens)]
+            out_ref[i] = du[:, part(own_index(chip_offset(i, j) ^ j), tokens)]
 
 
 def pairwise(values):
@@ -146,7 +152,7 @@
     up = None
     for i in range(shards // 2):
         for j, ref in enumerate((keep_ref, give_ref)):
-            term = dot_nt(acts_ref[:, part(own_index(2 * i + j), tokens)], ref[i])
+            term = dot_nt(acts_ref[:, part(own_index(chip_offset(i, j) ^ j), tokens)], ref[i])
             up = term if up is None else up + term
     adapter_ref[:, width:] = scale * up
 
@@ -193,18 +199,22 @@
     put(1, got_ref[0])
     for i, pack_ref in enumerate(pack_refs):
         for j in range(2):
-            put(2 * (i + 1) + j, pack_ref[j])
+            put(chip_offset(i + 1) ^ j, pack_ref[j])
 
 
 def adapter_sum_kernel(*refs):
     part_refs, down_out, up_out, total, chunks = refs[:-4], refs[-4], refs[-3], refs[-2], refs[-1]
     width = down_out.shape[2]
     chans = (part_refs[0].shape[1] - width) // 2
-    down_out[:, 0, :] = pairwise([ref[:, :width].astype(F32) for ref in part_refs])
+    sums = [ref[:, :width].astype(F32) for ref in part_refs]
+    if len(sums) > 2:
+        odd = jnp.bitwise_and(lax.axis_index("ctx"), 1) == 1
+        sums[1:3] = [jnp.where(odd, sums[2], sums[1]), jnp.where(odd, sums[1], sums[2])]
+    down_out[:, 0, :] = pairwise(sums)
     for i, ref in enumerate(part_refs):
         for j in range(2):
             block = ref[:, width + j * chans : width + (j + 1) * chans]
-            chunks[:, part(own_index(2 * i + j), chans)] = block.astype(F32)
+            chunks[:, part(own_index(chip_offset(i) ^ j), chans)] = block.astype(F32)
     up_out[:, 0, :] = chunks[...]
 
 
@@ -243,8 +253,13 @@
         kernel = functools.partial(pack_kernel, chips)
         return call(kernel, name, (pack,) * chips, (own, sibling, *early), early=len(early), flops=flops)
 
+    def to_chip(value, slot):
+        other = slot if chips < 4 or slot not in (1, 2) else 3 - slot
+        pairs = [(i, i ^ (2 * (other if i % 2 else slot))) for i in range(shards)]
+        return lax.ppermute(value, "ctx", pairs)
+
     def to_chips(packs):
-        return [packs[0]] + [send(packs[i], 2 * i) for i in range(1, chips)]
+        return [packs[0]] + [to_chip(packs[i], i) for i in range(1, chips)]
 
     vmem = pltpu.VMEM
     pack = shape((2, chans, tokens), BF16)
@@ -266,12 +281,14 @@
         scratch=[vmem((chans, length), BF16), vmem((chans, 2 * length), BF16), vmem((chans, length), BF16)],
     )
     chan_packs = to_chips(packed(tok_input, sibling_input, "input_pack"))
+    late_pack = chan_packs.pop(2)
     rank_parts, chan_packs = lax.optimization_barrier((rank_parts, chan_packs))
     all_parts = lax.all_to_all(rank_parts, ("ctx", "grp"), 0, 0, tiled=True)
     got = send(give, 1)
     du_packs = call(du_pack_kernel, "du_pack", (pack,) * (chips - 1), (keep, got))
-    tok_packs = [send(du_packs[i], 2 * (i + 1)) for i in range(chips - 1)]
-    all_parts, tok_packs = lax.optimization_barrier((all_parts, tok_packs))
+    tok_packs = [to_chip(du_packs[i], i + 1) for i in range(chips - 1)]
+    all_parts, tok_packs, late_pack = lax.optimization_barrier((all_parts, tok_packs, late_pack))
+    chan_packs.insert(2, late_pack)
     rank_grad, acts, adapter_part = call(
         functools.partial(rank_kernel, groups, float(length) ** -0.5),
         "rank_grad",
@@ -289,7 +306,7 @@
         shape((rank, width + 2 * chans), BF16),
         (adapter_part, other_part),
     )
-    chip_parts = [chip_part] + [send(chip_part, 2 * i) for i in range(1, chips)]
+    chip_parts = to_chips([chip_part] * chips)
     filt_grad = call(
         filter_grad_kernel,
         "filter_grad",

time: 48.1 us -> 47.4 us (0.985)
  starting transfers between devices: 23.2 us -> 22.1 us
  waiting for transfers between devices: 12.9 us -> 12 us
  Pallas kernels: 11 us -> 11.7 us
  local copies, waits for them, and re-layouts: 0.04 us -> 0.69 us
    ppermute x16 -> x4, starting transfers between devices: 18.2 us -> 0.97 us  [send(): lax.ppermute(value, axis, [(i, i ^ offset) for i in range(mesh.shape[axis...]
    ppermute x0 -> x12, starting transfers between devices: none -> 16.7 us  [to_chip(): return lax.ppermute(value, 'ctx', pairs)]
    ppermute x16 -> x4, waiting for transfers between devices: 12.9 us -> 1.87 us  [send(): lax.ppermute(value, axis, [(i, i ^ offset) for i in range(mesh.shape[axis...]
    ppermute x0 -> x12, waiting for transfers between devices: none -> 10.1 us  [to_chip(): return lax.ppermute(value, 'ctx', pairs)]
    pallas_call x12, Pallas kernels: 11 us -> 11.7 us  [call(): pl.pallas_call(kernel, out_shape=out_shape, in_specs=[local] * (len(args)...]
    unnamed x18, local copies, waits for them, and re-layouts: 0.04 us -> 0.69 us
  transfers between devices with their start and end apart: 17 -> 17, of which waited for: 8 -> 8; matrix products, arithmetic and copies ran while one was open for 0% -> 0% of each run, Pallas kernels for 20% -> 22%
where the time goes in v4:
time: 47.4 us; the launch traced here: 47.2 us
  starting transfers between devices  22.1 us (47%)
  waiting for transfers between devices  12 us (25%)
  Pallas kernels  11.7 us (25%)
  between operations  0.73 us (2%)
  local copies, waits for them, and re-layouts  0.69 us (1%)
    ppermute x12, starting transfers between devices, to_chip(): return lax.ppermute(value, 'ctx', pairs)  16.7 us
    pallas_call x12, Pallas kernels, call(): pl.pallas_call(kernel, out_shape=out_shape, in_specs=[local] * (len(args)...  11.7 us
    ppermute x12, waiting for transfers between devices, to_chip(): return lax.ppermute(value, 'ctx', pairs)  10.1 us
    all_to_all x1, starting transfers between devices, dense_body(): all_parts = lax.all_to_all(rank_parts, ('ctx', 'grp'), 0, 0, tiled=True)  4.48 us
    ppermute x4, waiting for transfers between devices, send(): lax.ppermute(value, axis, [(i, i ^ offset) for i in range(mesh.shape[axis...  1.87 us
    ppermute x4, starting transfers between devices, send(): lax.ppermute(value, axis, [(i, i ^ offset) for i in range(mesh.shape[axis...  0.97 us
  transfers between devices with their start and end apart: 17, of which 8 were waited for; matrix products, arithmetic and copies ran while one was open for 0% of the time, Pallas kernels for 22%

profile of v4, /device:TPU:0, one launch (start us, length us, event | category | flops | bytes accessed | tf_op | source)
XLA Modules:
  0.0 47.2 jit_solution(4058451259410082325)
XLA Ops:
  0.6 0.5 %collective-permute-start = (bf16[2048,128]{1,0:T(8,128)(2,1)}, bf16[2048,128]{1,0:T(8,128)(2,1)S(1)}, u32[]{:S(2)}, u32[]{:S(2)}) collective-permute-start(bf16[2048,128]{1,0:T(8,128)(2,1)} %bitcast.16), channel_id=1, source_target_pairs={{0,4},{4,0},{8,12},{12,8},{16,20},{20,16},{24,28},{28,24},{1,5},{5... | collective-permute-start | bytes 1572872 | tf_op jit(solution)/shard_map/ppermute | solution.py:250
  1.2 0.1 collective-permute-start.4
  1.2 1.6 %collective-permute-done.sibling_ref = bf16[2048,128]{1,0:T(8,128)(2,1)S(1)} collective-permute-done((bf16[2048,128]{1,0:T(8,128)(2,1)}, bf16[2048,128]{1,0:T(8,128)(2,1)S(1)}, u32[]{:S(2)}, u32[]{:S(2)}) %collective-permute-start) | collective-permute-done | bytes 524320 | tf_op jit(solution)/shard_map/ppermute | solution.py:250
  2.9 0.0 copy-done.6
  2.9 2.9 %collective-permute-start.1 = (bf16[2,256,128]{2,1,0:T(8,128)(2,1)S(1)}, bf16[2,256,128]{2,1,0:T(8,128)(2,1)S(1)}, u32[]{:S(2)}, u32[]{:S(2)}) collective-permute-start(bf16[2,256,128]{2,1,0:T(8,128)(2,1)S(1)} %get-tuple-element.36), channel_id=1, source_target_pairs={{0,8},{4,20},{8,0},{12,28},{16,24},{20,4},{24,16},{28,12},{1,9},{5... | collective-permute-start | bytes 393224 | tf_op jit(solution)/shard_map/ppermute | solution.py:259
  5.9 1.5 %collective-permute-start.2 = (bf16[2,256,128]{2,1,0:T(8,128)(2,1)S(1)}, bf16[2,256,128]{2,1,0:T(8,128)(2,1)S(1)}, u32[]{:S(2)}, u32[]{:S(2)}) collective-permute-start(bf16[2,256,128]{2,1,0:T(8,128)(2,1)S(1)} %get-tuple-element.37), channel_id=1, source_target_pairs={{0,16},{4,12},{8,24},{12,4},{16,0},{20,28},{24,8},{28,20},{1,17},{... | collective-permute-start | bytes 393224 | tf_op jit(solution)/shard_map/ppermute | solution.py:259
  7.4 0.0 collective-permute-start.3
  7.4 0.0 collective-permute-done.4.sibling_ref
  7.4 0.0 copy-done.2
  7.4 0.7 %input_pack.1 = (bf16[2,256,128]{2,1,0:T(8,128)(2,1)S(1)}, bf16[2,256,128]{2,1,0:T(8,128)(2,1)S(1)}, bf16[2,256,128]{2,1,0:T(8,128)(2,1)}, bf16[2,256,128]{2,1,0:T(8,128)(2,1)S(1)}) custom-call(bf16[2048,128]{1,0:T(8,128)(2,1)S(1)} %bitcast.8, bf16[2048,128]{1,0:T(8,128)(2,1)S(1)} %collective-permute-done.4.sibling_ref), custom_call_target="tpu_custom_call" | custom-call | bytes 524288 | tf_op jit(solution)/shard_map/input_pack/pallas_call | solution.py:238
  8.1 1.9 %collective-permute-start.5 = (bf16[2,256,128]{2,1,0:T(8,128)(2,1)S(1)}, bf16[2,256,128]{2,1,0:T(8,128)(2,1)S(1)}, u32[]{:S(2)}, u32[]{:S(2)}) collective-permute-start(bf16[2,256,128]{2,1,0:T(8,128)(2,1)S(1)} %get-tuple-element.41), channel_id=1, source_target_pairs={{0,8},{4,20},{8,0},{12,28},{16,24},{20,4},{24,16},{28,12},{1,9},{5... | collective-permute-start | bytes 393224 | tf_op jit(solution)/shard_map/ppermute | solution.py:259
  10.1 1.5 %collective-permute-start.6 = (bf16[2,256,128]{2,1,0:T(8,128)(2,1)S(1)}, bf16[2,256,128]{2,1,0:T(8,128)(2,1)S(1)}, u32[]{:S(2)}, u32[]{:S(2)}) collective-permute-start(bf16[2,256,128]{2,1,0:T(8,128)(2,1)S(1)} %get-tuple-element.42), channel_id=1, source_target_pairs={{0,24},{4,28},{8,16},{12,20},{16,8},{20,12},{24,0},{28,4},{1,25},{... | collective-permute-start | bytes 393224 | tf_op jit(solution)/shard_map/ppermute | solution.py:259
  11.5 0.0 copy-done.4
  11.5 0.2 rank_acts.1.acts_ref
  11.7 0.0 copy-done.3
  11.7 0.0 copy-done
  11.7 1.3 %filter_spec.1.filt_spec_ref = f32[256,2048]{1,0:T(8,128)S(1)} custom-call(f32[256,1024]{1,0:T(8,128)S(1)} %bitcast.11, bf16[1024,2048]{1,0:T(8,128)(2,1)S(1)} %copy-done), custom_call_target="tpu_custom_call" | custom-call | flops 1073741824 | bytes 2097152 | tf_op jit(solution)/shard_map/filter_spec/pallas_call | solution.py:238
  13.0 0.0 collective-permute-done.1.refs_1_
  13.0 2.5 %collective-permute-done.2.refs_2_ = bf16[2,256,128]{2,1,0:T(8,128)(2,1)S(1)} collective-permute-done((bf16[2,256,128]{2,1,0:T(8,128)(2,1)S(1)}, bf16[2,256,128]{2,1,0:T(8,128)(2,1)S(1)}, u32[]{:S(2)}, u32[]{:S(2)}) %collective-permute-start.2) | collective-permute-done | bytes 131104 | tf_op jit(solution)/shard_map/ppermute | solution.py:259
  15.5 0.0 collective-permute-done.3.refs_3_
  15.6 3.6 %grad_u.1 = (bf16[256,2048]{1,0:T(8,128)(2,1)S(1)}, bf16[4,256,128]{2,1,0:T(8,128)(2,1)S(1)}, bf16[4,256,128]{2,1,0:T(8,128)(2,1)S(1)}, bf16[32,32,128]{2,1,0:T(8,128)(2,1)}) custom-call(f32[256,2048]{1,0:T(8,128)S(1)} %filter_spec.1.filt_spec_ref, bf16[16,2048]{1,0:T(8,128)(2,1)S(1)} %bitcast.14, bf16[16,128]{1,0:T(8,128)(2,1)S(1)} %rank_acts.1.acts_ref, ...), custom_call_target="tpu_custom_call" | custom-call | bytes 1835008 | tf_op jit(solution)/shard_map/grad_u/pallas_call | solution.py:238
  19.1 0.0 collective-permute-done.5.refs_1_
  19.1 0.0 collective-permute-done.6.refs_3_
  19.1 4.5 %all-to-all-start = ((bf16[32,32,128]{2,1,0:T(8,128)(2,1)}), bf16[32,32,128]{2,1,0:T(8,128)(2,1)S(1)}, u32[]{:S(2)}, u32[]{:S(2)}) async-start(bf16[32,32,128]{2,1,0:T(8,128)(2,1)} %get-tuple-element.43), calls=%async_computation | async-start | bytes 524288 | tf_op jit(solution)/shard_map/all_to_all | solution.py:286
  23.6 0.3 collective-permute-start.7
  23.9 1.7 %collective-permute-start.11 = (bf16[2,256,128]{2,1,0:T(8,128)(2,1)}, bf16[2,256,128]{2,1,0:T(8,128)(2,1)S(1)}, u32[]{:S(2)}, u32[]{:S(2)}) collective-permute-start(bf16[2,256,128]{2,1,0:T(8,128)(2,1)} %get-tuple-element.49), channel_id=1, source_target_pairs={{0,16},{4,12},{8,24},{12,4},{16,0},{20,28},{24,8},{28,20},{1,17},{... | collective-permute-start | bytes 393224 | tf_op jit(solution)/shard_map/ppermute | solution.py:259
  25.6 0.0 collective-permute-done.7.got_ref
  25.6 2.3 %collective-permute-start.10 = (bf16[2,256,128]{2,1,0:T(8,128)(2,1)S(1)}, bf16[2,256,128]{2,1,0:T(8,128)(2,1)S(1)}, u32[]{:S(2)}, u32[]{:S(2)}) collective-permute-start(bf16[2,256,128]{2,1,0:T(8,128)(2,1)S(1)} %get-tuple-element.48), channel_id=1, source_target_pairs={{0,24},{4,28},{8,16},{12,20},{16,8},{20,12},{24,0},{28,4},{1,25},{... | collective-permute-start | bytes 393224 | tf_op jit(solution)/shard_map/ppermute | solution.py:259
  28.0 0.6 %collective-permute-start.8 = (bf16[2,256,128]{2,1,0:T(8,128)(2,1)S(1)}, bf16[2,256,128]{2,1,0:T(8,128)(2,1)S(1)}, u32[]{:S(2)}, u32[]{:S(2)}) collective-permute-start(bf16[2,256,128]{2,1,0:T(8,128)(2,1)S(1)} %get-tuple-element.46), channel_id=1, source_target_pairs={{0,8},{4,20},{8,0},{12,28},{16,24},{20,4},{24,16},{28,12},{1,9},{5... | collective-permute-start | bytes 393224 | tf_op jit(solution)/shard_map/ppermute | solution.py:259
  28.5 0.6 %collective-permute-start.9 = (bf16[2,256,128]{2,1,0:T(8,128)(2,1)S(1)}, bf16[2,256,128]{2,1,0:T(8,128)(2,1)S(1)}, u32[]{:S(2)}, u32[]{:S(2)}) collective-permute-start(bf16[2,256,128]{2,1,0:T(8,128)(2,1)S(1)} %get-tuple-element.47), channel_id=1, source_target_pairs={{0,16},{4,12},{8,24},{12,4},{16,0},{20,28},{24,8},{28,20},{1,17},{... | collective-permute-start | bytes 393224 | tf_op jit(solution)/shard_map/ppermute | solution.py:259
  29.2 4.0 %collective-permute-done.11.refs_2_ = bf16[2,256,128]{2,1,0:T(8,128)(2,1)S(1)} collective-permute-done((bf16[2,256,128]{2,1,0:T(8,128)(2,1)}, bf16[2,256,128]{2,1,0:T(8,128)(2,1)S(1)}, u32[]{:S(2)}, u32[]{:S(2)}) %collective-permute-start.11) | collective-permute-done | bytes 131104 | tf_op jit(solution)/shard_map/ppermute | solution.py:259
  33.2 0.7 %copy-done.7 = bf16[2,256,128]{2,1,0:T(8,128)(2,1)} copy-done((bf16[2,256,128]{2,1,0:T(8,128)(2,1)}, bf16[2,256,128]{2,1,0:T(8,128)(2,1)S(1)}, u32[]{:S(2)}) %copy-start.7) | copy-done | bytes 131096
  33.8 0.2 collective-permute-done.10.refs_2_
  34.0 2.5 %collective-permute-done.8.refs_0_ = bf16[2,256,128]{2,1,0:T(8,128)(2,1)S(1)} collective-permute-done((bf16[2,256,128]{2,1,0:T(8,128)(2,1)S(1)}, bf16[2,256,128]{2,1,0:T(8,128)(2,1)S(1)}, u32[]{:S(2)}, u32[]{:S(2)}) %collective-permute-start.8) | collective-permute-done | bytes 131104 | tf_op jit(solution)/shard_map/ppermute | solution.py:259
  36.5 0.4 collective-permute-done.9.refs_1_
  36.9 0.0 all-to-all-done.parts_ref
  37.0 0.4 rank_grad.1
  37.3 0.0 collective-permute-start.12
  37.4 1.1 %input_grad.1 = bf16[2048,128]{1,0:T(8,128)(2,1)} custom-call(bf16[4,256,128]{2,1,0:T(8,128)(2,1)S(1)} %get-tuple-element.44.keep_ref, bf16[4,256,128]{2,1,0:T(8,128)(2,1)S(1)} %collective-permute-done.7.got_ref, bf16[16,2048]{1,0:T(8,128)(2,1)S(1)} %bitcast.13, bf16[16,128]{1,0:T(8,128)(2,1)S(1)} %get-tuple-element.52.rank_ref, ...), custom_call_target="tpu_custom_call" | custom-call | bytes 524288 | tf_op jit(solution)/shard_map/input_grad/pallas_call | solution.py:238
  38.5 0.2 collective-permute-done.12.other_ref
  38.8 1.3 %collective-permute-start.13 = (bf16[16,2560]{1,0:T(8,128)(2,1)S(1)}, bf16[16,2560]{1,0:T(8,128)(2,1)S(1)}, u32[]{:S(2)}, u32[]{:S(2)}) collective-permute-start(bf16[16,2560]{1,0:T(8,128)(2,1)S(1)} %chip_sum.1.refs_0_), channel_id=1, source_target_pairs={{0,8},{4,20},{8,0},{12,28},{16,24},{20,4},{24,16},{28,12},{1,9},{5... | collective-permute-start | bytes 245768 | tf_op jit(solution)/shard_map/ppermute | solution.py:259
  40.0 1.0 %collective-permute-start.14 = (bf16[16,2560]{1,0:T(8,128)(2,1)S(1)}, bf16[16,2560]{1,0:T(8,128)(2,1)S(1)}, u32[]{:S(2)}, u32[]{:S(2)}) collective-permute-start(bf16[16,2560]{1,0:T(8,128)(2,1)S(1)} %chip_sum.1.refs_0_), channel_id=1, source_target_pairs={{0,16},{4,12},{8,24},{12,4},{16,0},{20,28},{24,8},{28,20},{1,17},{... | collective-permute-start | bytes 245768 | tf_op jit(solution)/shard_map/ppermute | solution.py:259
  41.1 1.3 %collective-permute-start.15 = (bf16[16,2560]{1,0:T(8,128)(2,1)S(1)}, bf16[16,2560]{1,0:T(8,128)(2,1)S(1)}, u32[]{:S(2)}, u32[]{:S(2)}) collective-permute-start(bf16[16,2560]{1,0:T(8,128)(2,1)S(1)} %chip_sum.1.refs_0_), channel_id=1, source_target_pairs={{0,24},{4,28},{8,16},{12,20},{16,8},{20,12},{24,0},{28,4},{1,25},{... | collective-permute-start | bytes 245768 | tf_op jit(solution)/shard_map/ppermute | solution.py:259
  42.3 3.5 %filter_grad.1 = f32[256,1024]{1,0:T(8,128)} custom-call(bf16[16,1024]{1,0:T(8,128)(2,1)S(1)} %get-tuple-element.57.acts_ref, bf16[16,2048]{1,0:T(8,128)(2,1)S(1)} %bitcast.15, bf16[256,2048]{1,0:T(8,128)(2,1)S(1)} %get-tuple-element.58.spec_ref, bf16[1024,2048]{1,0:T(8,128)(2,1)S(1)} %copy-done.1, bf16[2,256,128]{2,1,0:T(8,128)(2,1)S(1)} %get-tuple-element.59.refs_0_, ...), custom_call_target="tpu_custom_call" | custom-call | flops 2147483648 | bytes 1048576 | tf_op jit(solution)/shard_map/filter_grad/pallas_call | solution.py:238
  45.9 0.0 collective-permute-done.13.refs_1_
  45.9 0.0 collective-permute-done.14.refs_2_
  45.9 0.5 %collective-permute-done.15.refs_3_ = bf16[16,2560]{1,0:T(8,128)(2,1)S(1)} collective-permute-done((bf16[16,2560]{1,0:T(8,128)(2,1)S(1)}, bf16[16,2560]{1,0:T(8,128)(2,1)S(1)}, u32[]{:S(2)}, u32[]{:S(2)}) %collective-permute-start.15) | collective-permute-done | bytes 81952 | tf_op jit(solution)/shard_map/ppermute | solution.py:259
  46.4 0.8 %adapter_sum.1 = (f32[16,1,2048]{2,1,0:T(1,128)}, f32[16,1,2048]{2,1,0:T(1,128)}) custom-call(bf16[16,2560]{1,0:T(8,128)(2,1)S(1)} %chip_sum.1.refs_0_, bf16[16,2560]{1,0:T(8,128)(2,1)S(1)} %collective-permute-done.13.refs_1_, bf16[16,2560]{1,0:T(8,128)(2,1)S(1)} %collective-permute-done.14.refs_2_, bf16[16,2560]{1,0:T(8,128)(2,1)S(1)} %collective-permute-done.15.refs_3_), custom_call_target="tpu_custom_call" | custom-call | bytes 262144 | tf_op jit(solution)/shard_map/adapter_sum/pallas_call | solution.py:238
  (16 shorter events, 0.1 us)
Async XLA Ops:
  0.6 2.3 %collective-permute-start = (bf16[2048,128]{1,0:T(8,128)(2,1)}, bf16[2048,128]{1,0:T(8,128)(2,1)S(1)}, u32[]{:S(2)}, u32[]{:S(2)}) collective-permute-start(bf16[2048,128]{1,0:T(8,128)(2,1)} %bitcast.16), channel_id=1, source_target_pairs={{0,4},{4,0},{8,12},{12,8},{16,20},{20,16},{24,28},{28,24},{1,5},{5... | collective-permute-start | bytes 1572872 | tf_op jit(solution)/shard_map/ppermute | solution.py:250
  1.1 1.8 %copy-start.6 = (bf16[1,2048,128]{2,1,0:T(8,128)(2,1)S(1)}, bf16[1,2048,128]{2,1,0:T(8,128)(2,1)}, u32[]{:S(2)}) copy-start(bf16[1,2048,128]{2,1,0:T(8,128)(2,1)} %param.7) | copy-start | bytes 1572868
  1.2 6.3 %collective-permute-start.4 = (bf16[2048,128]{1,0:T(8,128)(2,1)}, bf16[2048,128]{1,0:T(8,128)(2,1)S(1)}, u32[]{:S(2)}, u32[]{:S(2)}) collective-permute-start(bf16[2048,128]{1,0:T(8,128)(2,1)} %bitcast.7), channel_id=1, source_target_pairs={{0,4},{4,0},{8,12},{12,8},{16,20},{20,16},{24,28},{28,24},{1,5},{5... | collective-permute-start | bytes 1572872 | tf_op jit(solution)/shard_map/ppermute | solution.py:250
  1.2 6.2 %copy-start.2 = (bf16[1,2048,128]{2,1,0:T(8,128)(2,1)S(1)}, bf16[1,2048,128]{2,1,0:T(8,128)(2,1)}, u32[]{:S(2)}) copy-start(bf16[1,2048,128]{2,1,0:T(8,128)(2,1)} %param.6) | copy-start | bytes 1572868
  1.2 10.3 %copy-start.4 = (bf16[16,1,2048]{2,0,1:T(8,128)(2,1)S(1)}, bf16[16,1,2048]{2,0,1:T(8,128)(2,1)}, u32[]{:S(2)}) copy-start(bf16[16,1,2048]{2,0,1:T(8,128)(2,1)} %param.9) | copy-start | bytes 196612
  1.2 10.5 %copy-start.3 = (f32[1,256,1024]{2,1,0:T(8,128)S(1)}, f32[1,256,1024]{2,1,0:T(8,128)}, u32[]{:S(2)}) copy-start(f32[1,256,1024]{2,1,0:T(8,128)} %param.8) | copy-start | bytes 3145732
  2.9 8.8 %copy-start = (bf16[1024,2048]{1,0:T(8,128)(2,1)S(1)}, bf16[1024,2048]{1,0:T(8,128)(2,1)}, u32[]{:S(2)}) copy-start(bf16[1024,2048]{1,0:T(8,128)(2,1)} %constant.2.clone.table_ref) | copy-start | bytes 12582916
  2.9 10.1 %collective-permute-start.1 = (bf16[2,256,128]{2,1,0:T(8,128)(2,1)S(1)}, bf16[2,256,128]{2,1,0:T(8,128)(2,1)S(1)}, u32[]{:S(2)}, u32[]{:S(2)}) collective-permute-start(bf16[2,256,128]{2,1,0:T(8,128)(2,1)S(1)} %get-tuple-element.36), channel_id=1, source_target_pairs={{0,8},{4,20},{8,0},{12,28},{16,24},{20,4},{24,16},{28,12},{1,9},{5... | collective-permute-start | bytes 393224 | tf_op jit(solution)/shard_map/ppermute | solution.py:259
  5.9 9.7 %collective-permute-start.2 = (bf16[2,256,128]{2,1,0:T(8,128)(2,1)S(1)}, bf16[2,256,128]{2,1,0:T(8,128)(2,1)S(1)}, u32[]{:S(2)}, u32[]{:S(2)}) collective-permute-start(bf16[2,256,128]{2,1,0:T(8,128)(2,1)S(1)} %get-tuple-element.37), channel_id=1, source_target_pairs={{0,16},{4,12},{8,24},{12,4},{16,0},{20,28},{24,8},{28,20},{1,17},{... | collective-permute-start | bytes 393224 | tf_op jit(solution)/shard_map/ppermute | solution.py:259
  7.4 8.1 %collective-permute-start.3 = (bf16[2,256,128]{2,1,0:T(8,128)(2,1)S(1)}, bf16[2,256,128]{2,1,0:T(8,128)(2,1)S(1)}, u32[]{:S(2)}, u32[]{:S(2)}) collective-permute-start(bf16[2,256,128]{2,1,0:T(8,128)(2,1)S(1)} %get-tuple-element.38), channel_id=1, source_target_pairs={{0,24},{4,28},{8,16},{12,20},{16,8},{20,12},{24,0},{28,4},{1,25},{... | collective-permute-start | bytes 393224 | tf_op jit(solution)/shard_map/ppermute | solution.py:259
  8.1 7.4 %copy-start.5 = (bf16[16,1,2048]{2,0,1:T(8,128)(2,1)S(1)}, bf16[16,1,2048]{2,0,1:T(8,128)(2,1)}, u32[]{:S(2)}) copy-start(bf16[16,1,2048]{2,0,1:T(8,128)(2,1)} %param.10) | copy-start | bytes 196612
  8.1 11.0 %collective-permute-start.5 = (bf16[2,256,128]{2,1,0:T(8,128)(2,1)S(1)}, bf16[2,256,128]{2,1,0:T(8,128)(2,1)S(1)}, u32[]{:S(2)}, u32[]{:S(2)}) collective-permute-start(bf16[2,256,128]{2,1,0:T(8,128)(2,1)S(1)} %get-tuple-element.41), channel_id=1, source_target_pairs={{0,8},{4,20},{8,0},{12,28},{16,24},{20,4},{24,16},{28,12},{1,9},{5... | collective-permute-start | bytes 393224 | tf_op jit(solution)/shard_map/ppermute | solution.py:259
  10.1 9.1 %collective-permute-start.6 = (bf16[2,256,128]{2,1,0:T(8,128)(2,1)S(1)}, bf16[2,256,128]{2,1,0:T(8,128)(2,1)S(1)}, u32[]{:S(2)}, u32[]{:S(2)}) collective-permute-start(bf16[2,256,128]{2,1,0:T(8,128)(2,1)S(1)} %get-tuple-element.42), channel_id=1, source_target_pairs={{0,24},{4,28},{8,16},{12,20},{16,8},{20,12},{24,0},{28,4},{1,25},{... | collective-permute-start | bytes 393224 | tf_op jit(solution)/shard_map/ppermute | solution.py:259
  19.1 17.8 %all-to-all-start = ((bf16[32,32,128]{2,1,0:T(8,128)(2,1)}), bf16[32,32,128]{2,1,0:T(8,128)(2,1)S(1)}, u32[]{:S(2)}, u32[]{:S(2)}) async-start(bf16[32,32,128]{2,1,0:T(8,128)(2,1)} %get-tuple-element.43), calls=%async_computation | async-start | bytes 524288 | tf_op jit(solution)/shard_map/all_to_all | solution.py:286
  23.6 2.0 %collective-permute-start.7 = (bf16[4,256,128]{2,1,0:T(8,128)(2,1)S(1)}, bf16[4,256,128]{2,1,0:T(8,128)(2,1)S(1)}, u32[]{:S(2)}, u32[]{:S(2)}) collective-permute-start(bf16[4,256,128]{2,1,0:T(8,128)(2,1)S(1)} %get-tuple-element.45.give_ref), channel_id=1, source_target_pairs={{0,4},{4,0},{8,12},{12,8},{16,20},{20,16},{24,28},{28,24},{1,5},{5... | collective-permute-start | bytes 786440 | tf_op jit(solution)/shard_map/ppermute | solution.py:250
  23.9 9.2 %collective-permute-start.11 = (bf16[2,256,128]{2,1,0:T(8,128)(2,1)}, bf16[2,256,128]{2,1,0:T(8,128)(2,1)S(1)}, u32[]{:S(2)}, u32[]{:S(2)}) collective-permute-start(bf16[2,256,128]{2,1,0:T(8,128)(2,1)} %get-tuple-element.49), channel_id=1, source_target_pairs={{0,16},{4,12},{8,24},{12,4},{16,0},{20,28},{24,8},{28,20},{1,17},{... | collective-permute-start | bytes 393224 | tf_op jit(solution)/shard_map/ppermute | solution.py:259
  25.6 8.4 %collective-permute-start.10 = (bf16[2,256,128]{2,1,0:T(8,128)(2,1)S(1)}, bf16[2,256,128]{2,1,0:T(8,128)(2,1)S(1)}, u32[]{:S(2)}, u32[]{:S(2)}) collective-permute-start(bf16[2,256,128]{2,1,0:T(8,128)(2,1)S(1)} %get-tuple-element.48), channel_id=1, source_target_pairs={{0,24},{4,28},{8,16},{12,20},{16,8},{20,12},{24,0},{28,4},{1,25},{... | collective-permute-start | bytes 393224 | tf_op jit(solution)/shard_map/ppermute | solution.py:259
  28.0 8.5 %collective-permute-start.8 = (bf16[2,256,128]{2,1,0:T(8,128)(2,1)S(1)}, bf16[2,256,128]{2,1,0:T(8,128)(2,1)S(1)}, u32[]{:S(2)}, u32[]{:S(2)}) collective-permute-start(bf16[2,256,128]{2,1,0:T(8,128)(2,1)S(1)} %get-tuple-element.46), channel_id=1, source_target_pairs={{0,8},{4,20},{8,0},{12,28},{16,24},{20,4},{24,16},{28,12},{1,9},{5... | collective-permute-start | bytes 393224 | tf_op jit(solution)/shard_map/ppermute | solution.py:259
  28.5 8.4 %collective-permute-start.9 = (bf16[2,256,128]{2,1,0:T(8,128)(2,1)S(1)}, bf16[2,256,128]{2,1,0:T(8,128)(2,1)S(1)}, u32[]{:S(2)}, u32[]{:S(2)}) collective-permute-start(bf16[2,256,128]{2,1,0:T(8,128)(2,1)S(1)} %get-tuple-element.47), channel_id=1, source_target_pairs={{0,16},{4,12},{8,24},{12,4},{16,0},{20,28},{24,8},{28,20},{1,17},{... | collective-permute-start | bytes 393224 | tf_op jit(solution)/shard_map/ppermute | solution.py:259
  33.2 0.7 %copy-start.7 = (bf16[2,256,128]{2,1,0:T(8,128)(2,1)}, bf16[2,256,128]{2,1,0:T(8,128)(2,1)S(1)}, u32[]{:S(2)}) copy-start(bf16[2,256,128]{2,1,0:T(8,128)(2,1)S(1)} %collective-permute-done.11.refs_2_) | copy-start | bytes 393220
  36.9 5.4 %copy-start.1 = (bf16[1024,2048]{1,0:T(8,128)(2,1)S(1)}, bf16[1024,2048]{1,0:T(8,128)(2,1)}, u32[]{:S(2)}) copy-start(bf16[1024,2048]{1,0:T(8,128)(2,1)} %constant.2.clone.table_ref) | copy-start | bytes 12582916
  36.9 5.4 %copy-start.8 = (bf16[2,256,128]{2,1,0:T(8,128)(2,1)S(1)}, bf16[2,256,128]{2,1,0:T(8,128)(2,1)}, u32[]{:S(2)}) copy-start(bf16[2,256,128]{2,1,0:T(8,128)(2,1)} %copy-done.7) | copy-start | bytes 393220
  37.3 1.4 %collective-permute-start.12 = (f32[16,2304]{1,0:T(8,128)S(1)}, f32[16,2304]{1,0:T(8,128)S(1)}, u32[]{:S(2)}, u32[]{:S(2)}) collective-permute-start(f32[16,2304]{1,0:T(8,128)S(1)} %get-tuple-element.51.own_ref), channel_id=1, source_target_pairs={{0,4},{4,0},{8,12},{12,8},{16,20},{20,16},{24,28},{28,24},{1,5},{5... | collective-permute-start | bytes 442376 | tf_op jit(solution)/shard_map/ppermute | solution.py:250
  38.8 7.1 %collective-permute-start.13 = (bf16[16,2560]{1,0:T(8,128)(2,1)S(1)}, bf16[16,2560]{1,0:T(8,128)(2,1)S(1)}, u32[]{:S(2)}, u32[]{:S(2)}) collective-permute-start(bf16[16,2560]{1,0:T(8,128)(2,1)S(1)} %chip_sum.1.refs_0_), channel_id=1, source_target_pairs={{0,8},{4,20},{8,0},{12,28},{16,24},{20,4},{24,16},{28,12},{1,9},{5... | collective-permute-start | bytes 245768 | tf_op jit(solution)/shard_map/ppermute | solution.py:259
  40.0 5.9 %collective-permute-start.14 = (bf16[16,2560]{1,0:T(8,128)(2,1)S(1)}, bf16[16,2560]{1,0:T(8,128)(2,1)S(1)}, u32[]{:S(2)}, u32[]{:S(2)}) collective-permute-start(bf16[16,2560]{1,0:T(8,128)(2,1)S(1)} %chip_sum.1.refs_0_), channel_id=1, source_target_pairs={{0,16},{4,12},{8,24},{12,4},{16,0},{20,28},{24,8},{28,20},{1,17},{... | collective-permute-start | bytes 245768 | tf_op jit(solution)/shard_map/ppermute | solution.py:259
  41.1 5.3 %collective-permute-start.15 = (bf16[16,2560]{1,0:T(8,128)(2,1)S(1)}, bf16[16,2560]{1,0:T(8,128)(2,1)S(1)}, u32[]{:S(2)}, u32[]{:S(2)}) collective-permute-start(bf16[16,2560]{1,0:T(8,128)(2,1)S(1)} %chip_sum.1.refs_0_), channel_id=1, source_target_pairs={{0,24},{4,28},{8,16},{12,20},{16,8},{20,12},{24,0},{28,4},{1,25},{... | collective-permute-start | bytes 245768 | tf_op jit(solution)/shard_map/ppermute | solution.py:259

commit v5 on v4

--- a/solution.py
+++ b/solution.py
@@ -281,14 +281,14 @@
         scratch=[vmem((chans, length), BF16), vmem((chans, 2 * length), BF16), vmem((chans, length), BF16)],
     )
     chan_packs = to_chips(packed(tok_input, sibling_input, "input_pack"))
-    late_pack = chan_packs.pop(2)
+    late_pack = chan_packs.pop(1)
     rank_parts, chan_packs = lax.optimization_barrier((rank_parts, chan_packs))
     all_parts = lax.all_to_all(rank_parts, ("ctx", "grp"), 0, 0, tiled=True)
     got = send(give, 1)
     du_packs = call(du_pack_kernel, "du_pack", (pack,) * (chips - 1), (keep, got))
     tok_packs = [to_chip(du_packs[i], i + 1) for i in range(chips - 1)]
-    all_parts, tok_packs, late_pack = lax.optimization_barrier((all_parts, tok_packs, late_pack))
-    chan_packs.insert(2, late_pack)
+    all_parts, tok_packs[:2], late_pack = lax.optimization_barrier((all_parts, tok_packs[:2], late_pack))
+    chan_packs.insert(1, late_pack)
     rank_grad, acts, adapter_part = call(
         functools.partial(rank_kernel, groups, float(length) ** -0.5),
         "rank_grad",
@@ -296,10 +296,7 @@
         (all_parts, tok_input, keep, give),
         flops=ahead,
     )
-    grad_input = call(
-        input_grad_kernel, "input_grad", shape((width, tokens), BF16), (keep, got, down, rank_grad, *tok_packs)
-    )
-    other_part, grad_input = lax.optimization_barrier((send(adapter_part, 1), grad_input))
+    other_part = send(adapter_part, 1)
     chip_part = call(
         chip_sum_kernel,
         "chip_sum",
@@ -316,10 +313,14 @@
             vmem((chans, length), BF16),
             vmem((chans, 2 * length), BF16),
             vmem((chans, length), F32),
-            pltpu.SemaphoreType.DMA((4,)),
+            pltpu.SemaphoreType.DMA((2,)),
         ],
         flops=2 * product,
         far_out=True,
+    )
+    filt_grad, got = lax.optimization_barrier((filt_grad, got))
+    grad_input = call(
+        input_grad_kernel, "input_grad", shape((width, tokens), BF16), (keep, got, down, rank_grad, *tok_packs)
     )
     grad_down, grad_up = call(
         adapter_sum_kernel,

time: 47.4 us -> 45.4 us (0.958)
  waiting for transfers between devices: 12 us -> 8.15 us
  starting transfers between devices: 22.1 us -> 23.8 us
  local copies, waits for them, and re-layouts: 0.69 us -> 1.49 us
  Pallas kernels: 11.7 us -> 11 us
    ppermute x12, waiting for transfers between devices: 10.1 us -> 6.12 us  [to_chip(): return lax.ppermute(value, 'ctx', pairs)]
    ppermute x12, starting transfers between devices: 16.7 us -> 17.8 us  [to_chip(): return lax.ppermute(value, 'ctx', pairs)]
    unnamed x18 -> x22, local copies, waits for them, and re-layouts: 0.69 us -> 1.49 us
    pallas_call x12, Pallas kernels: 11.7 us -> 11 us  [call(): pl.pallas_call(kernel, out_shape=out_shape, in_specs=[local] * (len(args)...]
  transfers between devices with their start and end apart: 17 -> 17, of which waited for: 8 -> 6; matrix products, arithmetic and copies ran while one was open for 0% -> 0% of each run, Pallas kernels for 22% -> 22%
where the time goes in v5:
time: 45.4 us; the launch traced here: 45.2 us
  starting transfers between devices  23.8 us (52%)
  Pallas kernels  11 us (24%)
  waiting for transfers between devices  8.15 us (18%)
  local copies, waits for them, and re-layouts  1.49 us (3%)
  between operations  0.74 us (2%)
    ppermute x12, starting transfers between devices, to_chip(): return lax.ppermute(value, 'ctx', pairs)  17.8 us
    pallas_call x12, Pallas kernels, call(): pl.pallas_call(kernel, out_shape=out_shape, in_specs=[local] * (len(args)...  11 us
    ppermute x12, waiting for transfers between devices, to_chip(): return lax.ppermute(value, 'ctx', pairs)  6.12 us
    all_to_all x1, starting transfers between devices, dense_body(): all_parts = lax.all_to_all(rank_parts, ('ctx', 'grp'), 0, 0, tiled=True)  4.69 us
    ppermute x4, waiting for transfers between devices, send(): lax.ppermute(value, axis, [(i, i ^ offset) for i in range(mesh.shape[axis...  1.66 us
    unnamed x22, local copies, waits for them, and re-layouts  1.49 us
    ppermute x4, starting transfers between devices, send(): lax.ppermute(value, axis, [(i, i ^ offset) for i in range(mesh.shape[axis...  1.29 us
  transfers between devices with their start and end apart: 17, of which 6 were waited for; matrix products, arithmetic and copies ran while one was open for 0% of the time, Pallas kernels for 22%

profile of v5, /device:TPU:0, one launch (start us, length us, event | category | flops | bytes accessed | tf_op | source)
XLA Modules:
  0.0 45.2 jit_solution(9402970633006155946)
XLA Ops:
  0.6 0.5 %collective-permute-start = (bf16[2048,128]{1,0:T(8,128)(2,1)}, bf16[2048,128]{1,0:T(8,128)(2,1)S(1)}, u32[]{:S(2)}, u32[]{:S(2)}) collective-permute-start(bf16[2048,128]{1,0:T(8,128)(2,1)} %bitcast.16), channel_id=1, source_target_pairs={{0,4},{4,0},{8,12},{12,8},{16,20},{20,16},{24,28},{28,24},{1,5},{5... | collective-permute-start | bytes 1572872 | tf_op jit(solution)/shard_map/ppermute | solution.py:250
  1.2 0.1 collective-permute-start.4
  1.2 1.6 %collective-permute-done.sibling_ref = bf16[2048,128]{1,0:T(8,128)(2,1)S(1)} collective-permute-done((bf16[2048,128]{1,0:T(8,128)(2,1)}, bf16[2048,128]{1,0:T(8,128)(2,1)S(1)}, u32[]{:S(2)}, u32[]{:S(2)}) %collective-permute-start) | collective-permute-done | bytes 524320 | tf_op jit(solution)/shard_map/ppermute | solution.py:250
  2.9 0.0 copy-done.6
  2.9 2.9 %collective-permute-start.1 = (bf16[2,256,128]{2,1,0:T(8,128)(2,1)S(1)}, bf16[2,256,128]{2,1,0:T(8,128)(2,1)S(1)}, u32[]{:S(2)}, u32[]{:S(2)}) collective-permute-start(bf16[2,256,128]{2,1,0:T(8,128)(2,1)S(1)} %get-tuple-element.35), channel_id=1, source_target_pairs={{0,8},{4,20},{8,0},{12,28},{16,24},{20,4},{24,16},{28,12},{1,9},{5... | collective-permute-start | bytes 393224 | tf_op jit(solution)/shard_map/ppermute | solution.py:259
  5.9 1.5 %collective-permute-start.2 = (bf16[2,256,128]{2,1,0:T(8,128)(2,1)S(1)}, bf16[2,256,128]{2,1,0:T(8,128)(2,1)S(1)}, u32[]{:S(2)}, u32[]{:S(2)}) collective-permute-start(bf16[2,256,128]{2,1,0:T(8,128)(2,1)S(1)} %get-tuple-element.36), channel_id=1, source_target_pairs={{0,16},{4,12},{8,24},{12,4},{16,0},{20,28},{24,8},{28,20},{1,17},{... | collective-permute-start | bytes 393224 | tf_op jit(solution)/shard_map/ppermute | solution.py:259
  7.4 0.0 collective-permute-start.3
  7.4 0.0 collective-permute-done.4.sibling_ref
  7.5 0.0 copy-start.5
  7.5 2.0 %collective-permute-start.5 = (bf16[2,256,128]{2,1,0:T(8,128)(2,1)S(1)}, bf16[2,256,128]{2,1,0:T(8,128)(2,1)S(1)}, u32[]{:S(2)}, u32[]{:S(2)}) collective-permute-start(bf16[2,256,128]{2,1,0:T(8,128)(2,1)S(1)} %get-tuple-element.41), channel_id=1, source_target_pairs={{0,16},{4,12},{8,24},{12,4},{16,0},{20,28},{24,8},{28,20},{1,17},{... | collective-permute-start | bytes 393224 | tf_op jit(solution)/shard_map/ppermute | solution.py:259
  9.5 1.4 %collective-permute-start.6 = (bf16[2,256,128]{2,1,0:T(8,128)(2,1)S(1)}, bf16[2,256,128]{2,1,0:T(8,128)(2,1)S(1)}, u32[]{:S(2)}, u32[]{:S(2)}) collective-permute-start(bf16[2,256,128]{2,1,0:T(8,128)(2,1)S(1)} %get-tuple-element.42), channel_id=1, source_target_pairs={{0,24},{4,28},{8,16},{12,20},{16,8},{20,12},{24,0},{28,4},{1,25},{... | collective-permute-start | bytes 393224 | tf_op jit(solution)/shard_map/ppermute | solution.py:259
  10.9 0.2 rank_acts.1.acts_ref
  11.1 0.0 copy-done
  11.1 1.3 %filter_spec.1.filt_spec_ref = f32[256,2048]{1,0:T(8,128)S(1)} custom-call(f32[256,1024]{1,0:T(8,128)S(1)} %bitcast.11, bf16[1024,2048]{1,0:T(8,128)(2,1)S(1)} %copy-done), custom_call_target="tpu_custom_call" | custom-call | flops 1073741824 | bytes 2097152 | tf_op jit(solution)/shard_map/filter_spec/pallas_call | solution.py:238
  12.4 0.0 collective-permute-done.1.refs_1_
  12.4 0.0 collective-permute-done.2.refs_2_
  12.4 2.3 %collective-permute-done.3.refs_3_ = bf16[2,256,128]{2,1,0:T(8,128)(2,1)S(1)} collective-permute-done((bf16[2,256,128]{2,1,0:T(8,128)(2,1)S(1)}, bf16[2,256,128]{2,1,0:T(8,128)(2,1)S(1)}, u32[]{:S(2)}, u32[]{:S(2)}) %collective-permute-start.3) | collective-permute-done | bytes 131104 | tf_op jit(solution)/shard_map/ppermute | solution.py:259
  14.8 3.6 %grad_u.1 = (bf16[256,2048]{1,0:T(8,128)(2,1)S(1)}, bf16[4,256,128]{2,1,0:T(8,128)(2,1)S(1)}, bf16[4,256,128]{2,1,0:T(8,128)(2,1)S(1)}, bf16[32,32,128]{2,1,0:T(8,128)(2,1)}) custom-call(f32[256,2048]{1,0:T(8,128)S(1)} %filter_spec.1.filt_spec_ref, bf16[16,2048]{1,0:T(8,128)(2,1)S(1)} %bitcast.14, bf16[16,128]{1,0:T(8,128)(2,1)S(1)} %rank_acts.1.acts_ref, ...), custom_call_target="tpu_custom_call" | custom-call | bytes 1835008 | tf_op jit(solution)/shard_map/grad_u/pallas_call | solution.py:238
  18.3 0.0 collective-permute-done.5.refs_2_
  18.3 0.0 collective-permute-done.6.refs_3_
  18.3 4.7 %all-to-all-start = ((bf16[32,32,128]{2,1,0:T(8,128)(2,1)}), bf16[32,32,128]{2,1,0:T(8,128)(2,1)S(1)}, u32[]{:S(2)}, u32[]{:S(2)}) async-start(bf16[32,32,128]{2,1,0:T(8,128)(2,1)} %get-tuple-element.43), calls=%async_computation | async-start | bytes 524288 | tf_op jit(solution)/shard_map/all_to_all | solution.py:286
  23.0 0.3 collective-permute-start.7
  23.4 1.7 %collective-permute-start.10 = (bf16[2,256,128]{2,1,0:T(8,128)(2,1)S(1)}, bf16[2,256,128]{2,1,0:T(8,128)(2,1)S(1)}, u32[]{:S(2)}, u32[]{:S(2)}) collective-permute-start(bf16[2,256,128]{2,1,0:T(8,128)(2,1)S(1)} %get-tuple-element.47), channel_id=1, source_target_pairs={{0,8},{4,20},{8,0},{12,28},{16,24},{20,4},{24,16},{28,12},{1,9},{5... | collective-permute-start | bytes 393224 | tf_op jit(solution)/shard_map/ppermute | solution.py:259
  25.0 0.0 collective-permute-done.7.got_ref
  25.1 0.0 copy-start.9
  25.1 0.6 %copy-done.9 = bf16[2,256,128]{2,1,0:T(8,128)(2,1)} copy-done((bf16[2,256,128]{2,1,0:T(8,128)(2,1)}, bf16[2,256,128]{2,1,0:T(8,128)(2,1)S(1)}, u32[]{:S(2)}) %copy-start.9) | copy-done | bytes 131096
  25.7 1.4 %collective-permute-start.8 = (bf16[2,256,128]{2,1,0:T(8,128)(2,1)S(1)}, bf16[2,256,128]{2,1,0:T(8,128)(2,1)S(1)}, u32[]{:S(2)}, u32[]{:S(2)}) collective-permute-start(bf16[2,256,128]{2,1,0:T(8,128)(2,1)S(1)} %get-tuple-element.45), channel_id=1, source_target_pairs={{0,8},{4,20},{8,0},{12,28},{16,24},{20,4},{24,16},{28,12},{1,9},{5... | collective-permute-start | bytes 393224 | tf_op jit(solution)/shard_map/ppermute | solution.py:259
  27.1 1.5 %collective-permute-start.9 = (bf16[2,256,128]{2,1,0:T(8,128)(2,1)S(1)}, bf16[2,256,128]{2,1,0:T(8,128)(2,1)S(1)}, u32[]{:S(2)}, u32[]{:S(2)}) collective-permute-start(bf16[2,256,128]{2,1,0:T(8,128)(2,1)S(1)} %get-tuple-element.46), channel_id=1, source_target_pairs={{0,16},{4,12},{8,24},{12,4},{16,0},{20,28},{24,8},{28,20},{1,17},{... | collective-permute-start | bytes 393224 | tf_op jit(solution)/shard_map/ppermute | solution.py:259
  28.6 0.9 %collective-permute-done.10.refs_1_ = bf16[2,256,128]{2,1,0:T(8,128)(2,1)S(1)} collective-permute-done((bf16[2,256,128]{2,1,0:T(8,128)(2,1)S(1)}, bf16[2,256,128]{2,1,0:T(8,128)(2,1)S(1)}, u32[]{:S(2)}, u32[]{:S(2)}) %collective-permute-start.10) | collective-permute-done | bytes 131104 | tf_op jit(solution)/shard_map/ppermute | solution.py:259
  29.4 0.7 %copy-done.7 = bf16[2,256,128]{2,1,0:T(8,128)(2,1)} copy-done((bf16[2,256,128]{2,1,0:T(8,128)(2,1)}, bf16[2,256,128]{2,1,0:T(8,128)(2,1)S(1)}, u32[]{:S(2)}) %copy-start.7) | copy-done | bytes 131096
  30.1 2.8 %collective-permute-done.8.refs_0_ = bf16[2,256,128]{2,1,0:T(8,128)(2,1)S(1)} collective-permute-done((bf16[2,256,128]{2,1,0:T(8,128)(2,1)S(1)}, bf16[2,256,128]{2,1,0:T(8,128)(2,1)S(1)}, u32[]{:S(2)}, u32[]{:S(2)}) %collective-permute-start.8) | collective-permute-done | bytes 131104 | tf_op jit(solution)/shard_map/ppermute | solution.py:259
  32.9 0.0 collective-permute-done.9.refs_1_
  32.9 0.4 all-to-all-done.parts_ref
  33.3 0.4 rank_grad.1
  33.7 0.4 collective-permute-start.12
  34.1 0.1 copy-done.10
  34.2 1.8 %collective-permute-start.11 = (bf16[2,256,128]{2,1,0:T(8,128)(2,1)S(1)}, bf16[2,256,128]{2,1,0:T(8,128)(2,1)S(1)}, u32[]{:S(2)}, u32[]{:S(2)}) collective-permute-start(bf16[2,256,128]{2,1,0:T(8,128)(2,1)S(1)} %copy-done.10), channel_id=1, source_target_pairs={{0,24},{4,28},{8,16},{12,20},{16,8},{20,12},{24,0},{28,4},{1,25},{... | collective-permute-start | bytes 393224 | tf_op jit(solution)/shard_map/ppermute | solution.py:259
  36.1 0.0 collective-permute-done.12.other_ref
  36.1 1.2 %collective-permute-start.13 = (bf16[16,2560]{1,0:T(8,128)(2,1)S(1)}, bf16[16,2560]{1,0:T(8,128)(2,1)S(1)}, u32[]{:S(2)}, u32[]{:S(2)}) collective-permute-start(bf16[16,2560]{1,0:T(8,128)(2,1)S(1)} %chip_sum.1.refs_0_), channel_id=1, source_target_pairs={{0,8},{4,20},{8,0},{12,28},{16,24},{20,4},{24,16},{28,12},{1,9},{5... | collective-permute-start | bytes 245768 | tf_op jit(solution)/shard_map/ppermute | solution.py:259
  37.3 0.5 %collective-permute-start.14 = (bf16[16,2560]{1,0:T(8,128)(2,1)S(1)}, bf16[16,2560]{1,0:T(8,128)(2,1)S(1)}, u32[]{:S(2)}, u32[]{:S(2)}) collective-permute-start(bf16[16,2560]{1,0:T(8,128)(2,1)S(1)} %chip_sum.1.refs_0_), channel_id=1, source_target_pairs={{0,16},{4,12},{8,24},{12,4},{16,0},{20,28},{24,8},{28,20},{1,17},{... | collective-permute-start | bytes 245768 | tf_op jit(solution)/shard_map/ppermute | solution.py:259
  37.8 1.8 %collective-permute-start.15 = (bf16[16,2560]{1,0:T(8,128)(2,1)S(1)}, bf16[16,2560]{1,0:T(8,128)(2,1)S(1)}, u32[]{:S(2)}, u32[]{:S(2)}) collective-permute-start(bf16[16,2560]{1,0:T(8,128)(2,1)S(1)} %chip_sum.1.refs_0_), channel_id=1, source_target_pairs={{0,24},{4,28},{8,16},{12,20},{16,8},{20,12},{24,0},{28,4},{1,25},{... | collective-permute-start | bytes 245768 | tf_op jit(solution)/shard_map/ppermute | solution.py:259
  39.6 3.5 %filter_grad.1 = f32[256,1024]{1,0:T(8,128)} custom-call(bf16[16,1024]{1,0:T(8,128)(2,1)S(1)} %get-tuple-element.49.acts_ref, bf16[16,2048]{1,0:T(8,128)(2,1)S(1)} %bitcast.15, bf16[256,2048]{1,0:T(8,128)(2,1)S(1)} %get-tuple-element.50.spec_ref, bf16[1024,2048]{1,0:T(8,128)(2,1)S(1)} %copy-done.1, bf16[2,256,128]{2,1,0:T(8,128)(2,1)S(1)} %get-tuple-element.51.refs_0_, ...), custom_call_target="tpu_custom_call" | custom-call | flops 2147483648 | bytes 1048576 | tf_op jit(solution)/shard_map/filter_grad/pallas_call | solution.py:238
  43.2 0.0 collective-permute-done.11.refs_2_
  43.2 1.1 %input_grad.1 = bf16[2048,128]{1,0:T(8,128)(2,1)} custom-call(bf16[4,256,128]{2,1,0:T(8,128)(2,1)S(1)} %get-tuple-element.38.keep_ref, bf16[4,256,128]{2,1,0:T(8,128)(2,1)S(1)} %collective-permute-done.7.got_ref, bf16[16,2048]{1,0:T(8,128)(2,1)S(1)} %bitcast.13, bf16[16,128]{1,0:T(8,128)(2,1)S(1)} %get-tuple-element.56.rank_ref, ...), custom_call_target="tpu_custom_call" | custom-call | bytes 524288 | tf_op jit(solution)/shard_map/input_grad/pallas_call | solution.py:238
  44.3 0.0 collective-permute-done.13.refs_1_
  44.3 0.0 collective-permute-done.14.refs_2_
  44.3 0.1 collective-permute-done.15.refs_3_
  44.4 0.8 %adapter_sum.1 = (f32[16,1,2048]{2,1,0:T(1,128)}, f32[16,1,2048]{2,1,0:T(1,128)}) custom-call(bf16[16,2560]{1,0:T(8,128)(2,1)S(1)} %chip_sum.1.refs_0_, bf16[16,2560]{1,0:T(8,128)(2,1)S(1)} %collective-permute-done.13.refs_1_, bf16[16,2560]{1,0:T(8,128)(2,1)S(1)} %collective-permute-done.14.refs_2_, bf16[16,2560]{1,0:T(8,128)(2,1)S(1)} %collective-permute-done.15.refs_3_), custom_call_target="tpu_custom_call" | custom-call | bytes 262144 | tf_op jit(solution)/shard_map/adapter_sum/pallas_call | solution.py:238
  (20 shorter events, 0.2 us)
Async XLA Ops:
  0.6 2.3 %collective-permute-start = (bf16[2048,128]{1,0:T(8,128)(2,1)}, bf16[2048,128]{1,0:T(8,128)(2,1)S(1)}, u32[]{:S(2)}, u32[]{:S(2)}) collective-permute-start(bf16[2048,128]{1,0:T(8,128)(2,1)} %bitcast.16), channel_id=1, source_target_pairs={{0,4},{4,0},{8,12},{12,8},{16,20},{20,16},{24,28},{28,24},{1,5},{5... | collective-permute-start | bytes 1572872 | tf_op jit(solution)/shard_map/ppermute | solution.py:250
  1.1 1.8 %copy-start.6 = (bf16[1,2048,128]{2,1,0:T(8,128)(2,1)S(1)}, bf16[1,2048,128]{2,1,0:T(8,128)(2,1)}, u32[]{:S(2)}) copy-start(bf16[1,2048,128]{2,1,0:T(8,128)(2,1)} %param.7) | copy-start | bytes 1572868
  1.2 6.3 %collective-permute-start.4 = (bf16[2048,128]{1,0:T(8,128)(2,1)}, bf16[2048,128]{1,0:T(8,128)(2,1)S(1)}, u32[]{:S(2)}, u32[]{:S(2)}) collective-permute-start(bf16[2048,128]{1,0:T(8,128)(2,1)} %bitcast.7), channel_id=1, source_target_pairs={{0,4},{4,0},{8,12},{12,8},{16,20},{20,16},{24,28},{28,24},{1,5},{5... | collective-permute-start | bytes 1572872 | tf_op jit(solution)/shard_map/ppermute | solution.py:250
  1.2 6.2 %copy-start.2 = (bf16[1,2048,128]{2,1,0:T(8,128)(2,1)S(1)}, bf16[1,2048,128]{2,1,0:T(8,128)(2,1)}, u32[]{:S(2)}) copy-start(bf16[1,2048,128]{2,1,0:T(8,128)(2,1)} %param.6) | copy-start | bytes 1572868
  1.2 9.7 %copy-start.4 = (bf16[16,1,2048]{2,0,1:T(8,128)(2,1)S(1)}, bf16[16,1,2048]{2,0,1:T(8,128)(2,1)}, u32[]{:S(2)}) copy-start(bf16[16,1,2048]{2,0,1:T(8,128)(2,1)} %param.9) | copy-start | bytes 196612
  1.2 9.9 %copy-start.3 = (f32[1,256,1024]{2,1,0:T(8,128)S(1)}, f32[1,256,1024]{2,1,0:T(8,128)}, u32[]{:S(2)}) copy-start(f32[1,256,1024]{2,1,0:T(8,128)} %param.8) | copy-start | bytes 3145732
  2.9 8.2 %copy-start = (bf16[1024,2048]{1,0:T(8,128)(2,1)S(1)}, bf16[1024,2048]{1,0:T(8,128)(2,1)}, u32[]{:S(2)}) copy-start(bf16[1024,2048]{1,0:T(8,128)(2,1)} %constant.2.clone.table_ref) | copy-start | bytes 12582916
  2.9 9.5 %collective-permute-start.1 = (bf16[2,256,128]{2,1,0:T(8,128)(2,1)S(1)}, bf16[2,256,128]{2,1,0:T(8,128)(2,1)S(1)}, u32[]{:S(2)}, u32[]{:S(2)}) collective-permute-start(bf16[2,256,128]{2,1,0:T(8,128)(2,1)S(1)} %get-tuple-element.35), channel_id=1, source_target_pairs={{0,8},{4,20},{8,0},{12,28},{16,24},{20,4},{24,16},{28,12},{1,9},{5... | collective-permute-start | bytes 393224 | tf_op jit(solution)/shard_map/ppermute | solution.py:259
  5.9 6.6 %collective-permute-start.2 = (bf16[2,256,128]{2,1,0:T(8,128)(2,1)S(1)}, bf16[2,256,128]{2,1,0:T(8,128)(2,1)S(1)}, u32[]{:S(2)}, u32[]{:S(2)}) collective-permute-start(bf16[2,256,128]{2,1,0:T(8,128)(2,1)S(1)} %get-tuple-element.36), channel_id=1, source_target_pairs={{0,16},{4,12},{8,24},{12,4},{16,0},{20,28},{24,8},{28,20},{1,17},{... | collective-permute-start | bytes 393224 | tf_op jit(solution)/shard_map/ppermute | solution.py:259
  7.4 7.4 %collective-permute-start.3 = (bf16[2,256,128]{2,1,0:T(8,128)(2,1)S(1)}, bf16[2,256,128]{2,1,0:T(8,128)(2,1)S(1)}, u32[]{:S(2)}, u32[]{:S(2)}) collective-permute-start(bf16[2,256,128]{2,1,0:T(8,128)(2,1)S(1)} %get-tuple-element.37), channel_id=1, source_target_pairs={{0,24},{4,28},{8,16},{12,20},{16,8},{20,12},{24,0},{28,4},{1,25},{... | collective-permute-start | bytes 393224 | tf_op jit(solution)/shard_map/ppermute | solution.py:259
  7.5 7.3 %copy-start.5 = (bf16[16,1,2048]{2,0,1:T(8,128)(2,1)S(1)}, bf16[16,1,2048]{2,0,1:T(8,128)(2,1)}, u32[]{:S(2)}) copy-start(bf16[16,1,2048]{2,0,1:T(8,128)(2,1)} %param.10) | copy-start | bytes 196612
  7.5 10.9 %collective-permute-start.5 = (bf16[2,256,128]{2,1,0:T(8,128)(2,1)S(1)}, bf16[2,256,128]{2,1,0:T(8,128)(2,1)S(1)}, u32[]{:S(2)}, u32[]{:S(2)}) collective-permute-start(bf16[2,256,128]{2,1,0:T(8,128)(2,1)S(1)} %get-tuple-element.41), channel_id=1, source_target_pairs={{0,16},{4,12},{8,24},{12,4},{16,0},{20,28},{24,8},{28,20},{1,17},{... | collective-permute-start | bytes 393224 | tf_op jit(solution)/shard_map/ppermute | solution.py:259
  9.5 8.8 %collective-permute-start.6 = (bf16[2,256,128]{2,1,0:T(8,128)(2,1)S(1)}, bf16[2,256,128]{2,1,0:T(8,128)(2,1)S(1)}, u32[]{:S(2)}, u32[]{:S(2)}) collective-permute-start(bf16[2,256,128]{2,1,0:T(8,128)(2,1)S(1)} %get-tuple-element.42), channel_id=1, source_target_pairs={{0,24},{4,28},{8,16},{12,20},{16,8},{20,12},{24,0},{28,4},{1,25},{... | collective-permute-start | bytes 393224 | tf_op jit(solution)/shard_map/ppermute | solution.py:259
  18.3 15.0 %all-to-all-start = ((bf16[32,32,128]{2,1,0:T(8,128)(2,1)}), bf16[32,32,128]{2,1,0:T(8,128)(2,1)S(1)}, u32[]{:S(2)}, u32[]{:S(2)}) async-start(bf16[32,32,128]{2,1,0:T(8,128)(2,1)} %get-tuple-element.43), calls=%async_computation | async-start | bytes 524288 | tf_op jit(solution)/shard_map/all_to_all | solution.py:286
  23.0 2.0 %collective-permute-start.7 = (bf16[4,256,128]{2,1,0:T(8,128)(2,1)S(1)}, bf16[4,256,128]{2,1,0:T(8,128)(2,1)S(1)}, u32[]{:S(2)}, u32[]{:S(2)}) collective-permute-start(bf16[4,256,128]{2,1,0:T(8,128)(2,1)S(1)} %get-tuple-element.44.give_ref), channel_id=1, source_target_pairs={{0,4},{4,0},{8,12},{12,8},{16,20},{20,16},{24,28},{28,24},{1,5},{5... | collective-permute-start | bytes 786440 | tf_op jit(solution)/shard_map/ppermute | solution.py:250
  23.4 6.1 %collective-permute-start.10 = (bf16[2,256,128]{2,1,0:T(8,128)(2,1)S(1)}, bf16[2,256,128]{2,1,0:T(8,128)(2,1)S(1)}, u32[]{:S(2)}, u32[]{:S(2)}) collective-permute-start(bf16[2,256,128]{2,1,0:T(8,128)(2,1)S(1)} %get-tuple-element.47), channel_id=1, source_target_pairs={{0,8},{4,20},{8,0},{12,28},{16,24},{20,4},{24,16},{28,12},{1,9},{5... | collective-permute-start | bytes 393224 | tf_op jit(solution)/shard_map/ppermute | solution.py:259
  25.1 0.7 %copy-start.9 = (bf16[2,256,128]{2,1,0:T(8,128)(2,1)}, bf16[2,256,128]{2,1,0:T(8,128)(2,1)S(1)}, u32[]{:S(2)}) copy-start(bf16[2,256,128]{2,1,0:T(8,128)(2,1)S(1)} %get-tuple-element.59) | copy-start | bytes 393220
  25.7 7.2 %collective-permute-start.8 = (bf16[2,256,128]{2,1,0:T(8,128)(2,1)S(1)}, bf16[2,256,128]{2,1,0:T(8,128)(2,1)S(1)}, u32[]{:S(2)}, u32[]{:S(2)}) collective-permute-start(bf16[2,256,128]{2,1,0:T(8,128)(2,1)S(1)} %get-tuple-element.45), channel_id=1, source_target_pairs={{0,8},{4,20},{8,0},{12,28},{16,24},{20,4},{24,16},{28,12},{1,9},{5... | collective-permute-start | bytes 393224 | tf_op jit(solution)/shard_map/ppermute | solution.py:259
  27.1 5.8 %collective-permute-start.9 = (bf16[2,256,128]{2,1,0:T(8,128)(2,1)S(1)}, bf16[2,256,128]{2,1,0:T(8,128)(2,1)S(1)}, u32[]{:S(2)}, u32[]{:S(2)}) collective-permute-start(bf16[2,256,128]{2,1,0:T(8,128)(2,1)S(1)} %get-tuple-element.46), channel_id=1, source_target_pairs={{0,16},{4,12},{8,24},{12,4},{16,0},{20,28},{24,8},{28,20},{1,17},{... | collective-permute-start | bytes 393224 | tf_op jit(solution)/shard_map/ppermute | solution.py:259
  29.4 0.7 %copy-start.7 = (bf16[2,256,128]{2,1,0:T(8,128)(2,1)}, bf16[2,256,128]{2,1,0:T(8,128)(2,1)S(1)}, u32[]{:S(2)}) copy-start(bf16[2,256,128]{2,1,0:T(8,128)(2,1)S(1)} %collective-permute-done.10.refs_1_) | copy-start | bytes 393220
  32.9 6.7 %copy-start.8 = (bf16[2,256,128]{2,1,0:T(8,128)(2,1)S(1)}, bf16[2,256,128]{2,1,0:T(8,128)(2,1)}, u32[]{:S(2)}) copy-start(bf16[2,256,128]{2,1,0:T(8,128)(2,1)} %copy-done.7) | copy-start | bytes 393220
  33.3 0.9 %copy-start.10 = (bf16[2,256,128]{2,1,0:T(8,128)(2,1)S(1)}, bf16[2,256,128]{2,1,0:T(8,128)(2,1)}, u32[]{:S(2)}) copy-start(bf16[2,256,128]{2,1,0:T(8,128)(2,1)} %copy-done.9) | copy-start | bytes 393220
  33.3 6.3 %copy-start.1 = (bf16[1024,2048]{1,0:T(8,128)(2,1)S(1)}, bf16[1024,2048]{1,0:T(8,128)(2,1)}, u32[]{:S(2)}) copy-start(bf16[1024,2048]{1,0:T(8,128)(2,1)} %constant.2.clone.table_ref) | copy-start | bytes 12582916
  33.7 2.4 %collective-permute-start.12 = (f32[16,2304]{1,0:T(8,128)S(1)}, f32[16,2304]{1,0:T(8,128)S(1)}, u32[]{:S(2)}, u32[]{:S(2)}) collective-permute-start(f32[16,2304]{1,0:T(8,128)S(1)} %get-tuple-element.61.own_ref), channel_id=1, source_target_pairs={{0,4},{4,0},{8,12},{12,8},{16,20},{20,16},{24,28},{28,24},{1,5},{5... | collective-permute-start | bytes 442376 | tf_op jit(solution)/shard_map/ppermute | solution.py:250
  34.2 9.0 %collective-permute-start.11 = (bf16[2,256,128]{2,1,0:T(8,128)(2,1)S(1)}, bf16[2,256,128]{2,1,0:T(8,128)(2,1)S(1)}, u32[]{:S(2)}, u32[]{:S(2)}) collective-permute-start(bf16[2,256,128]{2,1,0:T(8,128)(2,1)S(1)} %copy-done.10), channel_id=1, source_target_pairs={{0,24},{4,28},{8,16},{12,20},{16,8},{20,12},{24,0},{28,4},{1,25},{... | collective-permute-start | bytes 393224 | tf_op jit(solution)/shard_map/ppermute | solution.py:259
  36.1 8.3 %collective-permute-start.13 = (bf16[16,2560]{1,0:T(8,128)(2,1)S(1)}, bf16[16,2560]{1,0:T(8,128)(2,1)S(1)}, u32[]{:S(2)}, u32[]{:S(2)}) collective-permute-start(bf16[16,2560]{1,0:T(8,128)(2,1)S(1)} %chip_sum.1.refs_0_), channel_id=1, source_target_pairs={{0,8},{4,20},{8,0},{12,28},{16,24},{20,4},{24,16},{28,12},{1,9},{5... | collective-permute-start | bytes 245768 | tf_op jit(solution)/shard_map/ppermute | solution.py:259
  37.3 7.1 %collective-permute-start.14 = (bf16[16,2560]{1,0:T(8,128)(2,1)S(1)}, bf16[16,2560]{1,0:T(8,128)(2,1)S(1)}, u32[]{:S(2)}, u32[]{:S(2)}) collective-permute-start(bf16[16,2560]{1,0:T(8,128)(2,1)S(1)} %chip_sum.1.refs_0_), channel_id=1, source_target_pairs={{0,16},{4,12},{8,24},{12,4},{16,0},{20,28},{24,8},{28,20},{1,17},{... | collective-permute-start | bytes 245768 | tf_op jit(solution)/shard_map/ppermute | solution.py:259
  37.8 6.6 %collective-permute-start.15 = (bf16[16,2560]{1,0:T(8,128)(2,1)S(1)}, bf16[16,2560]{1,0:T(8,128)(2,1)S(1)}, u32[]{:S(2)}, u32[]{:S(2)}) collective-permute-start(bf16[16,2560]{1,0:T(8,128)(2,1)S(1)} %chip_sum.1.refs_0_), channel_id=1, source_target_pairs={{0,24},{4,28},{8,16},{12,20},{16,8},{20,12},{24,0},{28,4},{1,25},{... | collective-permute-start | bytes 245768 | tf_op jit(solution)/shard_map/ppermute | solution.py:259

commit v6 on v5

--- a/solution.py
+++ b/solution.py
@@ -101,7 +101,7 @@
 
 
 def grad_u_kernel(groups, filt_spec_ref, up_ref, acts_ref, table_ref, *refs):
-    pack_refs, (spec_ref, keep_ref, give_ref, rank_ref, signal, cross, du) = refs[:-7], refs[-7:]
+    pack_refs, (spec_ref, keep_ref, give_ref, rank_out, signal, cross, du, rank_ref, sems) = refs[:-9], refs[-9:]
     length = table_ref.shape[0]
     chips = len(pack_refs)
     _, chans, tokens = pack_refs[0].shape
@@ -118,9 +118,12 @@
         for j in range(groups):
             rank_ref[i * groups + j, : rank.shape[0]] = rank[:, i * tokens : (i + 1) * tokens]
             rank_ref[i * groups + j, rank.shape[0] :] = acts_ref[...]
+    copy = pltpu.make_async_copy(rank_ref, rank_out, sems.at[0])
+    copy.start()
     for i in range(chips):
         for j, out_ref in enumerate((keep_ref, give_ref)):
             out_ref[i] = du[:, part(own_index(chip_offset(i, j) ^ j), tokens)]
+    copy.wait()
 
 
 def pairwise(values):
@@ -207,14 +210,11 @@
     width = down_out.shape[2]
     chans = (part_refs[0].shape[1] - width) // 2
     sums = [ref[:, :width].astype(F32) for ref in part_refs]
-    if len(sums) > 2:
-        odd = jnp.bitwise_and(lax.axis_index("ctx"), 1) == 1
-        sums[1:3] = [jnp.where(odd, sums[2], sums[1]), jnp.where(odd, sums[1], sums[2])]
     down_out[:, 0, :] = pairwise(sums)
     for i, ref in enumerate(part_refs):
         for j in range(2):
             block = ref[:, width + j * chans : width + (j + 1) * chans]
-            chunks[:, part(own_index(chip_offset(i) ^ j), chans)] = block.astype(F32)
+            chunks[:, part(own_index(2 * i + j), chans)] = block.astype(F32)
     up_out[:, 0, :] = chunks[...]
 
 
@@ -230,11 +230,11 @@
     local = pl.BlockSpec(memory_space=pltpu.VMEM)
     product = 2 * chans * length * 2 * length
 
-    def call(kernel, name, out_shape, args, scratch=(), flops=0, early=0, far_out=False):
+    def call(kernel, name, out_shape, args, scratch=(), flops=0, early=0, far_out=()):
         outs = jax.tree.leaves(out_shape)
         moved = sum(int(np.prod(o.shape)) * o.dtype.itemsize for o in outs)
-        out_spec = pl.BlockSpec(memory_space=pl.ANY) if far_out else local
-        out_specs = (out_spec,) * len(outs) if isinstance(out_shape, tuple) else out_spec
+        out_specs = tuple(pl.BlockSpec(memory_space=pl.ANY) if i in far_out else local for i in range(len(outs)))
+        out_specs = out_specs if isinstance(out_shape, tuple) else out_specs[0]
         return pl.pallas_call(
             kernel,
             out_shape=out_shape,
@@ -278,7 +278,14 @@
         "grad_u",
         (shape((chans, 2 * length), BF16), half_du, half_du, shape((everyone, 2 * rank, tokens), BF16)),
         (filt_spec, up, acts_part, table, *chan_grad),
-        scratch=[vmem((chans, length), BF16), vmem((chans, 2 * length), BF16), vmem((chans, length), BF16)],
+        scratch=[
+            vmem((chans, length), BF16),
+            vmem((chans, 2 * length), BF16),
+            vmem((chans, length), BF16),
+            vmem((everyone, 2 * rank, tokens), BF16),
+            pltpu.SemaphoreType.DMA((1,)),
+        ],
+        far_out=(3,),
     )
     chan_packs = to_chips(packed(tok_input, sibling_input, "input_pack"))
     late_pack = chan_packs.pop(1)
@@ -303,7 +310,7 @@
         shape((rank, width + 2 * chans), BF16),
         (adapter_part, other_part),
     )
-    chip_parts = to_chips([chip_part] * chips)
+    chip_parts = [chip_part] + [send(chip_part, 2 * i) for i in range(1, chips)]
     filt_grad = call(
         filter_grad_kernel,
         "filter_grad",
@@ -316,7 +323,7 @@
             pltpu.SemaphoreType.DMA((2,)),
         ],
         flops=2 * product,
-        far_out=True,
+        far_out=(0,),
     )
     filt_grad, got = lax.optimization_barrier((filt_grad, got))
     grad_input = call(

time: 45.4 us -> 45.4 us (level)
    ppermute x12 -> x9, starting transfers between devices: 17.8 us -> 14.3 us  [to_chip(): return lax.ppermute(value, 'ctx', pairs)]
    ppermute x4 -> x7, starting transfers between devices: 1.29 us -> 4.84 us  [send(): lax.ppermute(value, axis, [(i, i ^ offset) for i in range(mesh.shape[axis...]
    ppermute x12 -> x9, waiting for transfers between devices: 6.12 us -> 6.06 us  [to_chip(): return lax.ppermute(value, 'ctx', pairs)]
    ppermute x4 -> x7, waiting for transfers between devices: 1.66 us -> 1.68 us  [send(): lax.ppermute(value, axis, [(i, i ^ offset) for i in range(mesh.shape[axis...]
  transfers between devices with their start and end apart: 17 -> 17, of which waited for: 6 -> 5; matrix products, arithmetic and copies ran while one was open for 0% -> 0% of each run, Pallas kernels for 22% -> 22%
where the time goes in v6:
time: 45.4 us; the launch traced here: 45.1 us
  starting transfers between devices  23.8 us (52%)
  Pallas kernels  11 us (24%)
  waiting for transfers between devices  8.11 us (18%)
  local copies, waits for them, and re-layouts  1.49 us (3%)
  between operations  0.77 us (2%)
    ppermute x9, starting transfers between devices, to_chip(): return lax.ppermute(value, 'ctx', pairs)  14.3 us
    pallas_call x12, Pallas kernels, call(): pl.pallas_call(kernel, out_shape=out_shape, in_specs=[local] * (len(args)...  11 us
    ppermute x9, waiting for transfers between devices, to_chip(): return lax.ppermute(value, 'ctx', pairs)  6.06 us
    ppermute x7, starting transfers between devices, send(): lax.ppermute(value, axis, [(i, i ^ offset) for i in range(mesh.shape[axis...  4.84 us
    all_to_all x1, starting transfers between devices, dense_body(): all_parts = lax.all_to_all(rank_parts, ('ctx', 'grp'), 0, 0, tiled=True)  4.67 us
    ppermute x7, waiting for transfers between devices, send(): lax.ppermute(value, axis, [(i, i ^ offset) for i in range(mesh.shape[axis...  1.68 us
    unnamed x22, local copies, waits for them, and re-layouts  1.49 us
  transfers between devices with their start and end apart: 17, of which 5 were waited for; matrix products, arithmetic and copies ran while one was open for 0% of the time, Pallas kernels for 22%

profile of v6, /device:TPU:0, one launch (start us, length us, event | category | flops | bytes accessed | tf_op | source)
XLA Modules:
  0.0 45.1 jit_solution(11901629328399917552)
XLA Ops:
  0.6 0.5 %collective-permute-start = (bf16[2048,128]{1,0:T(8,128)(2,1)}, bf16[2048,128]{1,0:T(8,128)(2,1)S(1)}, u32[]{:S(2)}, u32[]{:S(2)}) collective-permute-start(bf16[2048,128]{1,0:T(8,128)(2,1)} %bitcast.16), channel_id=1, source_target_pairs={{0,4},{4,0},{8,12},{12,8},{16,20},{20,16},{24,28},{28,24},{1,5},{5... | collective-permute-start | bytes 1572872 | tf_op jit(solution)/shard_map/ppermute | solution.py:250
  1.2 0.1 collective-permute-start.4
  1.2 1.6 %collective-permute-done.sibling_ref = bf16[2048,128]{1,0:T(8,128)(2,1)S(1)} collective-permute-done((bf16[2048,128]{1,0:T(8,128)(2,1)}, bf16[2048,128]{1,0:T(8,128)(2,1)S(1)}, u32[]{:S(2)}, u32[]{:S(2)}) %collective-permute-start) | collective-permute-done | bytes 524320 | tf_op jit(solution)/shard_map/ppermute | solution.py:250
  2.9 0.0 copy-done.6
  2.9 2.9 %collective-permute-start.1 = (bf16[2,256,128]{2,1,0:T(8,128)(2,1)S(1)}, bf16[2,256,128]{2,1,0:T(8,128)(2,1)S(1)}, u32[]{:S(2)}, u32[]{:S(2)}) collective-permute-start(bf16[2,256,128]{2,1,0:T(8,128)(2,1)S(1)} %get-tuple-element.35), channel_id=1, source_target_pairs={{0,8},{4,20},{8,0},{12,28},{16,24},{20,4},{24,16},{28,12},{1,9},{5... | collective-permute-start | bytes 393224 | tf_op jit(solution)/shard_map/ppermute | solution.py:259
  5.9 1.5 %collective-permute-start.2 = (bf16[2,256,128]{2,1,0:T(8,128)(2,1)S(1)}, bf16[2,256,128]{2,1,0:T(8,128)(2,1)S(1)}, u32[]{:S(2)}, u32[]{:S(2)}) collective-permute-start(bf16[2,256,128]{2,1,0:T(8,128)(2,1)S(1)} %get-tuple-element.36), channel_id=1, source_target_pairs={{0,16},{4,12},{8,24},{12,4},{16,0},{20,28},{24,8},{28,20},{1,17},{... | collective-permute-start | bytes 393224 | tf_op jit(solution)/shard_map/ppermute | solution.py:259
  7.4 0.0 collective-permute-start.3
  7.4 0.0 collective-permute-done.4.sibling_ref
  7.5 0.0 copy-start.5
  7.5 2.0 %collective-permute-start.5 = (bf16[2,256,128]{2,1,0:T(8,128)(2,1)S(1)}, bf16[2,256,128]{2,1,0:T(8,128)(2,1)S(1)}, u32[]{:S(2)}, u32[]{:S(2)}) collective-permute-start(bf16[2,256,128]{2,1,0:T(8,128)(2,1)S(1)} %get-tuple-element.41), channel_id=1, source_target_pairs={{0,16},{4,12},{8,24},{12,4},{16,0},{20,28},{24,8},{28,20},{1,17},{... | collective-permute-start | bytes 393224 | tf_op jit(solution)/shard_map/ppermute | solution.py:259
  9.5 1.4 %collective-permute-start.6 = (bf16[2,256,128]{2,1,0:T(8,128)(2,1)S(1)}, bf16[2,256,128]{2,1,0:T(8,128)(2,1)S(1)}, u32[]{:S(2)}, u32[]{:S(2)}) collective-permute-start(bf16[2,256,128]{2,1,0:T(8,128)(2,1)S(1)} %get-tuple-element.42), channel_id=1, source_target_pairs={{0,24},{4,28},{8,16},{12,20},{16,8},{20,12},{24,0},{28,4},{1,25},{... | collective-permute-start | bytes 393224 | tf_op jit(solution)/shard_map/ppermute | solution.py:259
  10.9 0.2 rank_acts.1.acts_ref
  11.1 0.0 copy-done
  11.1 1.3 %filter_spec.1.filt_spec_ref = f32[256,2048]{1,0:T(8,128)S(1)} custom-call(f32[256,1024]{1,0:T(8,128)S(1)} %bitcast.11, bf16[1024,2048]{1,0:T(8,128)(2,1)S(1)} %copy-done), custom_call_target="tpu_custom_call" | custom-call | flops 1073741824 | bytes 2097152 | tf_op jit(solution)/shard_map/filter_spec/pallas_call | solution.py:238
  12.4 0.0 collective-permute-done.1.refs_1_
  12.4 0.0 collective-permute-done.2.refs_2_
  12.4 2.3 %collective-permute-done.3.refs_3_ = bf16[2,256,128]{2,1,0:T(8,128)(2,1)S(1)} collective-permute-done((bf16[2,256,128]{2,1,0:T(8,128)(2,1)S(1)}, bf16[2,256,128]{2,1,0:T(8,128)(2,1)S(1)}, u32[]{:S(2)}, u32[]{:S(2)}) %collective-permute-start.3) | collective-permute-done | bytes 131104 | tf_op jit(solution)/shard_map/ppermute | solution.py:259
  14.8 3.6 %grad_u.1 = (bf16[256,2048]{1,0:T(8,128)(2,1)S(1)}, bf16[4,256,128]{2,1,0:T(8,128)(2,1)S(1)}, bf16[4,256,128]{2,1,0:T(8,128)(2,1)S(1)}, bf16[32,32,128]{2,1,0:T(8,128)(2,1)}) custom-call(f32[256,2048]{1,0:T(8,128)S(1)} %filter_spec.1.filt_spec_ref, bf16[16,2048]{1,0:T(8,128)(2,1)S(1)} %bitcast.14, bf16[16,128]{1,0:T(8,128)(2,1)S(1)} %rank_acts.1.acts_ref, ...), custom_call_target="tpu_custom_call" | custom-call | bytes 1835008 | tf_op jit(solution)/shard_map/grad_u/pallas_call | solution.py:238
  18.4 0.0 collective-permute-done.5.refs_2_
  18.4 0.0 collective-permute-done.6.refs_3_
  18.4 4.7 %all-to-all-start = ((bf16[32,32,128]{2,1,0:T(8,128)(2,1)}), bf16[32,32,128]{2,1,0:T(8,128)(2,1)S(1)}, u32[]{:S(2)}, u32[]{:S(2)}) async-start(bf16[32,32,128]{2,1,0:T(8,128)(2,1)} %get-tuple-element.43), calls=%async_computation | async-start | bytes 524288 | tf_op jit(solution)/shard_map/all_to_all | solution.py:293
  23.1 0.3 collective-permute-start.7
  23.4 1.7 %collective-permute-start.10 = (bf16[2,256,128]{2,1,0:T(8,128)(2,1)S(1)}, bf16[2,256,128]{2,1,0:T(8,128)(2,1)S(1)}, u32[]{:S(2)}, u32[]{:S(2)}) collective-permute-start(bf16[2,256,128]{2,1,0:T(8,128)(2,1)S(1)} %get-tuple-element.47), channel_id=1, source_target_pairs={{0,8},{4,20},{8,0},{12,28},{16,24},{20,4},{24,16},{28,12},{1,9},{5... | collective-permute-start | bytes 393224 | tf_op jit(solution)/shard_map/ppermute | solution.py:259
  25.0 0.0 collective-permute-done.7.got_ref
  25.1 0.0 copy-start.9
  25.1 0.6 %copy-done.9 = bf16[2,256,128]{2,1,0:T(8,128)(2,1)} copy-done((bf16[2,256,128]{2,1,0:T(8,128)(2,1)}, bf16[2,256,128]{2,1,0:T(8,128)(2,1)S(1)}, u32[]{:S(2)}) %copy-start.9) | copy-done | bytes 131096
  25.7 1.4 %collective-permute-start.8 = (bf16[2,256,128]{2,1,0:T(8,128)(2,1)S(1)}, bf16[2,256,128]{2,1,0:T(8,128)(2,1)S(1)}, u32[]{:S(2)}, u32[]{:S(2)}) collective-permute-start(bf16[2,256,128]{2,1,0:T(8,128)(2,1)S(1)} %get-tuple-element.45), channel_id=1, source_target_pairs={{0,8},{4,20},{8,0},{12,28},{16,24},{20,4},{24,16},{28,12},{1,9},{5... | collective-permute-start | bytes 393224 | tf_op jit(solution)/shard_map/ppermute | solution.py:259
  27.1 1.5 %collective-permute-start.9 = (bf16[2,256,128]{2,1,0:T(8,128)(2,1)S(1)}, bf16[2,256,128]{2,1,0:T(8,128)(2,1)S(1)}, u32[]{:S(2)}, u32[]{:S(2)}) collective-permute-start(bf16[2,256,128]{2,1,0:T(8,128)(2,1)S(1)} %get-tuple-element.46), channel_id=1, source_target_pairs={{0,16},{4,12},{8,24},{12,4},{16,0},{20,28},{24,8},{28,20},{1,17},{... | collective-permute-start | bytes 393224 | tf_op jit(solution)/shard_map/ppermute | solution.py:259
  28.6 0.9 %collective-permute-done.10.refs_1_ = bf16[2,256,128]{2,1,0:T(8,128)(2,1)S(1)} collective-permute-done((bf16[2,256,128]{2,1,0:T(8,128)(2,1)S(1)}, bf16[2,256,128]{2,1,0:T(8,128)(2,1)S(1)}, u32[]{:S(2)}, u32[]{:S(2)}) %collective-permute-start.10) | collective-permute-done | bytes 131104 | tf_op jit(solution)/shard_map/ppermute | solution.py:259
  29.5 0.7 %copy-done.7 = bf16[2,256,128]{2,1,0:T(8,128)(2,1)} copy-done((bf16[2,256,128]{2,1,0:T(8,128)(2,1)}, bf16[2,256,128]{2,1,0:T(8,128)(2,1)S(1)}, u32[]{:S(2)}) %copy-start.7) | copy-done | bytes 131096
  30.1 2.8 %collective-permute-done.8.refs_0_ = bf16[2,256,128]{2,1,0:T(8,128)(2,1)S(1)} collective-permute-done((bf16[2,256,128]{2,1,0:T(8,128)(2,1)S(1)}, bf16[2,256,128]{2,1,0:T(8,128)(2,1)S(1)}, u32[]{:S(2)}, u32[]{:S(2)}) %collective-permute-start.8) | collective-permute-done | bytes 131104 | tf_op jit(solution)/shard_map/ppermute | solution.py:259
  32.9 0.0 collective-permute-done.9.refs_1_
  33.0 0.4 all-to-all-done.parts_ref
  33.3 0.4 rank_grad.1
  33.7 0.4 collective-permute-start.12
  34.1 0.1 copy-done.10
  34.2 1.8 %collective-permute-start.11 = (bf16[2,256,128]{2,1,0:T(8,128)(2,1)S(1)}, bf16[2,256,128]{2,1,0:T(8,128)(2,1)S(1)}, u32[]{:S(2)}, u32[]{:S(2)}) collective-permute-start(bf16[2,256,128]{2,1,0:T(8,128)(2,1)S(1)} %copy-done.10), channel_id=1, source_target_pairs={{0,24},{4,28},{8,16},{12,20},{16,8},{20,12},{24,0},{28,4},{1,25},{... | collective-permute-start | bytes 393224 | tf_op jit(solution)/shard_map/ppermute | solution.py:259
  36.1 0.0 collective-permute-done.12.other_ref
  36.1 1.2 %collective-permute-start.13 = (bf16[16,2560]{1,0:T(8,128)(2,1)S(1)}, bf16[16,2560]{1,0:T(8,128)(2,1)S(1)}, u32[]{:S(2)}, u32[]{:S(2)}) collective-permute-start(bf16[16,2560]{1,0:T(8,128)(2,1)S(1)} %chip_sum.1.refs_0_), channel_id=1, source_target_pairs={{0,8},{4,12},{8,0},{12,4},{16,24},{20,28},{24,16},{28,20},{1,9},{5... | collective-permute-start | bytes 245768 | tf_op jit(solution)/shard_map/ppermute | solution.py:250
  37.3 0.5 %collective-permute-start.14 = (bf16[16,2560]{1,0:T(8,128)(2,1)S(1)}, bf16[16,2560]{1,0:T(8,128)(2,1)S(1)}, u32[]{:S(2)}, u32[]{:S(2)}) collective-permute-start(bf16[16,2560]{1,0:T(8,128)(2,1)S(1)} %chip_sum.1.refs_0_), channel_id=1, source_target_pairs={{0,16},{4,20},{8,24},{12,28},{16,0},{20,4},{24,8},{28,12},{1,17},{... | collective-permute-start | bytes 245768 | tf_op jit(solution)/shard_map/ppermute | solution.py:250
  37.8 1.8 %collective-permute-start.15 = (bf16[16,2560]{1,0:T(8,128)(2,1)S(1)}, bf16[16,2560]{1,0:T(8,128)(2,1)S(1)}, u32[]{:S(2)}, u32[]{:S(2)}) collective-permute-start(bf16[16,2560]{1,0:T(8,128)(2,1)S(1)} %chip_sum.1.refs_0_), channel_id=1, source_target_pairs={{0,24},{4,28},{8,16},{12,20},{16,8},{20,12},{24,0},{28,4},{1,25},{... | collective-permute-start | bytes 245768 | tf_op jit(solution)/shard_map/ppermute | solution.py:250
  39.7 3.5 %filter_grad.1 = f32[256,1024]{1,0:T(8,128)} custom-call(bf16[16,1024]{1,0:T(8,128)(2,1)S(1)} %get-tuple-element.49.acts_ref, bf16[16,2048]{1,0:T(8,128)(2,1)S(1)} %bitcast.15, bf16[256,2048]{1,0:T(8,128)(2,1)S(1)} %get-tuple-element.50.spec_ref, bf16[1024,2048]{1,0:T(8,128)(2,1)S(1)} %copy-done.1, bf16[2,256,128]{2,1,0:T(8,128)(2,1)S(1)} %get-tuple-element.51.refs_0_, ...), custom_call_target="tpu_custom_call" | custom-call | flops 2147483648 | bytes 1048576 | tf_op jit(solution)/shard_map/filter_grad/pallas_call | solution.py:238
  43.2 0.0 collective-permute-done.11.refs_2_
  43.2 1.1 %input_grad.1 = bf16[2048,128]{1,0:T(8,128)(2,1)} custom-call(bf16[4,256,128]{2,1,0:T(8,128)(2,1)S(1)} %get-tuple-element.38.keep_ref, bf16[4,256,128]{2,1,0:T(8,128)(2,1)S(1)} %collective-permute-done.7.got_ref, bf16[16,2048]{1,0:T(8,128)(2,1)S(1)} %bitcast.13, bf16[16,128]{1,0:T(8,128)(2,1)S(1)} %get-tuple-element.56.rank_ref, ...), custom_call_target="tpu_custom_call" | custom-call | bytes 524288 | tf_op jit(solution)/shard_map/input_grad/pallas_call | solution.py:238
  44.3 0.0 collective-permute-done.13.refs_1_
  44.3 0.0 collective-permute-done.14.refs_2_
  44.4 0.0 collective-permute-done.15.refs_3_
  44.4 0.8 %adapter_sum.1 = (f32[16,1,2048]{2,1,0:T(1,128)}, f32[16,1,2048]{2,1,0:T(1,128)}) custom-call(bf16[16,2560]{1,0:T(8,128)(2,1)S(1)} %chip_sum.1.refs_0_, bf16[16,2560]{1,0:T(8,128)(2,1)S(1)} %collective-permute-done.13.refs_1_, bf16[16,2560]{1,0:T(8,128)(2,1)S(1)} %collective-permute-done.14.refs_2_, bf16[16,2560]{1,0:T(8,128)(2,1)S(1)} %collective-permute-done.15.refs_3_), custom_call_target="tpu_custom_call" | custom-call | bytes 262144 | tf_op jit(solution)/shard_map/adapter_sum/pallas_call | solution.py:238
  (20 shorter events, 0.2 us)
Async XLA Ops:
  0.6 2.3 %collective-permute-start = (bf16[2048,128]{1,0:T(8,128)(2,1)}, bf16[2048,128]{1,0:T(8,128)(2,1)S(1)}, u32[]{:S(2)}, u32[]{:S(2)}) collective-permute-start(bf16[2048,128]{1,0:T(8,128)(2,1)} %bitcast.16), channel_id=1, source_target_pairs={{0,4},{4,0},{8,12},{12,8},{16,20},{20,16},{24,28},{28,24},{1,5},{5... | collective-permute-start | bytes 1572872 | tf_op jit(solution)/shard_map/ppermute | solution.py:250
  1.1 1.8 %copy-start.6 = (bf16[1,2048,128]{2,1,0:T(8,128)(2,1)S(1)}, bf16[1,2048,128]{2,1,0:T(8,128)(2,1)}, u32[]{:S(2)}) copy-start(bf16[1,2048,128]{2,1,0:T(8,128)(2,1)} %param.7) | copy-start | bytes 1572868
  1.2 6.3 %collective-permute-start.4 = (bf16[2048,128]{1,0:T(8,128)(2,1)}, bf16[2048,128]{1,0:T(8,128)(2,1)S(1)}, u32[]{:S(2)}, u32[]{:S(2)}) collective-permute-start(bf16[2048,128]{1,0:T(8,128)(2,1)} %bitcast.7), channel_id=1, source_target_pairs={{0,4},{4,0},{8,12},{12,8},{16,20},{20,16},{24,28},{28,24},{1,5},{5... | collective-permute-start | bytes 1572872 | tf_op jit(solution)/shard_map/ppermute | solution.py:250
  1.2 6.2 %copy-start.2 = (bf16[1,2048,128]{2,1,0:T(8,128)(2,1)S(1)}, bf16[1,2048,128]{2,1,0:T(8,128)(2,1)}, u32[]{:S(2)}) copy-start(bf16[1,2048,128]{2,1,0:T(8,128)(2,1)} %param.6) | copy-start | bytes 1572868
  1.2 9.7 %copy-start.4 = (bf16[16,1,2048]{2,0,1:T(8,128)(2,1)S(1)}, bf16[16,1,2048]{2,0,1:T(8,128)(2,1)}, u32[]{:S(2)}) copy-start(bf16[16,1,2048]{2,0,1:T(8,128)(2,1)} %param.9) | copy-start | bytes 196612
  1.2 9.9 %copy-start.3 = (f32[1,256,1024]{2,1,0:T(8,128)S(1)}, f32[1,256,1024]{2,1,0:T(8,128)}, u32[]{:S(2)}) copy-start(f32[1,256,1024]{2,1,0:T(8,128)} %param.8) | copy-start | bytes 3145732
  2.9 8.2 %copy-start = (bf16[1024,2048]{1,0:T(8,128)(2,1)S(1)}, bf16[1024,2048]{1,0:T(8,128)(2,1)}, u32[]{:S(2)}) copy-start(bf16[1024,2048]{1,0:T(8,128)(2,1)} %constant.2.clone.table_ref) | copy-start | bytes 12582916
  2.9 9.5 %collective-permute-start.1 = (bf16[2,256,128]{2,1,0:T(8,128)(2,1)S(1)}, bf16[2,256,128]{2,1,0:T(8,128)(2,1)S(1)}, u32[]{:S(2)}, u32[]{:S(2)}) collective-permute-start(bf16[2,256,128]{2,1,0:T(8,128)(2,1)S(1)} %get-tuple-element.35), channel_id=1, source_target_pairs={{0,8},{4,20},{8,0},{12,28},{16,24},{20,4},{24,16},{28,12},{1,9},{5... | collective-permute-start | bytes 393224 | tf_op jit(solution)/shard_map/ppermute | solution.py:259
  5.9 6.6 %collective-permute-start.2 = (bf16[2,256,128]{2,1,0:T(8,128)(2,1)S(1)}, bf16[2,256,128]{2,1,0:T(8,128)(2,1)S(1)}, u32[]{:S(2)}, u32[]{:S(2)}) collective-permute-start(bf16[2,256,128]{2,1,0:T(8,128)(2,1)S(1)} %get-tuple-element.36), channel_id=1, source_target_pairs={{0,16},{4,12},{8,24},{12,4},{16,0},{20,28},{24,8},{28,20},{1,17},{... | collective-permute-start | bytes 393224 | tf_op jit(solution)/shard_map/ppermute | solution.py:259
  7.4 7.4 %collective-permute-start.3 = (bf16[2,256,128]{2,1,0:T(8,128)(2,1)S(1)}, bf16[2,256,128]{2,1,0:T(8,128)(2,1)S(1)}, u32[]{:S(2)}, u32[]{:S(2)}) collective-permute-start(bf16[2,256,128]{2,1,0:T(8,128)(2,1)S(1)} %get-tuple-element.37), channel_id=1, source_target_pairs={{0,24},{4,28},{8,16},{12,20},{16,8},{20,12},{24,0},{28,4},{1,25},{... | collective-permute-start | bytes 393224 | tf_op jit(solution)/shard_map/ppermute | solution.py:259
  7.5 7.3 %copy-start.5 = (bf16[16,1,2048]{2,0,1:T(8,128)(2,1)S(1)}, bf16[16,1,2048]{2,0,1:T(8,128)(2,1)}, u32[]{:S(2)}) copy-start(bf16[16,1,2048]{2,0,1:T(8,128)(2,1)} %param.10) | copy-start | bytes 196612
  7.5 10.9 %collective-permute-start.5 = (bf16[2,256,128]{2,1,0:T(8,128)(2,1)S(1)}, bf16[2,256,128]{2,1,0:T(8,128)(2,1)S(1)}, u32[]{:S(2)}, u32[]{:S(2)}) collective-permute-start(bf16[2,256,128]{2,1,0:T(8,128)(2,1)S(1)} %get-tuple-element.41), channel_id=1, source_target_pairs={{0,16},{4,12},{8,24},{12,4},{16,0},{20,28},{24,8},{28,20},{1,17},{... | collective-permute-start | bytes 393224 | tf_op jit(solution)/shard_map/ppermute | solution.py:259
  9.5 8.9 %collective-permute-start.6 = (bf16[2,256,128]{2,1,0:T(8,128)(2,1)S(1)}, bf16[2,256,128]{2,1,0:T(8,128)(2,1)S(1)}, u32[]{:S(2)}, u32[]{:S(2)}) collective-permute-start(bf16[2,256,128]{2,1,0:T(8,128)(2,1)S(1)} %get-tuple-element.42), channel_id=1, source_target_pairs={{0,24},{4,28},{8,16},{12,20},{16,8},{20,12},{24,0},{28,4},{1,25},{... | collective-permute-start | bytes 393224 | tf_op jit(solution)/shard_map/ppermute | solution.py:259
  18.4 14.9 %all-to-all-start = ((bf16[32,32,128]{2,1,0:T(8,128)(2,1)}), bf16[32,32,128]{2,1,0:T(8,128)(2,1)S(1)}, u32[]{:S(2)}, u32[]{:S(2)}) async-start(bf16[32,32,128]{2,1,0:T(8,128)(2,1)} %get-tuple-element.43), calls=%async_computation | async-start | bytes 524288 | tf_op jit(solution)/shard_map/all_to_all | solution.py:293
  23.1 2.0 %collective-permute-start.7 = (bf16[4,256,128]{2,1,0:T(8,128)(2,1)S(1)}, bf16[4,256,128]{2,1,0:T(8,128)(2,1)S(1)}, u32[]{:S(2)}, u32[]{:S(2)}) collective-permute-start(bf16[4,256,128]{2,1,0:T(8,128)(2,1)S(1)} %get-tuple-element.44.give_ref), channel_id=1, source_target_pairs={{0,4},{4,0},{8,12},{12,8},{16,20},{20,16},{24,28},{28,24},{1,5},{5... | collective-permute-start | bytes 786440 | tf_op jit(solution)/shard_map/ppermute | solution.py:250
  23.4 6.1 %collective-permute-start.10 = (bf16[2,256,128]{2,1,0:T(8,128)(2,1)S(1)}, bf16[2,256,128]{2,1,0:T(8,128)(2,1)S(1)}, u32[]{:S(2)}, u32[]{:S(2)}) collective-permute-start(bf16[2,256,128]{2,1,0:T(8,128)(2,1)S(1)} %get-tuple-element.47), channel_id=1, source_target_pairs={{0,8},{4,20},{8,0},{12,28},{16,24},{20,4},{24,16},{28,12},{1,9},{5... | collective-permute-start | bytes 393224 | tf_op jit(solution)/shard_map/ppermute | solution.py:259
  25.1 0.7 %copy-start.9 = (bf16[2,256,128]{2,1,0:T(8,128)(2,1)}, bf16[2,256,128]{2,1,0:T(8,128)(2,1)S(1)}, u32[]{:S(2)}) copy-start(bf16[2,256,128]{2,1,0:T(8,128)(2,1)S(1)} %get-tuple-element.59) | copy-start | bytes 393220
  25.7 7.2 %collective-permute-start.8 = (bf16[2,256,128]{2,1,0:T(8,128)(2,1)S(1)}, bf16[2,256,128]{2,1,0:T(8,128)(2,1)S(1)}, u32[]{:S(2)}, u32[]{:S(2)}) collective-permute-start(bf16[2,256,128]{2,1,0:T(8,128)(2,1)S(1)} %get-tuple-element.45), channel_id=1, source_target_pairs={{0,8},{4,20},{8,0},{12,28},{16,24},{20,4},{24,16},{28,12},{1,9},{5... | collective-permute-start | bytes 393224 | tf_op jit(solution)/shard_map/ppermute | solution.py:259
  27.1 5.8 %collective-permute-start.9 = (bf16[2,256,128]{2,1,0:T(8,128)(2,1)S(1)}, bf16[2,256,128]{2,1,0:T(8,128)(2,1)S(1)}, u32[]{:S(2)}, u32[]{:S(2)}) collective-permute-start(bf16[2,256,128]{2,1,0:T(8,128)(2,1)S(1)} %get-tuple-element.46), channel_id=1, source_target_pairs={{0,16},{4,12},{8,24},{12,4},{16,0},{20,28},{24,8},{28,20},{1,17},{... | collective-permute-start | bytes 393224 | tf_op jit(solution)/shard_map/ppermute | solution.py:259
  29.5 0.7 %copy-start.7 = (bf16[2,256,128]{2,1,0:T(8,128)(2,1)}, bf16[2,256,128]{2,1,0:T(8,128)(2,1)S(1)}, u32[]{:S(2)}) copy-start(bf16[2,256,128]{2,1,0:T(8,128)(2,1)S(1)} %collective-permute-done.10.refs_1_) | copy-start | bytes 393220
  32.9 6.7 %copy-start.8 = (bf16[2,256,128]{2,1,0:T(8,128)(2,1)S(1)}, bf16[2,256,128]{2,1,0:T(8,128)(2,1)}, u32[]{:S(2)}) copy-start(bf16[2,256,128]{2,1,0:T(8,128)(2,1)} %copy-done.7) | copy-start | bytes 393220
  33.3 0.9 %copy-start.10 = (bf16[2,256,128]{2,1,0:T(8,128)(2,1)S(1)}, bf16[2,256,128]{2,1,0:T(8,128)(2,1)}, u32[]{:S(2)}) copy-start(bf16[2,256,128]{2,1,0:T(8,128)(2,1)} %copy-done.9) | copy-start | bytes 393220
  33.3 6.3 %copy-start.1 = (bf16[1024,2048]{1,0:T(8,128)(2,1)S(1)}, bf16[1024,2048]{1,0:T(8,128)(2,1)}, u32[]{:S(2)}) copy-start(bf16[1024,2048]{1,0:T(8,128)(2,1)} %constant.2.clone.table_ref) | copy-start | bytes 12582916
  33.7 2.4 %collective-permute-start.12 = (f32[16,2304]{1,0:T(8,128)S(1)}, f32[16,2304]{1,0:T(8,128)S(1)}, u32[]{:S(2)}, u32[]{:S(2)}) collective-permute-start(f32[16,2304]{1,0:T(8,128)S(1)} %get-tuple-element.61.own_ref), channel_id=1, source_target_pairs={{0,4},{4,0},{8,12},{12,8},{16,20},{20,16},{24,28},{28,24},{1,5},{5... | collective-permute-start | bytes 442376 | tf_op jit(solution)/shard_map/ppermute | solution.py:250
  34.2 9.0 %collective-permute-start.11 = (bf16[2,256,128]{2,1,0:T(8,128)(2,1)S(1)}, bf16[2,256,128]{2,1,0:T(8,128)(2,1)S(1)}, u32[]{:S(2)}, u32[]{:S(2)}) collective-permute-start(bf16[2,256,128]{2,1,0:T(8,128)(2,1)S(1)} %copy-done.10), channel_id=1, source_target_pairs={{0,24},{4,28},{8,16},{12,20},{16,8},{20,12},{24,0},{28,4},{1,25},{... | collective-permute-start | bytes 393224 | tf_op jit(solution)/shard_map/ppermute | solution.py:259
  36.1 8.3 %collective-permute-start.13 = (bf16[16,2560]{1,0:T(8,128)(2,1)S(1)}, bf16[16,2560]{1,0:T(8,128)(2,1)S(1)}, u32[]{:S(2)}, u32[]{:S(2)}) collective-permute-start(bf16[16,2560]{1,0:T(8,128)(2,1)S(1)} %chip_sum.1.refs_0_), channel_id=1, source_target_pairs={{0,8},{4,12},{8,0},{12,4},{16,24},{20,28},{24,16},{28,20},{1,9},{5... | collective-permute-start | bytes 245768 | tf_op jit(solution)/shard_map/ppermute | solution.py:250
  37.3 7.1 %collective-permute-start.14 = (bf16[16,2560]{1,0:T(8,128)(2,1)S(1)}, bf16[16,2560]{1,0:T(8,128)(2,1)S(1)}, u32[]{:S(2)}, u32[]{:S(2)}) collective-permute-start(bf16[16,2560]{1,0:T(8,128)(2,1)S(1)} %chip_sum.1.refs_0_), channel_id=1, source_target_pairs={{0,16},{4,20},{8,24},{12,28},{16,0},{20,4},{24,8},{28,12},{1,17},{... | collective-permute-start | bytes 245768 | tf_op jit(solution)/shard_map/ppermute | solution.py:250
  37.8 6.6 %collective-permute-start.15 = (bf16[16,2560]{1,0:T(8,128)(2,1)S(1)}, bf16[16,2560]{1,0:T(8,128)(2,1)S(1)}, u32[]{:S(2)}, u32[]{:S(2)}) collective-permute-start(bf16[16,2560]{1,0:T(8,128)(2,1)S(1)} %chip_sum.1.refs_0_), channel_id=1, source_target_pairs={{0,24},{4,28},{8,16},{12,20},{16,8},{20,12},{24,0},{28,4},{1,25},{... | collective-permute-start | bytes 245768 | tf_op jit(solution)/shard_map/ppermute | solution.py:250
